TPU v7x, 32 devices: a whole 2x2x4 slice. The times are simulated.
32 devices in a mesh: rows: 8 (over z, y), grp: 4 (over x, core).
Axes of the slice: x: 2, y: 2, z: 4, core: 2. Of those that a mesh axis runs over, the one named last changes fastest.
Arguments:
- start: float32 [256, 65536], P('grp', 'rows'), may hold values from -50 to 50
- momenta: float32 [256, 65536], P('grp', 'rows'), may hold values from -6 to 6
- observed: float32 [65536], P('rows'), may hold values from -6 to 6
- precision_obs: float32 [65536], P('rows'), may hold values from 0.5 to 4
- blocks: float32 [512, 4, 128, 128], P('rows'), may hold values from -0.08 to 9
- block_cols: int32 [512, 4], P('rows'), may hold values from 0 to 511, as said below
- block_count: int32 [512], P('rows'), may hold values from 2 to 4, as said below
- step_size: float32 [1], replicated, may hold values from 0.2 to 0.3
- trajectory: float32 [256], P('grp'), may hold values from 0.3 to 1.5
Outputs:
- position: float32 [256, 65536], P('grp', 'rows')
- momentum: float32 [256, 65536], P('grp', 'rows')
- chees: float32 [256], P('grp')
Inputs may be any that keep to these rules, and one draw needn't show every extreme that they name: `block_cols`: slot 0 of block row r names r; slots 1 to 3 name distinct block rows r + k modulo 512 with k from 1 to 64, and k = 64 occurs. `block_count`: 4 is reached.
All inputs are finite; a program needn't handle non-finite values.
Results may differ from a plain program's by a relative error of at most 0.0003.
Values sent between devices are 32-bit elements; how exact they have to be, the bound alone decides.
No kernel may reach another device: no remote copies, remote signals or barrier semaphores. Data moves between devices by JAX's collectives and lax.ppermute only.
A program may use at most 192 MiB of HBM per device.

v0:
```python
import functools

import jax
import jax.numpy as jnp
from jax import lax
from jax.experimental import pallas as pl
from jax.experimental.pallas import tpu as pltpu
from jax.sharding import PartitionSpec as P

CHUNKS = 2
GROUP = 12
CAP = 46
VMEM_LIMIT = 60 * 2**20
LIST_AT = 8
ROW_AT = 128
SLOT_AT = 384
PLACE_AT = 640
META = 896

NT = (((1,), (1,)), ((), ()))
NN = (((1,), (0,)), ((), ()))


def passed_along(value, steps):
    count = lax.axis_size("rows")
    pairs = [(source, (source + steps) % count) for source in range(count)]
    return lax.ppermute(value, "rows", pairs)


def product(left, right, dims):
    return lax.dot_general(left, right, dims, preferred_element_type=jnp.float32)


def halves(value):
    high = value.astype(jnp.bfloat16)
    low = (value - high.astype(jnp.float32)).astype(jnp.bfloat16)
    return high, low


def doubled(own, chains):
    top = jnp.concatenate([own[:chains], jnp.zeros_like(own[:chains])], axis=0)
    return jnp.concatenate([own, top], axis=1)


def folded_up(value, chains, side):
    return value[:chains, :side] + (value[:chains, side:] + value[chains:, :side])


def stacked(block):
    high, low = halves(block)
    return jnp.concatenate([high, low], axis=0)


def plan_kernel(first_ref, cols_ref, count_ref, far_ref, near_ref, seen, *, bands, slots, nblocks):
    first = first_ref[0]

    def clear(i, _):
        seen[i] = 0
        return 0

    lax.fori_loop(0, bands, clear, 0, unroll=8)

    def by_row(r, counts):
        edges, nears = counts
        live = count_ref[r]
        for s in range(1, slots):
            raw = cols_ref[s, r] - first
            col = jnp.where(raw < 0, raw + nblocks, raw)
            is_live = s < live
            near = jnp.logical_and(is_live, col < bands)
            far = jnp.logical_and(is_live, col >= bands)
            far_ref[ROW_AT + edges] = r
            far_ref[SLOT_AT + edges] = s
            far_ref[PLACE_AT + edges] = col - bands
            near_ref[ROW_AT + nears] = r
            near_ref[SLOT_AT + nears] = s
            near_ref[PLACE_AT + nears] = col
            seen[jnp.where(far, col - bands, bands)] = 1
            edges = edges + far.astype(jnp.int32)
            nears = nears + near.astype(jnp.int32)
        return edges, nears

    edges, nears = lax.fori_loop(0, bands, by_row, (jnp.int32(0), jnp.int32(0)), unroll=2)
    far_ref[0] = edges
    near_ref[0] = nears

    def by_tile(m, tiles):
        far_ref[LIST_AT + tiles] = m
        used = seen[m]
        seen[m] = tiles
        return tiles + used

    tiles = lax.fori_loop(0, bands, by_tile, jnp.int32(0), unroll=4)
    far_ref[1] = tiles

    def by_edge(e, _):
        far_ref[PLACE_AT + e] = seen[far_ref[PLACE_AT + e]]
        return 0

    lax.fori_loop(0, edges, by_edge, 0)

    for i in range(GROUP):
        far_ref[ROW_AT + edges + i] = bands
        far_ref[SLOT_AT + edges + i] = 0
        far_ref[PLACE_AT + edges + i] = bands
        near_ref[ROW_AT + nears + i] = bands
        near_ref[SLOT_AT + nears + i] = 0
        near_ref[PLACE_AT + nears + i] = bands


def near_kernel(
    list_ref, coef_ref, x_hbm, v_hbm, seen_ref, weight_ref, blocks_hbm, out_hbm,
    x_buf, v_buf, diag, raw, split, total, sems, diag_sems, sem_of,
    *, bands, side, x_row, v_row, scale_at,
):
    chains = x_buf.shape[0]
    cells = bands * side
    edges = list_ref[0]
    groups = lax.div(edges + GROUP - 1, GROUP)
    pieces = diag_sems.shape[0]
    piece = bands // pieces

    def tile_at(index):
        return pl.ds(pl.multiple_of(index * side, side), side)

    get_x = pltpu.make_async_copy(x_hbm.at[pl.ds(x_row, chains)], x_buf, sems.at[0])
    get_v = pltpu.make_async_copy(v_hbm.at[pl.ds(v_row, chains)], v_buf, sems.at[1])
    put_w = pltpu.make_async_copy(v_buf, out_hbm, sems.at[2])

    def fetch_diag(p):
        rows = pl.ds(p * piece, piece)
        return pltpu.make_async_copy(blocks_hbm.at[rows, 0], diag.at[rows], diag_sems.at[p])

    def fetch(e):
        return pltpu.make_async_copy(
            blocks_hbm.at[list_ref[ROW_AT + e], list_ref[SLOT_AT + e]], raw.at[e], sem_of.at[e]
        )

    get_x.start()
    for p in range(pieces):
        fetch_diag(p).start()

    def start_fetch(e, _):
        fetch(e).start()
        return 0

    lax.fori_loop(0, edges, start_fetch, 0)
    get_v.start()
    get_x.wait()
    high, low = halves(x_buf[...])
    split[:chains, :cells] = high
    split[chains:, :cells] = low
    split[:, cells:] = jnp.zeros((2 * chains, side), jnp.bfloat16)
    total[:, cells:] = jnp.zeros((chains, side), jnp.float32)

    def diag_piece(p, _):
        fetch_diag(p).wait()
        for i in range(piece):
            r = p * piece + i
            up = product(split[:, tile_at(r)], stacked(diag[r]), NT)
            total[:, tile_at(r)] = folded_up(up, chains, side)
        return 0

    lax.fori_loop(0, pieces, diag_piece, 0)

    def group(g, _):
        base = g * GROUP
        for i in range(GROUP):

            @pl.when(base + i < edges)
            def _():
                fetch(base + i).wait()

        ups, downs, rows, cols = [], [], [], []
        for i in range(GROUP):
            rows.append(list_ref[ROW_AT + base + i])
            cols.append(list_ref[PLACE_AT + base + i])
            value = stacked(raw[base + i])
            ups.append(folded_up(product(split[:, tile_at(cols[i])], value, NT), chains, side))
            down = product(doubled(split[:, tile_at(rows[i])], chains), value, NN)
            downs.append(down[:chains] + down[chains:])
        for i in range(GROUP):
            total[:, tile_at(rows[i])] += ups[i]
            total[:, tile_at(cols[i])] += downs[i]
        return 0

    lax.fori_loop(0, groups, group, 0)
    get_v.wait()
    pull = total[:, :cells] + weight_ref[...] * (x_buf[...] - seen_ref[...])
    v_buf[...] = v_buf[...] - coef_ref[scale_at] * pull
    put_w.start()
    put_w.wait()


def far_kernel(*refs, bands, side, cap, x_row, scale_at, receives, sends, ends, step_at=2):
    refs = list(refs)

    def take(count):
        taken = refs[:count]
        del refs[:count]
        return taken

    (meta_ref, blocks_hbm) = take(2)
    if receives:
        coef_ref, w_hbm, halo_hbm = take(3)
    if receives and sends:
        given_ref, carry_hbm = take(2)
    if sends:
        (x_hbm,) = take(1)
    if receives:
        (v_out,) = take(1)
    if receives and sends:
        x_out, halo_out = take(2)
    if ends:
        (column_out,) = take(1)
    if sends:
        (carry_out,) = take(1)
    raw, both, sem_of, sems = take(4)
    if receives:
        vel, halo_buf, halo_split = take(3)
    if receives and sends:
        carry_buf, packed_buf = take(2)
    if sends:
        x_buf, split, sum_carry = take(3)
    chains = (vel if receives else x_buf).shape[0]
    cells = bands * side
    edges = meta_ref[0]
    groups = lax.div(edges + GROUP - 1, GROUP)

    def tile_at(index):
        return pl.ds(pl.multiple_of(index * side, side), side)

    def fetch(e):
        return pltpu.make_async_copy(
            blocks_hbm.at[meta_ref[ROW_AT + e], meta_ref[SLOT_AT + e]], raw.at[e], sem_of.at[e]
        )

    def start_fetch(e, _):
        fetch(e).start()
        return 0

    def await_group(base):
        for i in range(GROUP):

            @pl.when(base + i < edges)
            def _():
                fetch(base + i).wait()

    if sends:
        get_x = pltpu.make_async_copy(x_hbm.at[pl.ds(x_row, chains)], x_buf, sems.at[0])
    if receives:
        get_halo = pltpu.make_async_copy(halo_hbm, halo_buf, sems.at[1])
        get_w = pltpu.make_async_copy(w_hbm, vel.at[:, pl.ds(0, cells)], sems.at[2])
        put_v = pltpu.make_async_copy(vel.at[:, pl.ds(0, cells)], v_out, sems.at[3])
        get_halo.start()
        get_w.start()
    if sends and not receives:
        get_x.start()
    lax.fori_loop(0, edges, start_fetch, 0)
    if receives and sends:
        get_carry = pltpu.make_async_copy(carry_hbm, carry_buf, sems.at[4])
        get_carry.start()
        get_x.start()

    if receives:
        scale = coef_ref[scale_at]
        get_halo.wait()
        high, low = halves(halo_buf[...])
        halo_split[:cap, :chains] = high
        halo_split[:cap, chains:] = low
        halo_split[cap] = jnp.zeros((2 * chains, side), jnp.bfloat16)
        get_w.wait()
        vel[:, cells:] = jnp.zeros((chains, side), jnp.float32)

        def up_group(g, _):
            base = g * GROUP
            await_group(base)
            sums, rows = [], []
            for i in range(GROUP):
                rows.append(meta_ref[ROW_AT + base + i])
                value = stacked(raw[base + i])
                if sends:
                    both[base + i] = value
                place = jnp.minimum(meta_ref[PLACE_AT + base + i], cap)
                sums.append(folded_up(product(halo_split[place], value, NT), chains, side))
            for i in range(GROUP):
                vel[:, tile_at(rows[i])] -= scale * sums[i]
            return 0

        lax.fori_loop(0, groups, up_group, 0)
    if receives and sends:
        given = jnp.minimum(given_ref[1], cap)
        get_carry.wait()

        def add_carry(k, _):
            vel[:, tile_at(given_ref[LIST_AT + k])] -= scale * carry_buf[k]
            return 0

        lax.fori_loop(0, given, add_carry, 0)
    if receives:
        put_v.start()
    if sends:
        get_x.wait()
    if receives and sends:
        x_buf[...] += coef_ref[step_at] * vel[:, :cells]
        put_x = pltpu.make_async_copy(x_buf, x_out, sems.at[5])
        put_x.start()
        if ends:
            column_out[...] = jnp.sum(x_buf[...], axis=0, keepdims=True)

        def pack(k, _):
            packed_buf[k] = x_buf[:, tile_at(given_ref[LIST_AT + k])]
            return 0

        lax.fori_loop(0, given, pack, 0)
        put_halo = pltpu.make_async_copy(packed_buf, halo_out, sems.at[6])
        put_halo.start()
    if sends:
        high, low = halves(x_buf[...])
        split[:chains, :cells] = high
        split[chains:, :cells] = low
        split[:, cells:] = jnp.zeros((2 * chains, side), jnp.bfloat16)
        sum_carry[...] = jnp.zeros_like(sum_carry)

        def down_group(g, _):
            base = g * GROUP
            if not receives:
                await_group(base)
            sums, places = [], []
            for i in range(GROUP):
                row = meta_ref[ROW_AT + base + i]
                places.append(jnp.minimum(meta_ref[PLACE_AT + base + i], cap))
                value = both[base + i] if receives else stacked(raw[base + i])
                down = product(doubled(split[:, tile_at(row)], chains), value, NN)
                sums.append(down[:chains] + down[chains:])
            for i in range(GROUP):
                sum_carry[places[i]] += sums[i]
            return 0

        lax.fori_loop(0, groups, down_group, 0)
        put_carry = pltpu.make_async_copy(sum_carry.at[pl.ds(0, cap)], carry_out, sems.at[7])
        put_carry.start()
        put_carry.wait()
    if receives and sends:
        put_x.wait()
        put_halo.wait()
    if receives:
        put_v.wait()


def pack_kernel(given_ref, x_ref, out_ref, *, cap):
    side = out_ref.shape[2]

    def pack(k, _):
        tile = pl.ds(pl.multiple_of(given_ref[LIST_AT + k] * side, side), side)
        out_ref[k] = x_ref[:, tile]
        return 0

    lax.fori_loop(0, jnp.minimum(given_ref[1], cap), pack, 0)


def end_kernel(given_ref, coef_ref, v_ref, carry_ref, off_ref, *rest, cap, scale_at):
    out_ref, dot_ref, sums = rest[-3:]
    side = carry_ref.shape[2]
    scale = coef_ref[scale_at]
    out_ref[...] = v_ref[...]

    def add_carry(k, _):
        tile = pl.ds(pl.multiple_of(given_ref[LIST_AT + k] * side, side), side)
        out_ref[:, tile] -= scale * carry_ref[k]
        return 0

    lax.fori_loop(0, jnp.minimum(given_ref[1], cap), add_carry, 0)
    cells = v_ref.shape[1]
    sums[...] = jnp.zeros_like(sums)
    wide = 8 * side

    def dot(i, _):
        part = pl.ds(pl.multiple_of(i * wide, wide), wide)
        sums[...] += out_ref[:, part] * off_ref[:, part]
        return 0

    lax.fori_loop(0, cells // wide, dot, 0)
    dot_ref[...] = sum(sums[:, i * side : (i + 1) * side] for i in range(8))


def spread_kernel(
    start_ref, *refs, side, chain_total
):
    *x_refs, sum_start_ref, sum_end_ref, position_ref, offset_ref, gain_ref, sums = refs
    chains = x_refs[0].shape[0]
    cells = start_ref.shape[1]
    sums[...] = jnp.zeros_like(sums)
    wide = 4 * side

    def one(i, _):
        part = pl.ds(pl.multiple_of(i * wide, wide), wide)
        mean_start = sum_start_ref[:, part] / chain_total
        mean_end = sum_end_ref[:, part] / chain_total
        for h, x_ref in enumerate(x_refs):
            rows = pl.ds(h * chains, chains)
            x = x_ref[:, part]
            position_ref[rows, part] = x
            off_end = x - mean_end
            offset_ref[rows, part] = off_end
            off_start = start_ref[rows, part] - mean_start
            sums[rows] += off_end * off_end - off_start * off_start
        return 0

    lax.fori_loop(0, cells // wide, one, 0)
    gain_ref[...] = sum(sums[:, i * side : (i + 1) * side] for i in range(4))


SMEM = pl.BlockSpec(memory_space=pltpu.SMEM)
VMEM = pl.BlockSpec(memory_space=pltpu.VMEM)
ANY = pl.BlockSpec(memory_space=pl.ANY)
PARAMS = pltpu.CompilerParams(vmem_limit_bytes=VMEM_LIMIT)
COST = pl.CostEstimate(flops=1000, bytes_accessed=1000, transcendentals=0)


def near_call(near_list, coef, x, v, seen, weight, blocks, chains, x_row, v_row, scale_at):
    bands, slots, side, _ = blocks.shape
    cells = bands * side
    most = bands * (slots - 1) + GROUP
    pieces = 8 if bands % 8 == 0 else 1
    return pl.pallas_call(
        functools.partial(
            near_kernel, bands=bands, side=side, x_row=x_row, v_row=v_row, scale_at=scale_at
        ),
        out_shape=jax.ShapeDtypeStruct((chains, cells), jnp.float32),
        in_specs=[SMEM, SMEM, ANY, ANY, VMEM, VMEM, ANY],
        out_specs=ANY,
        scratch_shapes=[
            pltpu.VMEM((chains, cells), jnp.float32),
            pltpu.VMEM((chains, cells), jnp.float32),
            pltpu.VMEM((bands, side, side), jnp.float32),
            pltpu.VMEM((most, side, side), jnp.float32),
            pltpu.VMEM((2 * chains, cells + side), jnp.bfloat16),
            pltpu.VMEM((chains, cells + side), jnp.float32),
            pltpu.SemaphoreType.DMA((3,)),
            pltpu.SemaphoreType.DMA((pieces,)),
            pltpu.SemaphoreType.DMA((most,)),
        ],
        compiler_params=PARAMS,
        cost_estimate=COST,
        name="near",
    )(near_list, coef, x, v, seen, weight, blocks)


def far_call(meta, given, coef, blocks, x, w, halo, carry, chains, x_row, scale_at, cap, ends=False):
    bands, slots, side, _ = blocks.shape
    cells = bands * side
    receives, sends = w is not None, x is not None
    most = bands * (slots - 1) + GROUP
    state = jax.ShapeDtypeStruct((chains, cells), jnp.float32)
    parcel = jax.ShapeDtypeStruct((cap, chains, side), jnp.float32)
    in_specs, args = [SMEM, ANY], [meta, blocks]
    out_shape = []
    scratch = [
        pltpu.VMEM((most, side, side), jnp.float32),
        pltpu.VMEM((most, 2 * side, side), jnp.bfloat16),
        pltpu.SemaphoreType.DMA((most,)),
        pltpu.SemaphoreType.DMA((8,)),
    ]
    if receives:
        in_specs += [SMEM, ANY, ANY]
        args += [coef, w, halo]
        out_shape += [state]
        scratch += [
            pltpu.VMEM((chains, cells + side), jnp.float32),
            pltpu.VMEM((cap, chains, side), jnp.float32),
            pltpu.VMEM((cap + 1, 2 * chains, side), jnp.bfloat16),
        ]
    if receives and sends:
        in_specs += [SMEM, ANY]
        args += [given, carry]
        out_shape += [state, parcel]
        if ends:
            out_shape += [jax.ShapeDtypeStruct((1, cells), jnp.float32)]
        scratch += [
            pltpu.VMEM((cap, chains, side), jnp.float32),
            pltpu.VMEM((cap, chains, side), jnp.float32),
        ]
    if sends:
        in_specs += [ANY]
        args += [x]
        out_shape += [parcel]
        scratch += [
            pltpu.VMEM((chains, cells), jnp.float32),
            pltpu.VMEM((2 * chains, cells + side), jnp.bfloat16),
            pltpu.VMEM((cap + 1, chains, side), jnp.float32),
        ]
    return pl.pallas_call(
        functools.partial(
            far_kernel, bands=bands, side=side, cap=cap, x_row=x_row, scale_at=scale_at,
            receives=receives, sends=sends, ends=ends,
        ),
        out_shape=out_shape,
        in_specs=in_specs,
        out_specs=[VMEM if o.shape == (1, cells) else ANY for o in out_shape],
        scratch_shapes=scratch,
        compiler_params=PARAMS,
        cost_estimate=COST,
        name="far",
    )(*args)


def pack_call(given, x, chains, part, cap, side):
    return pl.pallas_call(
        functools.partial(pack_kernel, cap=cap),
        out_shape=jax.ShapeDtypeStruct((cap, chains, side), jnp.float32),
        grid=(1,),
        in_specs=[SMEM, pl.BlockSpec((chains, x.shape[1]), lambda i: (part, 0))],
        out_specs=pl.BlockSpec((cap, chains, side), lambda i: (0, 0, 0)),
        compiler_params=PARAMS,
        cost_estimate=COST,
        name="pack",
    )(given, x)


def end_call(given, coef, v, carry, offset, earlier, part, scale_at):
    cap, chains, side = carry.shape
    cells = v.shape[1]
    in_specs = [
        SMEM,
        SMEM,
        pl.BlockSpec((chains, cells), lambda i: (0, 0)),
        pl.BlockSpec((cap, chains, side), lambda i: (0, 0, 0)),
        pl.BlockSpec((chains, cells), lambda i: (part, 0)),
    ]
    args = [given, coef, v, carry, offset]
    if earlier is not None:
        in_specs.append(ANY)
        args.append(earlier)
    return pl.pallas_call(
        functools.partial(end_kernel, cap=cap, scale_at=scale_at),
        out_shape=[
            jax.ShapeDtypeStruct(offset.shape, jnp.float32),
            jax.ShapeDtypeStruct((chains, side), jnp.float32),
        ],
        grid=(1,),
        in_specs=in_specs,
        out_specs=[
            pl.BlockSpec((chains, cells), lambda i: (part, 0)),
            pl.BlockSpec((chains, side), lambda i: (0, 0)),
        ],
        scratch_shapes=[pltpu.VMEM((chains, 8 * side), jnp.float32)],
        input_output_aliases={} if earlier is None else {5: 0},
        compiler_params=PARAMS,
        cost_estimate=COST,
        name="end",
    )(*args)


def spread_call(start, x, total_start, total_end, side, chain_total):
    return pl.pallas_call(
        functools.partial(spread_kernel, side=side, chain_total=chain_total),
        out_shape=[
            jax.ShapeDtypeStruct(start.shape, jnp.float32),
            jax.ShapeDtypeStruct(start.shape, jnp.float32),
            jax.ShapeDtypeStruct((start.shape[0], side), jnp.float32),
        ],
        in_specs=[VMEM] * (3 + len(x)),
        out_specs=[VMEM] * 3,
        scratch_shapes=[pltpu.VMEM((start.shape[0], 4 * side), jnp.float32)],
        compiler_params=PARAMS,
        cost_estimate=COST,
        name="spread",
    )(start, *x, total_start, total_end)


def summed_over_rows(value):
    count = lax.axis_size("rows")
    reach = 1
    while reach < count:
        radix = 2 if reach == 1 else 4 if count % (4 * reach) == 0 else 2
        own = value
        for k in range(1, radix):
            pairs = [(source, source ^ (k * reach)) for source in range(count)]
            value = value + lax.ppermute(own, "rows", pairs)
        reach *= radix
    return value


def on_device(
    start, momenta, observed, precision_obs, blocks, block_cols, block_count, step_size, trajectory
):
    bands, slots, side, _ = blocks.shape
    cells = bands * side
    local_chains = start.shape[0]
    chains = local_chains // CHUNKS
    nblocks = bands * lax.axis_size("rows")
    all_cells = cells * lax.axis_size("rows")
    chain_total = local_chains * lax.axis_size("grp")
    first = (lax.axis_index("rows") * bands).astype(jnp.int32).reshape(1)
    meta, near_list = pl.pallas_call(
        functools.partial(plan_kernel, bands=bands, slots=slots, nblocks=nblocks),
        out_shape=[jax.ShapeDtypeStruct((META,), jnp.int32)] * 2,
        in_specs=[SMEM, SMEM, SMEM],
        out_specs=[SMEM, SMEM],
        scratch_shapes=[pltpu.SMEM((bands + 8,), jnp.int32)],
        name="plan",
    )(first, block_cols.T, block_count)
    given = passed_along(meta[:ROW_AT], 1)
    step_len = step_size[0]
    coef = jnp.stack([step_len / 2, step_len, step_len])
    seen = observed.reshape(1, cells)
    weight = precision_obs.reshape(1, cells)
    parts = range(CHUNKS)

    def two_steps(cap, start, momenta):
        far = functools.partial(far_call, meta, given, coef, blocks)

        def near(x, v, x_row, v_row, scale_at):
            return near_call(
                near_list, coef, x, v, seen, weight, blocks, chains, x_row, v_row, scale_at
            )

        x, v, w, flight = [start] * CHUNKS, [momenta] * CHUNKS, [], []
        rows = [h * chains for h in parts]
        for h in parts:
            (carry,) = far(start, None, None, None, chains, rows[h], 0, cap)
            halo = pack_call(given, start, chains, h, cap, side)
            flight.append((passed_along(halo, -1), passed_along(carry, 1)))
        for h in parts:
            w.append(near(start, momenta, rows[h], rows[h], 0))
        w = list(lax.optimization_barrier(tuple(w)))
        columns = []
        for turn in range(2):
            for h in parts:
                halo, carry = flight[h]
                v[h], x[h], halo, *column, carry = far(
                    x[h], w[h], halo, carry, chains, rows[h], turn, cap, turn == 1
                )
                columns += column
                flight[h] = (passed_along(halo, -1), passed_along(carry, 1))
                rows[h] = 0
                w[h] = near(x[h], v[h], 0, 0, 1 - turn)
                w = list(lax.optimization_barrier(tuple(w)))
        total_start, total_end = lax.psum(
            (jnp.sum(start, axis=0, keepdims=True), sum(columns[1:], columns[0])), "grp"
        )
        momentum, dots = None, []
        for h in parts:
            halo, carry = flight[h]
            if h < CHUNKS - 1:
                halo, carry = lax.optimization_barrier((halo, carry))
            (v[h],) = far(None, w[h], halo, None, chains, 0, 0, cap)
            if h == 0:
                v[0], total_start, total_end = lax.optimization_barrier(
                    (v[0], total_start, total_end)
                )
                position, offset, gain = spread_call(
                    start, x, total_start, total_end, side, chain_total
                )
            momentum, dot = end_call(given, coef, v[h], carry, offset, momentum, h, 0)
            dots.append(dot)
            if h < CHUNKS - 1:
                w[h + 1], momentum = lax.optimization_barrier((w[h + 1], momentum))
        over = jnp.broadcast_to((meta[1] > cap).astype(jnp.float32), (8, side))
        sums = summed_over_rows(jnp.concatenate([gain, *dots, over], axis=0))
        per_chain = jnp.sum(sums, axis=1)
        spread = per_chain[:local_chains]
        inner = per_chain[local_chains : 2 * local_chains]
        chees = trajectory * (spread / all_cells) * (inner / all_cells)
        return sums[-1, 0], position, momentum, chees

    cap = min(CAP, bands)
    results = two_steps(cap, start, momenta)
    if cap < bands:
        results = lax.while_loop(
            lambda state: state[0] > 0.0,
            lambda state: two_steps(
                bands,
                jnp.where(state[0] > 0.0, start, 0.0),
                jnp.where(state[0] > 0.0, momenta, 0.0),
            ),
            results,
        )
    return tuple(results[1:])


def solution(mesh):
    placed = (
        P("grp", "rows"),
        P("grp", "rows"),
        P("rows"),
        P("rows"),
        P("rows", None, None, None),
        P("rows", None),
        P("rows"),
        P(),
        P("grp"),
    )
    return jax.shard_map(
        on_device,
        mesh=mesh,
        in_specs=placed,
        out_specs=(P("grp", "rows"), P("grp", "rows"), P("grp")),
        check_vma=False,
    )
```

profile of v0, /device:TPU:0, one launch (start us, length us, event | category | flops | bytes accessed | tf_op | source)
XLA Modules:
  0.0 261.7 jit_solution(10451310193908206894)
XLA Ops:
  7.2 4.2 %plan.1 = (s32[896]{0:T(1024)S(1)}, s32[896]{0:T(1024)S(1)}) custom-call(s32[1]{0:T(128)} %bitcast.2.first_ref, s32[4,64]{1,0:T(4,128)} %bitcast.30, s32[64]{0:T(128)} %count_ref.1), custom_call_target="tpu_custom_call" | custom-call | tf_op jit(solution)/shard_map/plan/pallas_call | solution.py:596
  14.4 6.5 %far.23 = f32[46,32,128]{2,1,0:T(8,128)} custom-call(s32[896]{0:T(1024)S(1)} %get-tuple-element.490.refs_0_, f32[64,4,128,128]{3,2,1,0:T(8,128)} %refs_1_.15, f32[64,8192]{1,0:T(8,128)} %start_ref.1), custom_call_target="tpu_custom_call" | custom-call | flops 1000 | bytes 1000 | tf_op jit(solution)/shard_map/far/pallas_call | solution.py:493
  27.5 6.3 %far.25 = f32[46,32,128]{2,1,0:T(8,128)} custom-call(s32[896]{0:T(1024)S(1)} %get-tuple-element.490.refs_0_, f32[64,4,128,128]{3,2,1,0:T(8,128)} %refs_1_.15, f32[64,8192]{1,0:T(8,128)S(1)} %copy-done), custom_call_target="tpu_custom_call" | custom-call | flops 1000 | bytes 1000 | tf_op jit(solution)/shard_map/far/pallas_call | solution.py:493
  35.6 4.7 %collective-permute-start.19 = (f32[46,32,128]{2,1,0:T(8,128)}, f32[46,32,128]{2,1,0:T(8,128)}, u32[]{:S(2)}, u32[]{:S(2)}) collective-permute-start(f32[46,32,128]{2,1,0:T(8,128)} %pack.7), channel_id=1, source_target_pairs={{0,28},{4,0},{8,4},{12,8},{16,12},{20,16},{24,20},{28,24},{1,29},{... | collective-permute-start | bytes 2261000 | tf_op jit(solution)/shard_map/ppermute | solution.py:27
  41.1 9.8 %near.18.refs_3_ = f32[32,8192]{1,0:T(8,128)} custom-call(s32[896]{0:T(1024)S(1)} %get-tuple-element.484.list_ref, f32[3]{0:T(128)S(1)} %pad_maximum_fusion.coef_ref.refs_2_, f32[64,8192]{1,0:T(8,128)S(1)} %copy-done, f32[64,8192]{1,0:T(8,128)} %v_hbm.3, f32[1,8192]{1,0:T(1,128)S(1)} %bitcast.14, f32[1,8192]{1,0:T(1,128)S(1)} %bitcast.21, ...), custom_call_target="tpu_custom_call" | custom-call | flops 1000 | bytes 1000 | tf_op jit(solution)/shard_map/near/pallas_call | solution.py:426
  50.9 9.8 %near.19.refs_3_ = f32[32,8192]{1,0:T(8,128)} custom-call(s32[896]{0:T(1024)S(1)} %get-tuple-element.484.list_ref, f32[3]{0:T(128)S(1)} %pad_maximum_fusion.coef_ref.refs_2_, f32[64,8192]{1,0:T(8,128)S(1)} %copy-done, f32[64,8192]{1,0:T(8,128)} %v_hbm.3, f32[1,8192]{1,0:T(1,128)S(1)} %bitcast.15, f32[1,8192]{1,0:T(1,128)S(1)} %bitcast.22, ...), custom_call_target="tpu_custom_call" | custom-call | flops 1000 | bytes 1000 | tf_op jit(solution)/shard_map/near/pallas_call | solution.py:426
  60.6 11.8 %collective-permute-done.18.refs_6_ = f32[46,32,128]{2,1,0:T(8,128)} collective-permute-done((f32[46,32,128]{2,1,0:T(8,128)}, f32[46,32,128]{2,1,0:T(8,128)}, u32[]{:S(2)}, u32[]{:S(2)}) %collective-permute-start.18) | collective-permute-done | bytes 753696 | tf_op jit(solution)/shard_map/ppermute | solution.py:27
  74.7 10.1 %far.24 = (f32[32,8192]{1,0:T(8,128)}, f32[32,8192]{1,0:T(8,128)}, f32[46,32,128]{2,1,0:T(8,128)}, f32[46,32,128]{2,1,0:T(8,128)}) custom-call(s32[896]{0:T(1024)S(1)} %get-tuple-element.490.refs_0_, f32[64,4,128,128]{3,2,1,0:T(8,128)} %refs_1_.15, f32[3]{0:T(128)S(1)} %pad_maximum_fusion.coef_ref.refs_2_, f32[32,8192]{1,0:T(8,128)} %near.18.refs_3_, ...), custom_call_target="tpu_custom_call" | custom-call | flops 1000 | bytes 1000 | tf_op jit(solution)/shard_map/far/pallas_call | solution.py:493
  86.9 11.2 %near.20.refs_3_ = f32[32,8192]{1,0:T(8,128)} custom-call(s32[896]{0:T(1024)S(1)} %get-tuple-element.484.list_ref, f32[3]{0:T(128)S(1)} %pad_maximum_fusion.coef_ref.refs_2_, f32[32,8192]{1,0:T(8,128)} %get-tuple-element.213.x_hbm.refs_7_, f32[32,8192]{1,0:T(8,128)} %get-tuple-element.214.v_hbm, f32[1,8192]{1,0:T(1,128)S(1)} %bitcast.16, ...), custom_call_target="tpu_custom_call" | custom-call | flops 1000 | bytes 1000 | tf_op jit(solution)/shard_map/near/pallas_call | solution.py:426
  98.1 6.5 %collective-permute-done.20.refs_6_ = f32[46,32,128]{2,1,0:T(8,128)S(1)} collective-permute-done((f32[46,32,128]{2,1,0:T(8,128)}, f32[46,32,128]{2,1,0:T(8,128)S(1)}, u32[]{:S(2)}, u32[]{:S(2)}) %collective-permute-start.20) | collective-permute-done | bytes 753696 | tf_op jit(solution)/shard_map/ppermute | solution.py:27
  105.4 10.1 %far.26 = (f32[32,8192]{1,0:T(8,128)}, f32[32,8192]{1,0:T(8,128)}, f32[46,32,128]{2,1,0:T(8,128)}, f32[46,32,128]{2,1,0:T(8,128)}) custom-call(s32[896]{0:T(1024)S(1)} %get-tuple-element.490.refs_0_, f32[64,4,128,128]{3,2,1,0:T(8,128)} %refs_1_.15, f32[3]{0:T(128)S(1)} %pad_maximum_fusion.coef_ref.refs_2_, f32[32,8192]{1,0:T(8,128)} %near.19.refs_3_, ...), custom_call_target="tpu_custom_call" | custom-call | flops 1000 | bytes 1000 | tf_op jit(solution)/shard_map/far/pallas_call | solution.py:493
  119.2 11.4 %near.21.refs_3_ = f32[32,8192]{1,0:T(8,128)} custom-call(s32[896]{0:T(1024)S(1)} %get-tuple-element.484.list_ref, f32[3]{0:T(128)S(1)} %pad_maximum_fusion.coef_ref.refs_2_, f32[32,8192]{1,0:T(8,128)} %get-tuple-element.218.x_hbm.refs_7_, f32[32,8192]{1,0:T(8,128)} %get-tuple-element.219.v_hbm, f32[1,8192]{1,0:T(1,128)S(1)} %bitcast.17, ...), custom_call_target="tpu_custom_call" | custom-call | flops 1000 | bytes 1000 | tf_op jit(solution)/shard_map/near/pallas_call | solution.py:426
  130.6 6.2 %collective-permute-done.22.refs_6_ = f32[46,32,128]{2,1,0:T(8,128)} collective-permute-done((f32[46,32,128]{2,1,0:T(8,128)}, f32[46,32,128]{2,1,0:T(8,128)}, u32[]{:S(2)}, u32[]{:S(2)}) %collective-permute-start.22) | collective-permute-done | bytes 753696 | tf_op jit(solution)/shard_map/ppermute | solution.py:27
  136.8 10.8 %far.27 = (f32[32,8192]{1,0:T(8,128)}, f32[32,8192]{1,0:T(8,128)}, f32[46,32,128]{2,1,0:T(8,128)}, f32[1,8192]{1,0:T(1,128)}, f32[46,32,128]{2,1,0:T(8,128)}) custom-call(s32[896]{0:T(1024)S(1)} %get-tuple-element.490.refs_0_, f32[64,4,128,128]{3,2,1,0:T(8,128)} %refs_1_.15, f32[3]{0:T(128)S(1)} %pad_maximum_fusion.coef_ref.refs_2_, ...), custom_call_target="tpu_custom_call" | custom-call | flops 1000 | bytes 1000 | tf_op jit(solution)/shard_map/far/pallas_call | solution.py:493
  147.7 3.6 %collective-permute-start.25 = (f32[46,32,128]{2,1,0:T(8,128)}, f32[46,32,128]{2,1,0:T(8,128)}, u32[]{:S(2)}, u32[]{:S(2)}) collective-permute-start(f32[46,32,128]{2,1,0:T(8,128)} %get-tuple-element.233), channel_id=1, source_target_pairs={{0,28},{4,0},{8,4},{12,8},{16,12},{20,16},{24,20},{28,24},{1,29},{... | collective-permute-start | bytes 2261000 | tf_op jit(solution)/shard_map/ppermute | solution.py:27
  151.3 11.2 %near.22.refs_3_ = f32[32,8192]{1,0:T(8,128)} custom-call(s32[896]{0:T(1024)S(1)} %get-tuple-element.484.list_ref, f32[3]{0:T(128)S(1)} %pad_maximum_fusion.coef_ref.refs_2_, f32[32,8192]{1,0:T(8,128)} %get-tuple-element.223.x_hbm.refs_0_, f32[32,8192]{1,0:T(8,128)} %get-tuple-element.224.v_hbm, f32[1,8192]{1,0:T(1,128)S(1)} %bitcast.18, ...), custom_call_target="tpu_custom_call" | custom-call | flops 1000 | bytes 1000 | tf_op jit(solution)/shard_map/near/pallas_call | solution.py:426
  162.5 6.6 %collective-permute-done.24.refs_6_ = f32[46,32,128]{2,1,0:T(8,128)} collective-permute-done((f32[46,32,128]{2,1,0:T(8,128)}, f32[46,32,128]{2,1,0:T(8,128)}, u32[]{:S(2)}, u32[]{:S(2)}) %collective-permute-start.24) | collective-permute-done | bytes 753696 | tf_op jit(solution)/shard_map/ppermute | solution.py:27
  169.1 10.9 %far.28 = (f32[32,8192]{1,0:T(8,128)}, f32[32,8192]{1,0:T(8,128)}, f32[46,32,128]{2,1,0:T(8,128)}, f32[1,8192]{1,0:T(1,128)}, f32[46,32,128]{2,1,0:T(8,128)}) custom-call(s32[896]{0:T(1024)S(1)} %get-tuple-element.490.refs_0_, f32[64,4,128,128]{3,2,1,0:T(8,128)} %refs_1_.15, f32[3]{0:T(128)S(1)} %pad_maximum_fusion.coef_ref.refs_2_, ...), custom_call_target="tpu_custom_call" | custom-call | flops 1000 | bytes 1000 | tf_op jit(solution)/shard_map/far/pallas_call | solution.py:493
  180.1 4.3 %collective-permute-start.27 = (f32[46,32,128]{2,1,0:T(8,128)}, f32[46,32,128]{2,1,0:T(8,128)S(1)}, u32[]{:S(2)}, u32[]{:S(2)}) collective-permute-start(f32[46,32,128]{2,1,0:T(8,128)} %get-tuple-element.248), channel_id=1, source_target_pairs={{0,28},{4,0},{8,4},{12,8},{16,12},{20,16},{24,20},{28,24},{1,29},{... | collective-permute-start | bytes 2261000 | tf_op jit(solution)/shard_map/ppermute | solution.py:27
  187.0 11.2 %near.23.refs_3_ = f32[32,8192]{1,0:T(8,128)} custom-call(s32[896]{0:T(1024)S(1)} %get-tuple-element.484.list_ref, f32[3]{0:T(128)S(1)} %pad_maximum_fusion.coef_ref.refs_2_, f32[32,8192]{1,0:T(8,128)} %get-tuple-element.229.x_hbm.refs_1_, f32[32,8192]{1,0:T(8,128)} %get-tuple-element.231.v_hbm, f32[1,8192]{1,0:T(1,128)S(1)} %bitcast.19, ...), custom_call_target="tpu_custom_call" | custom-call | flops 1000 | bytes 1000 | tf_op jit(solution)/shard_map/near/pallas_call | solution.py:426
  201.4 7.6 %far.29.v_ref = f32[32,8192]{1,0:T(8,128)} custom-call(s32[896]{0:T(1024)S(1)} %get-tuple-element.490.refs_0_, f32[64,4,128,128]{3,2,1,0:T(8,128)} %refs_1_.15, f32[3]{0:T(128)S(1)} %pad_maximum_fusion.coef_ref.refs_2_, f32[32,8192]{1,0:T(8,128)} %near.22.refs_3_, f32[46,32,128]{2,1,0:T(8,128)} %collective-permute-done.25.refs_4_), custom_call_target="tpu_custom_call" | custom-call | flops 1000 | bytes 1000 | tf_op jit(solution)/shard_map/far/pallas_call | solution.py:493
  209.0 9.5 %all-reduce.7.cloned.1.call-done = (f32[1,8192]{1,0:T(1,128)}, f32[1,8192]{1,0:T(1,128)}) async-done(((f32[1,8192]{1,0:T(1,128)}, f32[1,8192]{1,0:T(1,128)}), (f32[1,8192]{1,0:T(1,128)}, f32[1,8192]{1,0:T(1,128)})) %all-reduce.7.cloned.1.call-update) | async-done | bytes 65552 | tf_op jit(solution)/shard_map/psum | solution.py:640
  218.5 4.2 %spread.3 = (f32[64,8192]{1,0:T(8,128)}, f32[64,8192]{1,0:T(8,128)}, f32[64,128]{1,0:T(8,128)}) custom-call(f32[64,8192]{1,0:T(8,128)S(1)} %copy-done, f32[32,8192]{1,0:T(8,128)} %get-tuple-element.223.x_hbm.refs_0_, f32[32,8192]{1,0:T(8,128)} %get-tuple-element.229.x_hbm.refs_1_, f32[1,8192]{1,0:T(1,128)} %get-tuple-element.238.refs_2_, ...), custom_call_target="tpu_custom_call" | custom-call | flops 1000 | bytes 1000 | tf_op jit(solution)/shard_map/spread/pallas_call | solution.py:556
  226.9 7.6 %far.30.v_ref = f32[32,8192]{1,0:T(8,128)} custom-call(s32[896]{0:T(1024)S(1)} %get-tuple-element.490.refs_0_, f32[64,4,128,128]{3,2,1,0:T(8,128)} %refs_1_.15, f32[3]{0:T(128)S(1)} %pad_maximum_fusion.coef_ref.refs_2_, f32[32,8192]{1,0:T(8,128)} %near.23.refs_3_, f32[46,32,128]{2,1,0:T(8,128)} %copy-done.8), custom_call_target="tpu_custom_call" | custom-call | flops 1000 | bytes 1000 | tf_op jit(solution)/shard_map/far/pallas_call | solution.py:493
  (70 shorter events, 49.3 us)
Async XLA Ops:
  7.2 211.3 %all-reduce.7.cloned.1.call-start = ((), (), s32[]{:S(2)}) async-start(), calls=%async_computation | async-start | bytes 131072 | tf_op jit(solution)/shard_map/psum | solution.py:640
  11.4 11.1 %copy-start = (f32[64,8192]{1,0:T(8,128)S(1)}, f32[64,8192]{1,0:T(8,128)}, u32[]{:S(2)}) copy-start(f32[64,8192]{1,0:T(8,128)} %start_ref.1) | copy-start | bytes 6291460
  11.4 11.1 %collective-permute-start.16 = (s32[128]{0:T(128)S(1)}, s32[128]{0:T(128)S(1)}, u32[]{:S(2)}, u32[]{:S(2)}) collective-permute-start(s32[128]{0:T(128)S(1)} %slice.30), channel_id=1, source_target_pairs={{0,4},{4,8},{8,12},{12,16},{16,20},{20,24},{24,28},{28,0},{1,5},{5... | collective-permute-start | bytes 1544 | tf_op jit(solution)/shard_map/ppermute | solution.py:27
  21.0 51.5 %collective-permute-start.18 = (f32[46,32,128]{2,1,0:T(8,128)}, f32[46,32,128]{2,1,0:T(8,128)}, u32[]{:S(2)}, u32[]{:S(2)}) collective-permute-start(f32[46,32,128]{2,1,0:T(8,128)} %far.23), channel_id=1, source_target_pairs={{0,4},{4,8},{8,12},{12,16},{16,20},{20,24},{24,28},{28,0},{1,5},{5... | collective-permute-start | bytes 2261000 | tf_op jit(solution)/shard_map/ppermute | solution.py:27
  24.3 50.5 %collective-permute-start.17 = (f32[46,32,128]{2,1,0:T(8,128)}, f32[46,32,128]{2,1,0:T(8,128)}, u32[]{:S(2)}, u32[]{:S(2)}) collective-permute-start(f32[46,32,128]{2,1,0:T(8,128)} %pack.6), channel_id=1, source_target_pairs={{0,28},{4,0},{8,4},{12,8},{16,12},{20,16},{24,20},{28,24},{1,29},{... | collective-permute-start | bytes 2261000 | tf_op jit(solution)/shard_map/ppermute | solution.py:27
  33.8 7.2 %copy-start.1 = (f32[8192]{0:T(1024)S(1)}, f32[8192]{0:T(1024)}, u32[]{:S(2)}) copy-start(f32[8192]{0:T(1024)} %param.13) | copy-start | bytes 98308
  33.8 7.2 %copy-start.2 = (f32[8192]{0:T(1024)S(1)}, f32[8192]{0:T(1024)}, u32[]{:S(2)}) copy-start(f32[8192]{0:T(1024)} %param.14) | copy-start | bytes 98308
  33.8 70.7 %collective-permute-start.20 = (f32[46,32,128]{2,1,0:T(8,128)}, f32[46,32,128]{2,1,0:T(8,128)S(1)}, u32[]{:S(2)}, u32[]{:S(2)}) collective-permute-start(f32[46,32,128]{2,1,0:T(8,128)} %far.25), channel_id=1, source_target_pairs={{0,4},{4,8},{8,12},{12,16},{16,20},{20,24},{24,28},{28,0},{1,5},{5... | collective-permute-start | bytes 2261000 | tf_op jit(solution)/shard_map/ppermute | solution.py:27
  35.6 68.9 %collective-permute-start.19 = (f32[46,32,128]{2,1,0:T(8,128)}, f32[46,32,128]{2,1,0:T(8,128)}, u32[]{:S(2)}, u32[]{:S(2)}) collective-permute-start(f32[46,32,128]{2,1,0:T(8,128)} %pack.7), channel_id=1, source_target_pairs={{0,28},{4,0},{8,4},{12,8},{16,12},{20,16},{24,20},{28,24},{1,29},{... | collective-permute-start | bytes 2261000 | tf_op jit(solution)/shard_map/ppermute | solution.py:27
  84.8 45.8 %collective-permute-start.21 = (f32[46,32,128]{2,1,0:T(8,128)}, f32[46,32,128]{2,1,0:T(8,128)}, u32[]{:S(2)}, u32[]{:S(2)}) collective-permute-start(f32[46,32,128]{2,1,0:T(8,128)} %get-tuple-element.221), channel_id=1, source_target_pairs={{0,28},{4,0},{8,4},{12,8},{16,12},{20,16},{24,20},{28,24},{1,29},{... | collective-permute-start | bytes 2261000 | tf_op jit(solution)/shard_map/ppermute | solution.py:27
  86.6 50.3 %collective-permute-start.22 = (f32[46,32,128]{2,1,0:T(8,128)}, f32[46,32,128]{2,1,0:T(8,128)}, u32[]{:S(2)}, u32[]{:S(2)}) collective-permute-start(f32[46,32,128]{2,1,0:T(8,128)} %get-tuple-element.222), channel_id=1, source_target_pairs={{0,4},{4,8},{8,12},{12,16},{16,20},{20,24},{24,28},{28,0},{1,5},{5... | collective-permute-start | bytes 2261000 | tf_op jit(solution)/shard_map/ppermute | solution.py:27
  115.6 47.0 %collective-permute-start.23 = (f32[46,32,128]{2,1,0:T(8,128)}, f32[46,32,128]{2,1,0:T(8,128)S(1)}, u32[]{:S(2)}, u32[]{:S(2)}) collective-permute-start(f32[46,32,128]{2,1,0:T(8,128)} %get-tuple-element.227), channel_id=1, source_target_pairs={{0,28},{4,0},{8,4},{12,8},{16,12},{20,16},{24,20},{28,24},{1,29},{... | collective-permute-start | bytes 2261000 | tf_op jit(solution)/shard_map/ppermute | solution.py:27
  119.2 50.0 %collective-permute-start.24 = (f32[46,32,128]{2,1,0:T(8,128)}, f32[46,32,128]{2,1,0:T(8,128)}, u32[]{:S(2)}, u32[]{:S(2)}) collective-permute-start(f32[46,32,128]{2,1,0:T(8,128)} %get-tuple-element.228), channel_id=1, source_target_pairs={{0,4},{4,8},{8,12},{12,16},{16,20},{20,24},{24,28},{28,0},{1,5},{5... | collective-permute-start | bytes 2261000 | tf_op jit(solution)/shard_map/ppermute | solution.py:27
  147.7 50.5 %collective-permute-start.25 = (f32[46,32,128]{2,1,0:T(8,128)}, f32[46,32,128]{2,1,0:T(8,128)}, u32[]{:S(2)}, u32[]{:S(2)}) collective-permute-start(f32[46,32,128]{2,1,0:T(8,128)} %get-tuple-element.233), channel_id=1, source_target_pairs={{0,28},{4,0},{8,4},{12,8},{16,12},{20,16},{24,20},{28,24},{1,29},{... | collective-permute-start | bytes 2261000 | tf_op jit(solution)/shard_map/ppermute | solution.py:27
  151.3 50.1 %collective-permute-start.26 = (f32[46,32,128]{2,1,0:T(8,128)}, f32[46,32,128]{2,1,0:T(8,128)}, u32[]{:S(2)}, u32[]{:S(2)}) collective-permute-start(f32[46,32,128]{2,1,0:T(8,128)} %get-tuple-element.234), channel_id=1, source_target_pairs={{0,4},{4,8},{8,12},{12,16},{16,20},{20,24},{24,28},{28,0},{1,5},{5... | collective-permute-start | bytes 2261000 | tf_op jit(solution)/shard_map/ppermute | solution.py:27
  162.5 6.6 %copy-start.10 = (f32[46,32,128]{2,1,0:T(8,128)}, f32[46,32,128]{2,1,0:T(8,128)S(1)}, u32[]{:S(2)}) copy-start(f32[46,32,128]{2,1,0:T(8,128)S(1)} %collective-permute-done.23.refs_4_) | copy-start | bytes 2260996
  180.1 46.0 %collective-permute-start.27 = (f32[46,32,128]{2,1,0:T(8,128)}, f32[46,32,128]{2,1,0:T(8,128)S(1)}, u32[]{:S(2)}, u32[]{:S(2)}) collective-permute-start(f32[46,32,128]{2,1,0:T(8,128)} %get-tuple-element.248), channel_id=1, source_target_pairs={{0,28},{4,0},{8,4},{12,8},{16,12},{20,16},{24,20},{28,24},{1,29},{... | collective-permute-start | bytes 2261000 | tf_op jit(solution)/shard_map/ppermute | solution.py:27
  184.3 50.2 %collective-permute-start.28 = (f32[46,32,128]{2,1,0:T(8,128)}, f32[46,32,128]{2,1,0:T(8,128)}, u32[]{:S(2)}, u32[]{:S(2)}) collective-permute-start(f32[46,32,128]{2,1,0:T(8,128)} %get-tuple-element.249), channel_id=1, source_target_pairs={{0,4},{4,8},{8,12},{12,16},{16,20},{20,24},{24,28},{28,0},{1,5},{5... | collective-permute-start | bytes 2261000 | tf_op jit(solution)/shard_map/ppermute | solution.py:27
  234.5 18.8 %copy-start.15 = (f32[64]{0:T(128)S(1)}, f32[64]{0:T(128)}, u32[]{:S(2)}) copy-start(f32[64]{0:T(128)} %param.19) | copy-start | bytes 772
  234.5 19.4 %copy-start.16 = (f32[64]{0:T(128)S(1)}, f32[64]{0:T(128)}, u32[]{:S(2)}) copy-start(f32[64]{0:T(128)} %param.19) | copy-start | bytes 772
  238.7 4.4 %collective-permute-start.29 = (f32[136,128]{1,0:T(8,128)S(1)}, f32[136,128]{1,0:T(8,128)S(1)}, u32[]{:S(2)}, u32[]{:S(2)}) collective-permute-start(f32[136,128]{1,0:T(8,128)S(1)} %maximum_maximum_fusion.1), channel_id=1, source_target_pairs={{0,4},{4,0},{8,12},{12,8},{16,20},{20,16},{24,28},{28,24},{1,5},{5... | collective-permute-start | bytes 208904 | tf_op jit(solution)/shard_map/ppermute | solution.py:580
  243.9 6.8 %collective-permute-start.32 = (f32[136,128]{1,0:T(8,128)S(1)}, f32[136,128]{1,0:T(8,128)S(1)}, u32[]{:S(2)}, u32[]{:S(2)}) collective-permute-start(f32[136,128]{1,0:T(8,128)S(1)} %fusion.1), channel_id=1, source_target_pairs={{0,24},{4,28},{8,16},{12,20},{16,8},{20,12},{24,0},{28,4},{1,25},{... | collective-permute-start | bytes 208904 | tf_op jit(solution)/shard_map/ppermute | solution.py:580
  247.4 5.2 %collective-permute-start.31 = (f32[136,128]{1,0:T(8,128)S(1)}, f32[136,128]{1,0:T(8,128)S(1)}, u32[]{:S(2)}, u32[]{:S(2)}) collective-permute-start(f32[136,128]{1,0:T(8,128)S(1)} %fusion.1), channel_id=1, source_target_pairs={{0,16},{4,20},{8,24},{12,28},{16,0},{20,4},{24,8},{28,12},{1,17},{... | collective-permute-start | bytes 208904 | tf_op jit(solution)/shard_map/ppermute | solution.py:580
  247.4 5.2 %collective-permute-start.30 = (f32[136,128]{1,0:T(8,128)S(1)}, f32[136,128]{1,0:T(8,128)S(1)}, u32[]{:S(2)}, u32[]{:S(2)}) collective-permute-start(f32[136,128]{1,0:T(8,128)S(1)} %fusion.1), channel_id=1, source_target_pairs={{0,8},{4,12},{8,0},{12,4},{16,24},{20,28},{24,16},{28,20},{1,9},{5... | collective-permute-start | bytes 208904 | tf_op jit(solution)/shard_map/ppermute | solution.py:580
  (6 other events, 18.6 us)
Sparse Core Ops, SparseCore 0:
  185.9 32.5 all-reduce.6
where the time goes:
time: 262 us
  Pallas kernels  153 us (58%)
  waiting for transfers between devices  52.5 us (20%)
  starting transfers between devices  32.2 us (12%)
  between operations  16.3 us (6%)
  other arithmetic  3.77 us (1%)
  local copies, waits for them, and re-layouts  2.97 us (1%)
    pallas_call x8, Pallas kernels, far_call(): pl.pallas_call(functools.partial(far_kernel, bands=bands, side=side, cap=...  70 us
    pallas_call x6, Pallas kernels, near_call(): pl.pallas_call(functools.partial(near_kernel, bands=bands, side=side, x_r...  64.5 us
    ppermute x13, waiting for transfers between devices, passed_along(): return lax.ppermute(value, 'rows', pairs)  36.6 us
    ppermute x13, starting transfers between devices, passed_along(): return lax.ppermute(value, 'rows', pairs)  26.1 us
    psum x1, waiting for transfers between devices, two_steps(): lax.psum((jnp.sum(start, axis=0, keepdims=True), sum(columns[1:], columns...  9.45 us
    pallas_call x2, Pallas kernels, end_call(): pl.pallas_call(functools.partial(end_kernel, cap=cap, scale_at=scale_at),...  6.7 us
    ppermute x4, waiting for transfers between devices, summed_over_rows(): value = value + lax.ppermute(own, 'rows', pairs)  6.4 us
    ppermute x4, starting transfers between devices, summed_over_rows(): value = value + lax.ppermute(own, 'rows', pairs)  6.01 us
  transfers between devices with their start and end apart: 18, of which 10 were waited for; matrix products, arithmetic and copies ran while one was open for 1% of the time, Pallas kernels for 56%

commit v1 on v0

--- a/solution.py
+++ b/solution.py
@@ -51,54 +51,65 @@
     return jnp.concatenate([high, low], axis=0)
 
 
-def plan_kernel(first_ref, cols_ref, count_ref, far_ref, near_ref, seen, *, bands, slots, nblocks):
+def local_column(cols_ref, r, s, first, bands, nblocks):
+    raw = cols_ref[s, r] - first
+    return jnp.where(raw < 0, raw + nblocks, raw)
+
+
+def tiles_kernel(first_ref, cols_ref, count_ref, tiles_ref, place_ref, *, bands, slots, nblocks):
     first = first_ref[0]
 
     def clear(i, _):
-        seen[i] = 0
+        place_ref[i] = 0
         return 0
 
     lax.fori_loop(0, bands, clear, 0, unroll=8)
+
+    def by_row(r, _):
+        live = count_ref[r]
+        for s in range(1, slots):
+            col = local_column(cols_ref, r, s, first, bands, nblocks)
+            far = jnp.logical_and(s < live, col >= bands)
+            place_ref[jnp.where(far, col - bands, bands)] = 1
+        return 0
+
+    lax.fori_loop(0, bands, by_row, 0, unroll=4)
+
+    def by_tile(m, tiles):
+        tiles_ref[LIST_AT + tiles] = m
+        used = place_ref[m]
+        place_ref[m] = tiles
+        return tiles + used
+
+    tiles_ref[1] = lax.fori_loop(0, bands, by_tile, jnp.int32(0), unroll=4)
+
+
+def edges_kernel(
+    first_ref, cols_ref, count_ref, place_ref, far_ref, near_ref, *, bands, slots, nblocks
+):
+    first = first_ref[0]
 
     def by_row(r, counts):
         edges, nears = counts
         live = count_ref[r]
         for s in range(1, slots):
-            raw = cols_ref[s, r] - first
-            col = jnp.where(raw < 0, raw + nblocks, raw)
+            col = local_column(cols_ref, r, s, first, bands, nblocks)
             is_live = s < live
             near = jnp.logical_and(is_live, col < bands)
             far = jnp.logical_and(is_live, col >= bands)
             far_ref[ROW_AT + edges] = r
             far_ref[SLOT_AT + edges] = s
-            far_ref[PLACE_AT + edges] = col - bands
+            far_ref[PLACE_AT + edges] = place_ref[jnp.where(far, col - bands, 0)]
             near_ref[ROW_AT + nears] = r
             near_ref[SLOT_AT + nears] = s
             near_ref[PLACE_AT + nears] = col
-            seen[jnp.where(far, col - bands, bands)] = 1
             edges = edges + far.astype(jnp.int32)
             nears = nears + near.astype(jnp.int32)
         return edges, nears
 
-    edges, nears = lax.fori_loop(0, bands, by_row, (jnp.int32(0), jnp.int32(0)), unroll=2)
+    edges, nears = lax.fori_loop(0, bands, by_row, (jnp.int32(0), jnp.int32(0)), unroll=4)
     far_ref[0] = edges
     near_ref[0] = nears
-
-    def by_tile(m, tiles):
-        far_ref[LIST_AT + tiles] = m
-        used = seen[m]
-        seen[m] = tiles
-        return tiles + used
-
-    tiles = lax.fori_loop(0, bands, by_tile, jnp.int32(0), unroll=4)
-    far_ref[1] = tiles
-
-    def by_edge(e, _):
-        far_ref[PLACE_AT + e] = seen[far_ref[PLACE_AT + e]]
-        return 0
-
-    lax.fori_loop(0, edges, by_edge, 0)
-
     for i in range(GROUP):
         far_ref[ROW_AT + edges + i] = bands
         far_ref[SLOT_AT + edges + i] = 0
@@ -192,7 +203,10 @@
     put_w.wait()
 
 
-def far_kernel(*refs, bands, side, cap, x_row, scale_at, receives, sends, ends, step_at=2):
+def far_kernel(
+    *refs, bands, side, cap, x_row, scale_at, receives, sends, ends, dots=False,
+    out_row=0, follows=False, step_at=2,
+):
     refs = list(refs)
 
     def take(count):
@@ -203,12 +217,19 @@
     (meta_ref, blocks_hbm) = take(2)
     if receives:
         coef_ref, w_hbm, halo_hbm = take(3)
-    if receives and sends:
         given_ref, carry_hbm = take(2)
     if sends:
         (x_hbm,) = take(1)
+    if ends:
+        (before_ref,) = take(1)
+    if dots:
+        (off_hbm,) = take(1)
+    if follows:
+        take(1)
     if receives:
         (v_out,) = take(1)
+    if dots:
+        (dot_out,) = take(1)
     if receives and sends:
         x_out, halo_out = take(2)
     if ends:
@@ -217,9 +238,11 @@
         (carry_out,) = take(1)
     raw, both, sem_of, sems = take(4)
     if receives:
-        vel, halo_buf, halo_split = take(3)
+        vel, halo_buf, halo_split, carry_buf = take(4)
     if receives and sends:
-        carry_buf, packed_buf = take(2)
+        (packed_buf,) = take(1)
+    if dots:
+        off_buf, sums = take(2)
     if sends:
         x_buf, split, sum_carry = take(3)
     chains = (vel if receives else x_buf).shape[0]
@@ -251,16 +274,21 @@
     if receives:
         get_halo = pltpu.make_async_copy(halo_hbm, halo_buf, sems.at[1])
         get_w = pltpu.make_async_copy(w_hbm, vel.at[:, pl.ds(0, cells)], sems.at[2])
-        put_v = pltpu.make_async_copy(vel.at[:, pl.ds(0, cells)], v_out, sems.at[3])
+        v_target = v_out if sends else v_out.at[pl.ds(out_row, chains)]
+        put_v = pltpu.make_async_copy(vel.at[:, pl.ds(0, cells)], v_target, sems.at[3])
         get_halo.start()
         get_w.start()
     if sends and not receives:
         get_x.start()
     lax.fori_loop(0, edges, start_fetch, 0)
-    if receives and sends:
+    if receives:
         get_carry = pltpu.make_async_copy(carry_hbm, carry_buf, sems.at[4])
         get_carry.start()
+    if receives and sends:
         get_x.start()
+    if dots:
+        get_off = pltpu.make_async_copy(off_hbm, off_buf, sems.at[5])
+        get_off.start()
 
     if receives:
         scale = coef_ref[scale_at]
@@ -288,7 +316,7 @@
             return 0
 
         lax.fori_loop(0, groups, up_group, 0)
-    if receives and sends:
+    if receives:
         given = jnp.minimum(given_ref[1], cap)
         get_carry.wait()
 
@@ -299,6 +327,9 @@
         lax.fori_loop(0, given, add_carry, 0)
     if receives:
         put_v.start()
+    if dots:
+        get_off.wait()
+        dot_out[...] = chain_sums(lambda part: vel[:, part] * off_buf[:, part], sums, cells)
     if sends:
         get_x.wait()
     if receives and sends:
@@ -306,7 +337,10 @@
         put_x = pltpu.make_async_copy(x_buf, x_out, sems.at[5])
         put_x.start()
         if ends:
-            column_out[...] = jnp.sum(x_buf[...], axis=0, keepdims=True)
+            column_out[:, :cells] = before_ref[:, :cells]
+            column_out[:, cells:] = before_ref[:, cells:] + jnp.sum(
+                x_buf[...], axis=0, keepdims=True
+            )
 
         def pack(k, _):
             packed_buf[k] = x_buf[:, tile_at(given_ref[LIST_AT + k])]
@@ -359,56 +393,53 @@
     lax.fori_loop(0, jnp.minimum(given_ref[1], cap), pack, 0)
 
 
-def end_kernel(given_ref, coef_ref, v_ref, carry_ref, off_ref, *rest, cap, scale_at):
-    out_ref, dot_ref, sums = rest[-3:]
-    side = carry_ref.shape[2]
-    scale = coef_ref[scale_at]
-    out_ref[...] = v_ref[...]
-
-    def add_carry(k, _):
-        tile = pl.ds(pl.multiple_of(given_ref[LIST_AT + k] * side, side), side)
-        out_ref[:, tile] -= scale * carry_ref[k]
+def chain_sums(piece, sums, cells):
+    wide = sums.shape[1]
+    side = wide // 4
+    sums[...] = jnp.zeros_like(sums)
+
+    def add(i, _):
+        sums[...] += piece(pl.ds(pl.multiple_of(i * wide, wide), wide))
         return 0
 
-    lax.fori_loop(0, jnp.minimum(given_ref[1], cap), add_carry, 0)
-    cells = v_ref.shape[1]
-    sums[...] = jnp.zeros_like(sums)
-    wide = 8 * side
-
-    def dot(i, _):
-        part = pl.ds(pl.multiple_of(i * wide, wide), wide)
-        sums[...] += out_ref[:, part] * off_ref[:, part]
-        return 0
-
-    lax.fori_loop(0, cells // wide, dot, 0)
-    dot_ref[...] = sum(sums[:, i * side : (i + 1) * side] for i in range(8))
+    lax.fori_loop(0, cells // wide, add, 0, unroll=2)
+    lanes = sum(sums[:, i * side : (i + 1) * side] for i in range(4))
+    return lax.dot_general(
+        jnp.ones((8, side), jnp.float32), lanes, NT,
+        precision=lax.Precision.HIGHEST, preferred_element_type=jnp.float32,
+    )
 
 
 def spread_kernel(
-    start_ref, *refs, side, chain_total
+    start_ref, x0_ref, x1_ref, v_ref, *refs, chain_total
 ):
-    *x_refs, sum_start_ref, sum_end_ref, position_ref, offset_ref, gain_ref, sums = refs
-    chains = x_refs[0].shape[0]
+    *column_refs, position_ref, offset_ref, gain_ref, dot_ref, sums, means = refs
+    chains = x0_ref.shape[0]
     cells = start_ref.shape[1]
-    sums[...] = jnp.zeros_like(sums)
-    wide = 4 * side
-
-    def one(i, _):
-        part = pl.ds(pl.multiple_of(i * wide, wide), wide)
-        mean_start = sum_start_ref[:, part] / chain_total
-        mean_end = sum_end_ref[:, part] / chain_total
-        for h, x_ref in enumerate(x_refs):
-            rows = pl.ds(h * chains, chains)
-            x = x_ref[:, part]
-            position_ref[rows, part] = x
-            off_end = x - mean_end
-            offset_ref[rows, part] = off_end
-            off_start = start_ref[rows, part] - mean_start
-            sums[rows] += off_end * off_end - off_start * off_start
-        return 0
-
-    lax.fori_loop(0, cells // wide, one, 0)
-    gain_ref[...] = sum(sums[:, i * side : (i + 1) * side] for i in range(4))
+    means[...] = sum(ref[...] for ref in column_refs) / chain_total
+    upper = pl.ds(0, chains)
+    lower = pl.ds(chains, chains)
+
+    def ends(part):
+        mean_start = means[:, part]
+        mean_end = means[:, pl.ds(pl.multiple_of(cells + part.start, 128), part.size)]
+        x0 = x0_ref[:, part]
+        x1 = x1_ref[:, part]
+        position_ref[upper, part] = x0
+        position_ref[lower, part] = x1
+        off_start = start_ref[:, part] - mean_start
+        off1 = x1 - mean_end
+        offset_ref[:, part] = off1
+        off_end = jnp.concatenate([x0 - mean_end, off1], axis=0)
+        return off_end * off_end - off_start * off_start
+
+    gain_ref[...] = chain_sums(ends, sums, cells)
+
+    def first_dot(part):
+        mean_end = means[:, pl.ds(pl.multiple_of(cells + part.start, 128), part.size)]
+        return (x0_ref[:, part] - mean_end) * v_ref[:, part]
+
+    dot_ref[...] = chain_sums(first_dot, sums.at[upper], cells)
 
 
 SMEM = pl.BlockSpec(memory_space=pltpu.SMEM)
@@ -447,15 +478,19 @@
     )(near_list, coef, x, v, seen, weight, blocks)
 
 
-def far_call(meta, given, coef, blocks, x, w, halo, carry, chains, x_row, scale_at, cap, ends=False):
+def far_call(
+    meta, given, coef, blocks, x, w, halo, carry, chains, x_row, scale_at, cap, before=None,
+    offset=None, earlier=None, out_row=0,
+):
     bands, slots, side, _ = blocks.shape
     cells = bands * side
     receives, sends = w is not None, x is not None
+    ends, dots, follows = before is not None, offset is not None, earlier is not None
     most = bands * (slots - 1) + GROUP
     state = jax.ShapeDtypeStruct((chains, cells), jnp.float32)
     parcel = jax.ShapeDtypeStruct((cap, chains, side), jnp.float32)
     in_specs, args = [SMEM, ANY], [meta, blocks]
-    out_shape = []
+    out_shape, out_specs = [], []
     scratch = [
         pltpu.VMEM((most, side, side), jnp.float32),
         pltpu.VMEM((most, 2 * side, side), jnp.bfloat16),
@@ -463,42 +498,62 @@
         pltpu.SemaphoreType.DMA((8,)),
     ]
     if receives:
-        in_specs += [SMEM, ANY, ANY]
-        args += [coef, w, halo]
-        out_shape += [state]
+        in_specs += [SMEM, ANY, ANY, SMEM, ANY]
+        args += [coef, w, halo, given, carry]
+        full = jax.ShapeDtypeStruct((CHUNKS * chains, cells), jnp.float32)
+        out_shape += [state if sends else full]
+        out_specs += [ANY]
         scratch += [
             pltpu.VMEM((chains, cells + side), jnp.float32),
             pltpu.VMEM((cap, chains, side), jnp.float32),
             pltpu.VMEM((cap + 1, 2 * chains, side), jnp.bfloat16),
+            pltpu.VMEM((cap, chains, side), jnp.float32),
         ]
     if receives and sends:
-        in_specs += [SMEM, ANY]
-        args += [given, carry]
         out_shape += [state, parcel]
+        out_specs += [ANY, ANY]
         if ends:
-            out_shape += [jax.ShapeDtypeStruct((1, cells), jnp.float32)]
+            out_shape += [jax.ShapeDtypeStruct(before.shape, jnp.float32)]
+            out_specs += [VMEM]
+        scratch += [pltpu.VMEM((cap, chains, side), jnp.float32)]
+    if dots:
+        in_specs += [ANY]
+        args += [offset]
+        out_shape += [jax.ShapeDtypeStruct((8, chains), jnp.float32)]
+        out_specs += [VMEM]
         scratch += [
-            pltpu.VMEM((cap, chains, side), jnp.float32),
-            pltpu.VMEM((cap, chains, side), jnp.float32),
+            pltpu.VMEM((chains, cells), jnp.float32),
+            pltpu.VMEM((chains, 4 * side), jnp.float32),
         ]
     if sends:
         in_specs += [ANY]
         args += [x]
         out_shape += [parcel]
+        out_specs += [ANY]
         scratch += [
             pltpu.VMEM((chains, cells), jnp.float32),
             pltpu.VMEM((2 * chains, cells + side), jnp.bfloat16),
             pltpu.VMEM((cap + 1, chains, side), jnp.float32),
         ]
+    if ends:
+        in_specs += [VMEM]
+        args += [before]
+    aliases = {}
+    if follows:
+        aliases = {len(args): 0}
+        in_specs += [ANY]
+        args += [earlier]
     return pl.pallas_call(
         functools.partial(
             far_kernel, bands=bands, side=side, cap=cap, x_row=x_row, scale_at=scale_at,
-            receives=receives, sends=sends, ends=ends,
+            receives=receives, sends=sends, ends=ends, dots=dots, out_row=out_row,
+            follows=follows,
         ),
         out_shape=out_shape,
         in_specs=in_specs,
-        out_specs=[VMEM if o.shape == (1, cells) else ANY for o in out_shape],
+        out_specs=out_specs,
         scratch_shapes=scratch,
+        input_output_aliases=aliases,
         compiler_params=PARAMS,
         cost_estimate=COST,
         name="far",
@@ -518,66 +573,49 @@
     )(given, x)
 
 
-def end_call(given, coef, v, carry, offset, earlier, part, scale_at):
-    cap, chains, side = carry.shape
-    cells = v.shape[1]
-    in_specs = [
-        SMEM,
-        SMEM,
-        pl.BlockSpec((chains, cells), lambda i: (0, 0)),
-        pl.BlockSpec((cap, chains, side), lambda i: (0, 0, 0)),
-        pl.BlockSpec((chains, cells), lambda i: (part, 0)),
-    ]
-    args = [given, coef, v, carry, offset]
-    if earlier is not None:
-        in_specs.append(ANY)
-        args.append(earlier)
+def spread_call(start, x, v, columns, side, chain_total):
+    local_chains, cells = start.shape
+    chains = x[0].shape[0]
     return pl.pallas_call(
-        functools.partial(end_kernel, cap=cap, scale_at=scale_at),
+        functools.partial(spread_kernel, chain_total=chain_total),
         out_shape=[
-            jax.ShapeDtypeStruct(offset.shape, jnp.float32),
-            jax.ShapeDtypeStruct((chains, side), jnp.float32),
+            jax.ShapeDtypeStruct(start.shape, jnp.float32),
+            jax.ShapeDtypeStruct((chains, cells), jnp.float32),
+            jax.ShapeDtypeStruct((8, local_chains), jnp.float32),
+            jax.ShapeDtypeStruct((8, chains), jnp.float32),
         ],
         grid=(1,),
-        in_specs=in_specs,
-        out_specs=[
-            pl.BlockSpec((chains, cells), lambda i: (part, 0)),
-            pl.BlockSpec((chains, side), lambda i: (0, 0)),
+        in_specs=[VMEM, VMEM, VMEM, pl.BlockSpec((chains, cells), lambda i: (0, 0))]
+        + [VMEM] * len(columns),
+        out_specs=[VMEM] * 4,
+        scratch_shapes=[
+            pltpu.VMEM((local_chains, 4 * side), jnp.float32),
+            pltpu.VMEM((1, 2 * cells), jnp.float32),
         ],
-        scratch_shapes=[pltpu.VMEM((chains, 8 * side), jnp.float32)],
-        input_output_aliases={} if earlier is None else {5: 0},
-        compiler_params=PARAMS,
-        cost_estimate=COST,
-        name="end",
-    )(*args)
-
-
-def spread_call(start, x, total_start, total_end, side, chain_total):
-    return pl.pallas_call(
-        functools.partial(spread_kernel, side=side, chain_total=chain_total),
-        out_shape=[
-            jax.ShapeDtypeStruct(start.shape, jnp.float32),
-            jax.ShapeDtypeStruct(start.shape, jnp.float32),
-            jax.ShapeDtypeStruct((start.shape[0], side), jnp.float32),
-        ],
-        in_specs=[VMEM] * (3 + len(x)),
-        out_specs=[VMEM] * 3,
-        scratch_shapes=[pltpu.VMEM((start.shape[0], 4 * side), jnp.float32)],
         compiler_params=PARAMS,
         cost_estimate=COST,
         name="spread",
-    )(start, *x, total_start, total_end)
-
-
-def summed_over_rows(value):
-    count = lax.axis_size("rows")
+    )(start, *x, v, *columns)
+
+
+def shared_over(axis, value):
+    count = lax.axis_size(axis)
+    shared = [value]
+    for k in range(1, count):
+        pairs = [(source, (source + k) % count) for source in range(count)]
+        shared.append(lax.ppermute(value, axis, pairs))
+    return shared
+
+
+def summed_over(axis, value):
+    count = lax.axis_size(axis)
     reach = 1
     while reach < count:
-        radix = 2 if reach == 1 else 4 if count % (4 * reach) == 0 else 2
+        radix = 4 if count % (4 * reach) == 0 and (reach > 1 or count == 4) else 2
         own = value
         for k in range(1, radix):
             pairs = [(source, source ^ (k * reach)) for source in range(count)]
-            value = value + lax.ppermute(own, "rows", pairs)
+            value = value + lax.ppermute(own, axis, pairs)
         reach *= radix
     return value
 
@@ -593,77 +631,84 @@
     all_cells = cells * lax.axis_size("rows")
     chain_total = local_chains * lax.axis_size("grp")
     first = (lax.axis_index("rows") * bands).astype(jnp.int32).reshape(1)
+    plan = (first, block_cols.T, block_count)
+    sizes = dict(bands=bands, slots=slots, nblocks=nblocks)
+    tiles, places = pl.pallas_call(
+        functools.partial(tiles_kernel, **sizes),
+        out_shape=[
+            jax.ShapeDtypeStruct((ROW_AT,), jnp.int32),
+            jax.ShapeDtypeStruct((bands + 8,), jnp.int32),
+        ],
+        in_specs=[SMEM] * 3,
+        out_specs=[SMEM] * 2,
+        cost_estimate=COST,
+        name="tiles",
+    )(*plan)
+    given = passed_along(tiles, 1)
     meta, near_list = pl.pallas_call(
-        functools.partial(plan_kernel, bands=bands, slots=slots, nblocks=nblocks),
+        functools.partial(edges_kernel, **sizes),
         out_shape=[jax.ShapeDtypeStruct((META,), jnp.int32)] * 2,
-        in_specs=[SMEM, SMEM, SMEM],
-        out_specs=[SMEM, SMEM],
-        scratch_shapes=[pltpu.SMEM((bands + 8,), jnp.int32)],
-        name="plan",
-    )(first, block_cols.T, block_count)
-    given = passed_along(meta[:ROW_AT], 1)
+        in_specs=[SMEM] * 4,
+        out_specs=[SMEM] * 2,
+        cost_estimate=COST,
+        name="edges",
+    )(*plan, places)
     step_len = step_size[0]
     coef = jnp.stack([step_len / 2, step_len, step_len])
     seen = observed.reshape(1, cells)
     weight = precision_obs.reshape(1, cells)
     parts = range(CHUNKS)
+    first_rows = [h * chains for h in parts]
+
+    def near(x, v, x_row, v_row, scale_at):
+        return near_call(
+            near_list, coef, x, v, seen, weight, blocks, chains, x_row, v_row, scale_at
+        )
 
     def two_steps(cap, start, momenta):
         far = functools.partial(far_call, meta, given, coef, blocks)
-
-        def near(x, v, x_row, v_row, scale_at):
-            return near_call(
-                near_list, coef, x, v, seen, weight, blocks, chains, x_row, v_row, scale_at
+        x, v, w, flight = [start] * CHUNKS, [momenta] * CHUNKS, [], []
+        rows = list(first_rows)
+        edges = meta
+        for h in parts:
+            halo = pack_call(given, start, chains, h, cap, side)
+            edges, halo = lax.optimization_barrier((edges, halo))
+            (carry,) = far_call(
+                edges, given, coef, blocks, start, None, None, None, chains, rows[h], 0, cap
             )
-
-        x, v, w, flight = [start] * CHUNKS, [momenta] * CHUNKS, [], []
-        rows = [h * chains for h in parts]
-        for h in parts:
-            (carry,) = far(start, None, None, None, chains, rows[h], 0, cap)
-            halo = pack_call(given, start, chains, h, cap, side)
             flight.append((passed_along(halo, -1), passed_along(carry, 1)))
         for h in parts:
             w.append(near(start, momenta, rows[h], rows[h], 0))
         w = list(lax.optimization_barrier(tuple(w)))
-        columns = []
+        column = jnp.concatenate(
+            [jnp.sum(start, axis=0, keepdims=True), jnp.zeros((1, cells), jnp.float32)], axis=1
+        )
         for turn in range(2):
             for h in parts:
                 halo, carry = flight[h]
-                v[h], x[h], halo, *column, carry = far(
-                    x[h], w[h], halo, carry, chains, rows[h], turn, cap, turn == 1
+                before = column if turn == 1 else None
+                v[h], x[h], halo, *after, carry = far(
+                    x[h], w[h], halo, carry, chains, rows[h], turn, cap, before
                 )
-                columns += column
+                if after:
+                    (column,) = after
                 flight[h] = (passed_along(halo, -1), passed_along(carry, 1))
                 rows[h] = 0
                 w[h] = near(x[h], v[h], 0, 0, 1 - turn)
                 w = list(lax.optimization_barrier(tuple(w)))
-        total_start, total_end = lax.psum(
-            (jnp.sum(start, axis=0, keepdims=True), sum(columns[1:], columns[0])), "grp"
+        column, w[1] = lax.optimization_barrier((column, w[1]))
+        (momentum,) = far(None, w[0], *flight[0], chains, 0, 0, cap)
+        position, offset, gain, dot = spread_call(
+            start, x, momentum, shared_over("grp", column), side, chain_total
         )
-        momentum, dots = None, []
-        for h in parts:
-            halo, carry = flight[h]
-            if h < CHUNKS - 1:
-                halo, carry = lax.optimization_barrier((halo, carry))
-            (v[h],) = far(None, w[h], halo, None, chains, 0, 0, cap)
-            if h == 0:
-                v[0], total_start, total_end = lax.optimization_barrier(
-                    (v[0], total_start, total_end)
-                )
-                position, offset, gain = spread_call(
-                    start, x, total_start, total_end, side, chain_total
-                )
-            momentum, dot = end_call(given, coef, v[h], carry, offset, momentum, h, 0)
-            dots.append(dot)
-            if h < CHUNKS - 1:
-                w[h + 1], momentum = lax.optimization_barrier((w[h + 1], momentum))
-        over = jnp.broadcast_to((meta[1] > cap).astype(jnp.float32), (8, side))
-        sums = summed_over_rows(jnp.concatenate([gain, *dots, over], axis=0))
-        per_chain = jnp.sum(sums, axis=1)
-        spread = per_chain[:local_chains]
-        inner = per_chain[local_chains : 2 * local_chains]
+        momentum, last_dot = far(
+            None, w[1], *flight[1], chains, 0, 0, cap, None, offset, momentum, chains
+        )
+        over = jnp.full((8, 8), (tiles[1] > cap).astype(jnp.float32))
+        sums = summed_over("rows", jnp.concatenate([gain, dot, last_dot, over], axis=1))[0]
+        spread, inner = sums[:local_chains], sums[local_chains : 2 * local_chains]
         chees = trajectory * (spread / all_cells) * (inner / all_cells)
-        return sums[-1, 0], position, momentum, chees
+        return sums[-1], position, momentum, chees
 
     cap = min(CAP, bands)
     results = two_steps(cap, start, momenta)

time: 262 us -> 244 us (0.931)
  between operations: 16.3 us -> 3.07 us
  waiting for transfers between devices: 52.5 us -> 49.3 us
  local copies, waits for them, and re-layouts: 2.97 us -> 6.04 us
    psum x1 -> x0, waiting for transfers between devices: 9.45 us -> none  [two_steps(): lax.psum((jnp.sum(start, axis=0, keepdims=True), sum(columns[1:], columns...]
    ppermute x13, waiting for transfers between devices: 36.6 us -> 41.7 us  [passed_along(): return lax.ppermute(value, 'rows', pairs)]
    pallas_call x4 -> x3, Pallas kernels: 15.1 us -> 10.6 us  [the longest x1 4.79 us: spread_call(): pl.pallas_call(functools.partial(spread_kernel, chain_total=chain_total),...]
    ppermute x13, starting transfers between devices: 26.1 us -> 23.4 us  [passed_along(): return lax.ppermute(value, 'rows', pairs)]
    ppermute x4 -> x7, starting transfers between devices: 6.01 us -> 8.53 us  [the longest x4 6.77 us: summed_over(): value = value + lax.ppermute(own, axis, pairs)]
    ppermute x4 -> x7, waiting for transfers between devices: 6.4 us -> 7.66 us  [the longest x4 7.65 us: summed_over(): value = value + lax.ppermute(own, axis, pairs)]
  transfers between devices with their start and end apart: 18 -> 20, of which waited for: 10 -> 12; matrix products, arithmetic and copies ran while one was open for 1% -> 1% of each run, Pallas kernels for 56% -> 54%
where the time goes in v1:
time: 244 us
  Pallas kernels  151 us (62%)
  waiting for transfers between devices  49.3 us (20%)
  starting transfers between devices  32 us (13%)
  local copies, waits for them, and re-layouts  6.04 us (2%)
  between operations  3.07 us (1%)
    pallas_call x8, Pallas kernels, far_call(): pl.pallas_call(functools.partial(far_kernel, bands=bands, side=side, cap=...  71.4 us
    pallas_call x6, Pallas kernels, near_call(): pl.pallas_call(functools.partial(near_kernel, bands=bands, side=side, x_r...  64.5 us
    ppermute x13, waiting for transfers between devices, passed_along(): return lax.ppermute(value, 'rows', pairs)  41.7 us
    ppermute x13, starting transfers between devices, passed_along(): return lax.ppermute(value, 'rows', pairs)  23.4 us
    ppermute x4, waiting for transfers between devices, summed_over(): value = value + lax.ppermute(own, axis, pairs)  7.65 us
    ppermute x4, starting transfers between devices, summed_over(): value = value + lax.ppermute(own, axis, pairs)  6.77 us
  transfers between devices with their start and end apart: 20, of which 12 were waited for; matrix products, arithmetic and copies ran while one was open for 1% of the time, Pallas kernels for 54%

profile of v1, /device:TPU:0, one launch (start us, length us, event | category | flops | bytes accessed | tf_op | source)
XLA Modules:
  0.0 244.1 jit_solution(2027343548525130649)
XLA Ops:
  13.4 6.3 %far.30 = f32[46,32,128]{2,1,0:T(8,128)} custom-call(s32[896]{0:T(1024)S(1)} %get-tuple-element.259.refs_0_, f32[64,4,128,128]{3,2,1,0:T(8,128)} %refs_1_.15, f32[64,8192]{1,0:T(8,128)S(1)} %copy-done), custom_call_target="tpu_custom_call" | custom-call | flops 1000 | bytes 1000 | tf_op jit(solution)/shard_map/far/pallas_call | solution.py:546
  19.8 4.6 %collective-permute-start.20 = (f32[46,32,128]{2,1,0:T(8,128)}, f32[46,32,128]{2,1,0:T(8,128)}, u32[]{:S(2)}, u32[]{:S(2)}) collective-permute-start(f32[46,32,128]{2,1,0:T(8,128)} %pack.8), channel_id=1, source_target_pairs={{0,28},{4,0},{8,4},{12,8},{16,12},{20,16},{24,20},{28,24},{1,29},{... | collective-permute-start | bytes 2261000 | tf_op jit(solution)/shard_map/ppermute | solution.py:27
  26.2 6.3 %far.32 = f32[46,32,128]{2,1,0:T(8,128)} custom-call(s32[896]{0:T(1024)S(1)} %get-tuple-element.259.refs_0_, f32[64,4,128,128]{3,2,1,0:T(8,128)} %refs_1_.15, f32[64,8192]{1,0:T(8,128)S(1)} %copy-done), custom_call_target="tpu_custom_call" | custom-call | flops 1000 | bytes 1000 | tf_op jit(solution)/shard_map/far/pallas_call | solution.py:546
  32.6 4.7 %collective-permute-start.22 = (f32[46,32,128]{2,1,0:T(8,128)}, f32[46,32,128]{2,1,0:T(8,128)S(1)}, u32[]{:S(2)}, u32[]{:S(2)}) collective-permute-start(f32[46,32,128]{2,1,0:T(8,128)} %pack.9), channel_id=1, source_target_pairs={{0,28},{4,0},{8,4},{12,8},{16,12},{20,16},{24,20},{28,24},{1,29},{... | collective-permute-start | bytes 2261000 | tf_op jit(solution)/shard_map/ppermute | solution.py:27
  38.1 9.8 %near.25.refs_3_ = f32[32,8192]{1,0:T(8,128)} custom-call(s32[896]{0:T(1024)S(1)} %get-tuple-element.500.list_ref, f32[3]{0:T(128)S(1)} %pad_maximum_fusion.coef_ref.refs_2_, f32[64,8192]{1,0:T(8,128)S(1)} %copy-done, f32[64,8192]{1,0:T(8,128)} %v_hbm.3, f32[1,8192]{1,0:T(1,128)S(1)} %bitcast.38, f32[1,8192]{1,0:T(1,128)S(1)} %bitcast.45, ...), custom_call_target="tpu_custom_call" | custom-call | flops 1000 | bytes 1000 | tf_op jit(solution)/shard_map/near/pallas_call | solution.py:457
  47.9 9.8 %near.24.refs_3_ = f32[32,8192]{1,0:T(8,128)} custom-call(s32[896]{0:T(1024)S(1)} %get-tuple-element.500.list_ref, f32[3]{0:T(128)S(1)} %pad_maximum_fusion.coef_ref.refs_2_, f32[64,8192]{1,0:T(8,128)S(1)} %copy-done, f32[64,8192]{1,0:T(8,128)} %v_hbm.3, f32[1,8192]{1,0:T(1,128)S(1)} %bitcast.39, f32[1,8192]{1,0:T(1,128)S(1)} %bitcast.46, ...), custom_call_target="tpu_custom_call" | custom-call | flops 1000 | bytes 1000 | tf_op jit(solution)/shard_map/near/pallas_call | solution.py:457
  57.7 12.1 %collective-permute-done.21.refs_6_ = f32[46,32,128]{2,1,0:T(8,128)} collective-permute-done((f32[46,32,128]{2,1,0:T(8,128)}, f32[46,32,128]{2,1,0:T(8,128)}, u32[]{:S(2)}, u32[]{:S(2)}) %collective-permute-start.21) | collective-permute-done | bytes 753696 | tf_op jit(solution)/shard_map/ppermute | solution.py:27
  72.2 10.1 %far.31 = (f32[32,8192]{1,0:T(8,128)}, f32[32,8192]{1,0:T(8,128)}, f32[46,32,128]{2,1,0:T(8,128)}, f32[46,32,128]{2,1,0:T(8,128)}) custom-call(s32[896]{0:T(1024)S(1)} %get-tuple-element.259.refs_0_, f32[64,4,128,128]{3,2,1,0:T(8,128)} %refs_1_.15, f32[3]{0:T(128)S(1)} %pad_maximum_fusion.coef_ref.refs_2_, f32[32,8192]{1,0:T(8,128)} %near.24.refs_3_, ...), custom_call_target="tpu_custom_call" | custom-call | flops 1000 | bytes 1000 | tf_op jit(solution)/shard_map/far/pallas_call | solution.py:546
  84.4 11.1 %near.26.refs_3_ = f32[32,8192]{1,0:T(8,128)} custom-call(s32[896]{0:T(1024)S(1)} %get-tuple-element.500.list_ref, f32[3]{0:T(128)S(1)} %pad_maximum_fusion.coef_ref.refs_2_, f32[32,8192]{1,0:T(8,128)} %get-tuple-element.253.x_hbm.refs_7_, f32[32,8192]{1,0:T(8,128)} %get-tuple-element.254.v_hbm, f32[1,8192]{1,0:T(1,128)S(1)} %bitcast.40, ...), custom_call_target="tpu_custom_call" | custom-call | flops 1000 | bytes 1000 | tf_op jit(solution)/shard_map/near/pallas_call | solution.py:457
  95.6 6.5 %collective-permute-done.23.refs_6_ = f32[46,32,128]{2,1,0:T(8,128)S(1)} collective-permute-done((f32[46,32,128]{2,1,0:T(8,128)}, f32[46,32,128]{2,1,0:T(8,128)S(1)}, u32[]{:S(2)}, u32[]{:S(2)}) %collective-permute-start.23) | collective-permute-done | bytes 753696 | tf_op jit(solution)/shard_map/ppermute | solution.py:27
  105.3 10.1 %far.33 = (f32[32,8192]{1,0:T(8,128)}, f32[32,8192]{1,0:T(8,128)}, f32[46,32,128]{2,1,0:T(8,128)}, f32[46,32,128]{2,1,0:T(8,128)}) custom-call(s32[896]{0:T(1024)S(1)} %get-tuple-element.259.refs_0_, f32[64,4,128,128]{3,2,1,0:T(8,128)} %refs_1_.15, f32[3]{0:T(128)S(1)} %pad_maximum_fusion.coef_ref.refs_2_, f32[32,8192]{1,0:T(8,128)} %near.25.refs_3_, ...), custom_call_target="tpu_custom_call" | custom-call | flops 1000 | bytes 1000 | tf_op jit(solution)/shard_map/far/pallas_call | solution.py:546
  119.0 11.4 %near.27.refs_3_ = f32[32,8192]{1,0:T(8,128)} custom-call(s32[896]{0:T(1024)S(1)} %get-tuple-element.500.list_ref, f32[3]{0:T(128)S(1)} %pad_maximum_fusion.coef_ref.refs_2_, f32[32,8192]{1,0:T(8,128)} %get-tuple-element.260.x_hbm.refs_7_, f32[32,8192]{1,0:T(8,128)} %get-tuple-element.261.v_hbm, f32[1,8192]{1,0:T(1,128)S(1)} %bitcast.41, ...), custom_call_target="tpu_custom_call" | custom-call | flops 1000 | bytes 1000 | tf_op jit(solution)/shard_map/near/pallas_call | solution.py:457
  130.4 3.9 %collective-permute-done.25.refs_6_ = f32[46,32,128]{2,1,0:T(8,128)} collective-permute-done((f32[46,32,128]{2,1,0:T(8,128)}, f32[46,32,128]{2,1,0:T(8,128)}, u32[]{:S(2)}, u32[]{:S(2)}) %collective-permute-start.25) | collective-permute-done | bytes 753696 | tf_op jit(solution)/shard_map/ppermute | solution.py:27
  134.3 11.1 %far.34 = (f32[32,8192]{1,0:T(8,128)}, f32[32,8192]{1,0:T(8,128)}, f32[46,32,128]{2,1,0:T(8,128)}, f32[1,16384]{1,0:T(1,128)}, f32[46,32,128]{2,1,0:T(8,128)}) custom-call(s32[896]{0:T(1024)S(1)} %get-tuple-element.259.refs_0_, f32[64,4,128,128]{3,2,1,0:T(8,128)} %refs_1_.15, f32[3]{0:T(128)S(1)} %pad_maximum_fusion.coef_ref.refs_2_, ...), custom_call_target="tpu_custom_call" | custom-call | flops 1000 | bytes 1000 | tf_op jit(solution)/shard_map/far/pallas_call | solution.py:546
  145.5 4.0 %collective-permute-start.28 = (f32[46,32,128]{2,1,0:T(8,128)}, f32[46,32,128]{2,1,0:T(8,128)}, u32[]{:S(2)}, u32[]{:S(2)}) collective-permute-start(f32[46,32,128]{2,1,0:T(8,128)} %get-tuple-element.276), channel_id=1, source_target_pairs={{0,28},{4,0},{8,4},{12,8},{16,12},{20,16},{24,20},{28,24},{1,29},{... | collective-permute-start | bytes 2261000 | tf_op jit(solution)/shard_map/ppermute | solution.py:27
  149.4 11.2 %near.28.refs_3_ = f32[32,8192]{1,0:T(8,128)} custom-call(s32[896]{0:T(1024)S(1)} %get-tuple-element.500.list_ref, f32[3]{0:T(128)S(1)} %pad_maximum_fusion.coef_ref.refs_2_, f32[32,8192]{1,0:T(8,128)} %get-tuple-element.265.x_hbm.x0_ref, f32[32,8192]{1,0:T(8,128)} %get-tuple-element.266.v_hbm, f32[1,8192]{1,0:T(1,128)S(1)} %bitcast.42, ...), custom_call_target="tpu_custom_call" | custom-call | flops 1000 | bytes 1000 | tf_op jit(solution)/shard_map/near/pallas_call | solution.py:457
  160.6 8.4 %collective-permute-done.26.refs_4_ = f32[46,32,128]{2,1,0:T(8,128)S(1)} collective-permute-done((f32[46,32,128]{2,1,0:T(8,128)}, f32[46,32,128]{2,1,0:T(8,128)S(1)}, u32[]{:S(2)}, u32[]{:S(2)}) %collective-permute-start.26) | collective-permute-done | bytes 753696 | tf_op jit(solution)/shard_map/ppermute | solution.py:27
  169.9 11.1 %far.35 = (f32[32,8192]{1,0:T(8,128)}, f32[32,8192]{1,0:T(8,128)}, f32[46,32,128]{2,1,0:T(8,128)}, f32[1,16384]{1,0:T(1,128)}, f32[46,32,128]{2,1,0:T(8,128)}) custom-call(s32[896]{0:T(1024)S(1)} %get-tuple-element.259.refs_0_, f32[64,4,128,128]{3,2,1,0:T(8,128)} %refs_1_.15, f32[3]{0:T(128)S(1)} %pad_maximum_fusion.coef_ref.refs_2_, ...), custom_call_target="tpu_custom_call" | custom-call | flops 1000 | bytes 1000 | tf_op jit(solution)/shard_map/far/pallas_call | solution.py:546
  183.1 11.2 %near.29.refs_3_ = f32[32,8192]{1,0:T(8,128)} custom-call(s32[896]{0:T(1024)S(1)} %get-tuple-element.500.list_ref, f32[3]{0:T(128)S(1)} %pad_maximum_fusion.coef_ref.refs_2_, f32[32,8192]{1,0:T(8,128)} %get-tuple-element.272.x_hbm.x1_ref, f32[32,8192]{1,0:T(8,128)} %get-tuple-element.274.v_hbm, f32[1,8192]{1,0:T(1,128)S(1)} %bitcast.43, ...), custom_call_target="tpu_custom_call" | custom-call | flops 1000 | bytes 1000 | tf_op jit(solution)/shard_map/near/pallas_call | solution.py:457
  200.0 7.9 %far.36.v_ref.refs_8_ = f32[64,8192]{1,0:T(8,128)} custom-call(s32[896]{0:T(1024)S(1)} %get-tuple-element.259.refs_0_, f32[64,4,128,128]{3,2,1,0:T(8,128)} %refs_1_.15, f32[3]{0:T(128)S(1)} %pad_maximum_fusion.coef_ref.refs_2_, f32[32,8192]{1,0:T(8,128)} %near.28.refs_3_, f32[46,32,128]{2,1,0:T(8,128)} %collective-permute-done.28.refs_4_, ...), custom_call_target="tpu_custom_call" | custom-call | flops 1000 | bytes 1000 | tf_op jit(solution)/shard_map/far/pallas_call | solution.py:546
  209.2 4.8 %spread.4 = (f32[64,8192]{1,0:T(8,128)}, f32[32,8192]{1,0:T(8,128)}, f32[8,64]{1,0:T(8,128)}, f32[8,32]{1,0:T(8,128)}) custom-call(f32[64,8192]{1,0:T(8,128)S(1)} %copy-done, f32[32,8192]{1,0:T(8,128)} %get-tuple-element.265.x_hbm.x0_ref, f32[32,8192]{1,0:T(8,128)} %get-tuple-element.272.x_hbm.x1_ref, f32[64,8192]{1,0:T(8,128)} %far.36.v_ref.refs_8_, ...), custom_call_target="tpu_custom_call" | custom-call | flops 1000 | bytes 1000 | tf_op jit(solution)/shard_map/spread/pallas_call | solution.py:579
  216.9 8.5 %far.37 = (f32[64,8192]{1,0:T(8,128)}, f32[8,32]{1,0:T(8,128)}) custom-call(s32[896]{0:T(1024)S(1)} %get-tuple-element.259.refs_0_, f32[64,4,128,128]{3,2,1,0:T(8,128)} %refs_1_.15, f32[3]{0:T(128)S(1)} %pad_maximum_fusion.coef_ref.refs_2_, f32[32,8192]{1,0:T(8,128)} %near.29.refs_3_, f32[46,32,128]{2,1,0:T(8,128)} %copy-done.10, ...), custom_call_target="tpu_custom_call", output_to_operand_aliasing={{0}: (8, {})} | custom-call | flops 1000 | bytes 1000 | tf_op jit(solution)/shard_map/far/pallas_call | solution.py:546
  230.8 4.9 %collective-permute-start.37 = (f32[8,136]{1,0:T(8,128)S(1)}, f32[8,136]{1,0:T(8,128)S(1)}, u32[]{:S(2)}, u32[]{:S(2)}) collective-permute-start(f32[8,136]{1,0:T(8,128)S(1)} %add.36), channel_id=1, source_target_pairs={{0,16},{4,20},{8,24},{12,28},{16,0},{20,4},{24,8},{28,12},{1,17},{... | collective-permute-start | bytes 13064 | tf_op jit(solution)/shard_map/ppermute | solution.py:618
  237.4 3.8 %collective-permute-done.38 = f32[8,136]{1,0:T(8,128)S(1)} collective-permute-done((f32[8,136]{1,0:T(8,128)S(1)}, f32[8,136]{1,0:T(8,128)S(1)}, u32[]{:S(2)}, u32[]{:S(2)}) %collective-permute-start.38) | collective-permute-done | bytes 4384 | tf_op jit(solution)/shard_map/ppermute | solution.py:618
  (77 shorter events, 47.4 us)
Async XLA Ops:
  0.6 12.7 %copy-start = (f32[64,8192]{1,0:T(8,128)S(1)}, f32[64,8192]{1,0:T(8,128)}, u32[]{:S(2)}) copy-start(f32[64,8192]{1,0:T(8,128)} %start_ref.1) | copy-start | bytes 6291460
  3.1 7.8 %collective-permute-start.19 = (s32[128]{0:T(128)}, s32[128]{0:T(128)S(1)}, u32[]{:S(2)}, u32[]{:S(2)}) collective-permute-start(s32[128]{0:T(128)} %get-tuple-element.250), channel_id=1, source_target_pairs={{0,4},{4,8},{8,12},{12,16},{16,20},{20,24},{24,28},{28,0},{1,5},{5... | collective-permute-start | bytes 1544 | tf_op jit(solution)/shard_map/ppermute | solution.py:27
  19.7 50.0 %collective-permute-start.21 = (f32[46,32,128]{2,1,0:T(8,128)}, f32[46,32,128]{2,1,0:T(8,128)}, u32[]{:S(2)}, u32[]{:S(2)}) collective-permute-start(f32[46,32,128]{2,1,0:T(8,128)} %far.30), channel_id=1, source_target_pairs={{0,4},{4,8},{8,12},{12,16},{16,20},{20,24},{24,28},{28,0},{1,5},{5... | collective-permute-start | bytes 2261000 | tf_op jit(solution)/shard_map/ppermute | solution.py:27
  19.8 52.4 %collective-permute-start.20 = (f32[46,32,128]{2,1,0:T(8,128)}, f32[46,32,128]{2,1,0:T(8,128)}, u32[]{:S(2)}, u32[]{:S(2)}) collective-permute-start(f32[46,32,128]{2,1,0:T(8,128)} %pack.8), channel_id=1, source_target_pairs={{0,28},{4,0},{8,4},{12,8},{16,12},{20,16},{24,20},{28,24},{1,29},{... | collective-permute-start | bytes 2261000 | tf_op jit(solution)/shard_map/ppermute | solution.py:27
  26.2 11.8 %copy-start.1 = (f32[8192]{0:T(1024)S(1)}, f32[8192]{0:T(1024)}, u32[]{:S(2)}) copy-start(f32[8192]{0:T(1024)} %param.13) | copy-start | bytes 98308
  26.2 11.8 %copy-start.2 = (f32[8192]{0:T(1024)S(1)}, f32[8192]{0:T(1024)}, u32[]{:S(2)}) copy-start(f32[8192]{0:T(1024)} %param.14) | copy-start | bytes 98308
  32.6 69.5 %collective-permute-start.23 = (f32[46,32,128]{2,1,0:T(8,128)}, f32[46,32,128]{2,1,0:T(8,128)S(1)}, u32[]{:S(2)}, u32[]{:S(2)}) collective-permute-start(f32[46,32,128]{2,1,0:T(8,128)} %far.32), channel_id=1, source_target_pairs={{0,4},{4,8},{8,12},{12,16},{16,20},{20,24},{24,28},{28,0},{1,5},{5... | collective-permute-start | bytes 2261000 | tf_op jit(solution)/shard_map/ppermute | solution.py:27
  32.6 71.8 %collective-permute-start.22 = (f32[46,32,128]{2,1,0:T(8,128)}, f32[46,32,128]{2,1,0:T(8,128)S(1)}, u32[]{:S(2)}, u32[]{:S(2)}) collective-permute-start(f32[46,32,128]{2,1,0:T(8,128)} %pack.9), channel_id=1, source_target_pairs={{0,28},{4,0},{8,4},{12,8},{16,12},{20,16},{24,20},{28,24},{1,29},{... | collective-permute-start | bytes 2261000 | tf_op jit(solution)/shard_map/ppermute | solution.py:27
  82.3 48.1 %collective-permute-start.24 = (f32[46,32,128]{2,1,0:T(8,128)}, f32[46,32,128]{2,1,0:T(8,128)}, u32[]{:S(2)}, u32[]{:S(2)}) collective-permute-start(f32[46,32,128]{2,1,0:T(8,128)} %get-tuple-element.263), channel_id=1, source_target_pairs={{0,28},{4,0},{8,4},{12,8},{16,12},{20,16},{24,20},{28,24},{1,29},{... | collective-permute-start | bytes 2261000 | tf_op jit(solution)/shard_map/ppermute | solution.py:27
  84.2 50.1 %collective-permute-start.25 = (f32[46,32,128]{2,1,0:T(8,128)}, f32[46,32,128]{2,1,0:T(8,128)}, u32[]{:S(2)}, u32[]{:S(2)}) collective-permute-start(f32[46,32,128]{2,1,0:T(8,128)} %get-tuple-element.264), channel_id=1, source_target_pairs={{0,4},{4,8},{8,12},{12,16},{16,20},{20,24},{24,28},{28,0},{1,5},{5... | collective-permute-start | bytes 2261000 | tf_op jit(solution)/shard_map/ppermute | solution.py:27
  115.4 53.6 %collective-permute-start.26 = (f32[46,32,128]{2,1,0:T(8,128)}, f32[46,32,128]{2,1,0:T(8,128)S(1)}, u32[]{:S(2)}, u32[]{:S(2)}) collective-permute-start(f32[46,32,128]{2,1,0:T(8,128)} %get-tuple-element.269), channel_id=1, source_target_pairs={{0,28},{4,0},{8,4},{12,8},{16,12},{20,16},{24,20},{28,24},{1,29},{... | collective-permute-start | bytes 2261000 | tf_op jit(solution)/shard_map/ppermute | solution.py:27
  118.2 50.9 %collective-permute-start.27 = (f32[46,32,128]{2,1,0:T(8,128)}, f32[46,32,128]{2,1,0:T(8,128)}, u32[]{:S(2)}, u32[]{:S(2)}) collective-permute-start(f32[46,32,128]{2,1,0:T(8,128)} %get-tuple-element.270), channel_id=1, source_target_pairs={{0,4},{4,8},{8,12},{12,16},{16,20},{20,24},{24,28},{28,0},{1,5},{5... | collective-permute-start | bytes 2261000 | tf_op jit(solution)/shard_map/ppermute | solution.py:27
  145.5 48.9 %collective-permute-start.28 = (f32[46,32,128]{2,1,0:T(8,128)}, f32[46,32,128]{2,1,0:T(8,128)}, u32[]{:S(2)}, u32[]{:S(2)}) collective-permute-start(f32[46,32,128]{2,1,0:T(8,128)} %get-tuple-element.276), channel_id=1, source_target_pairs={{0,28},{4,0},{8,4},{12,8},{16,12},{20,16},{24,20},{28,24},{1,29},{... | collective-permute-start | bytes 2261000 | tf_op jit(solution)/shard_map/ppermute | solution.py:27
  149.4 49.3 %collective-permute-start.29 = (f32[46,32,128]{2,1,0:T(8,128)}, f32[46,32,128]{2,1,0:T(8,128)}, u32[]{:S(2)}, u32[]{:S(2)}) collective-permute-start(f32[46,32,128]{2,1,0:T(8,128)} %get-tuple-element.277), channel_id=1, source_target_pairs={{0,4},{4,8},{8,12},{12,16},{16,20},{20,24},{24,28},{28,0},{1,5},{5... | collective-permute-start | bytes 2261000 | tf_op jit(solution)/shard_map/ppermute | solution.py:27
  181.0 34.7 %collective-permute-start.33 = (f32[46,32,128]{2,1,0:T(8,128)}, f32[46,32,128]{2,1,0:T(8,128)S(1)}, u32[]{:S(2)}, u32[]{:S(2)}) collective-permute-start(f32[46,32,128]{2,1,0:T(8,128)} %get-tuple-element.284), channel_id=1, source_target_pairs={{0,28},{4,0},{8,4},{12,8},{16,12},{20,16},{24,20},{28,24},{1,29},{... | collective-permute-start | bytes 2261000 | tf_op jit(solution)/shard_map/ppermute | solution.py:27
  182.1 33.6 %collective-permute-start.34 = (f32[46,32,128]{2,1,0:T(8,128)}, f32[46,32,128]{2,1,0:T(8,128)S(1)}, u32[]{:S(2)}, u32[]{:S(2)}) collective-permute-start(f32[46,32,128]{2,1,0:T(8,128)} %get-tuple-element.285), channel_id=1, source_target_pairs={{0,4},{4,8},{8,12},{12,16},{16,20},{20,24},{24,28},{28,0},{1,5},{5... | collective-permute-start | bytes 2261000 | tf_op jit(solution)/shard_map/ppermute | solution.py:27
  183.1 15.7 %copy-start.23 = (s32[128]{0:T(128)S(1)}, s32[128]{0:T(128)}, u32[]{:S(2)}) copy-start(s32[128]{0:T(128)} %get-tuple-element.250) | copy-start | bytes 1540
  194.3 13.7 %collective-permute-start.30 = (f32[1,16384]{1,0:T(1,128)S(1)}, f32[1,16384]{1,0:T(1,128)S(1)}, u32[]{:S(2)}, u32[]{:S(2)}) collective-permute-start(f32[1,16384]{1,0:T(1,128)S(1)} %copy-done.17), channel_id=1, source_target_pairs={{0,1},{1,2},{2,3},{3,0},{4,5},{5,6},{6,7},{7,4},{8,9},{9,10},{10,1... | collective-permute-start | bytes 196616 | tf_op jit(solution)/shard_map/ppermute | solution.py:606
  194.3 13.6 %collective-permute-start.31 = (f32[1,16384]{1,0:T(1,128)S(1)}, f32[1,16384]{1,0:T(1,128)S(1)}, u32[]{:S(2)}, u32[]{:S(2)}) collective-permute-start(f32[1,16384]{1,0:T(1,128)S(1)} %copy-done.17), channel_id=1, source_target_pairs={{0,2},{1,3},{2,0},{3,1},{4,6},{5,7},{6,4},{7,5},{8,10},{9,11},{10,... | collective-permute-start | bytes 196616 | tf_op jit(solution)/shard_map/ppermute | solution.py:606
  198.8 9.2 %collective-permute-start.32 = (f32[1,16384]{1,0:T(1,128)S(1)}, f32[1,16384]{1,0:T(1,128)S(1)}, u32[]{:S(2)}, u32[]{:S(2)}) collective-permute-start(f32[1,16384]{1,0:T(1,128)S(1)} %copy-done.17), channel_id=1, source_target_pairs={{0,3},{1,0},{2,1},{3,2},{4,7},{5,4},{6,5},{7,6},{8,11},{9,8},{10,9... | collective-permute-start | bytes 196616 | tf_op jit(solution)/shard_map/ppermute | solution.py:606
  226.1 3.7 %collective-permute-start.35 = (f32[8,136]{1,0:T(8,128)S(1)}, f32[8,136]{1,0:T(8,128)S(1)}, u32[]{:S(2)}, u32[]{:S(2)}) collective-permute-start(f32[8,136]{1,0:T(8,128)S(1)} %maximum_maximum_fusion.1), channel_id=1, source_target_pairs={{0,4},{4,0},{8,12},{12,8},{16,20},{20,16},{24,28},{28,24},{1,5},{5... | collective-permute-start | bytes 13064 | tf_op jit(solution)/shard_map/ppermute | solution.py:618
  229.8 6.6 %collective-permute-start.36 = (f32[8,136]{1,0:T(8,128)S(1)}, f32[8,136]{1,0:T(8,128)S(1)}, u32[]{:S(2)}, u32[]{:S(2)}) collective-permute-start(f32[8,136]{1,0:T(8,128)S(1)} %add.36), channel_id=1, source_target_pairs={{0,8},{4,12},{8,0},{12,4},{16,24},{20,28},{24,16},{28,20},{1,9},{5... | collective-permute-start | bytes 13064 | tf_op jit(solution)/shard_map/ppermute | solution.py:618
  230.8 6.5 %collective-permute-start.37 = (f32[8,136]{1,0:T(8,128)S(1)}, f32[8,136]{1,0:T(8,128)S(1)}, u32[]{:S(2)}, u32[]{:S(2)}) collective-permute-start(f32[8,136]{1,0:T(8,128)S(1)} %add.36), channel_id=1, source_target_pairs={{0,16},{4,20},{8,24},{12,28},{16,0},{20,4},{24,8},{28,12},{1,17},{... | collective-permute-start | bytes 13064 | tf_op jit(solution)/shard_map/ppermute | solution.py:618
  235.8 5.4 %collective-permute-start.38 = (f32[8,136]{1,0:T(8,128)S(1)}, f32[8,136]{1,0:T(8,128)S(1)}, u32[]{:S(2)}, u32[]{:S(2)}) collective-permute-start(f32[8,136]{1,0:T(8,128)S(1)} %add.36), channel_id=1, source_target_pairs={{0,24},{4,28},{8,16},{12,20},{16,8},{20,12},{24,0},{28,4},{1,25},{... | collective-permute-start | bytes 13064 | tf_op jit(solution)/shard_map/ppermute | solution.py:618
  (11 other events, 36.3 us)

commit v2 on v1

--- a/solution.py
+++ b/solution.py
@@ -560,6 +560,22 @@
     )(*args)
 
 
+def relay_kernel(coef_ref, parcel_ref, out_ref):
+    for i in range(3):
+        out_ref[i] = coef_ref[i]
+
+
+def relay_call(coef, parcel):
+    return pl.pallas_call(
+        relay_kernel,
+        out_shape=jax.ShapeDtypeStruct(coef.shape, coef.dtype),
+        in_specs=[SMEM, ANY],
+        out_specs=SMEM,
+        cost_estimate=COST,
+        name="relay",
+    )(coef, parcel)
+
+
 def pack_call(given, x, chains, part, cap, side):
     return pl.pallas_call(
         functools.partial(pack_kernel, cap=cap),
@@ -666,7 +682,6 @@
         )
 
     def two_steps(cap, start, momenta):
-        far = functools.partial(far_call, meta, given, coef, blocks)
         x, v, w, flight = [start] * CHUNKS, [momenta] * CHUNKS, [], []
         rows = list(first_rows)
         edges = meta
@@ -687,6 +702,8 @@
             for h in parts:
                 halo, carry = flight[h]
                 before = column if turn == 1 else None
+                scales = relay_call(coef, halo) if turn == 0 and h == 0 else coef
+                far = functools.partial(far_call, meta, given, scales, blocks)
                 v[h], x[h], halo, *after, carry = far(
                     x[h], w[h], halo, carry, chains, rows[h], turn, cap, before
                 )

time: 244 us -> 236 us (0.967)
  waiting for transfers between devices: 49.3 us -> 35.3 us
  Pallas kernels: 151 us -> 155 us
    ppermute x13, waiting for transfers between devices: 41.7 us -> 29.8 us  [passed_along(): return lax.ppermute(value, 'rows', pairs)]
    ppermute x13, starting transfers between devices: 23.4 us -> 28.2 us  [passed_along(): return lax.ppermute(value, 'rows', pairs)]
    pallas_call x6, Pallas kernels: 64.5 us -> 67.4 us  [near_call(): pl.pallas_call(functools.partial(near_kernel, bands=bands, side=side, x_r...]
  transfers between devices with their start and end apart: 20 -> 20, of which waited for: 12 -> 8; matrix products, arithmetic and copies ran while one was open for 1% -> 1% of each run, Pallas kernels for 54% -> 60%
where the time goes in v2:
time: 236 us; the launch traced here: 235 us
  Pallas kernels  155 us (66%)
  waiting for transfers between devices  35.3 us (15%)
  starting transfers between devices  34.3 us (15%)
  local copies, waits for them, and re-layouts  5.12 us (2%)
  between operations  3.13 us (1%)
    pallas_call x8, Pallas kernels, far_call(): pl.pallas_call(functools.partial(far_kernel, bands=bands, side=side, cap=...  71.4 us
    pallas_call x6, Pallas kernels, near_call(): pl.pallas_call(functools.partial(near_kernel, bands=bands, side=side, x_r...  67.4 us
    ppermute x13, waiting for transfers between devices, passed_along(): return lax.ppermute(value, 'rows', pairs)  29.8 us
    ppermute x13, starting transfers between devices, passed_along(): return lax.ppermute(value, 'rows', pairs)  28.2 us
    ppermute x4, waiting for transfers between devices, summed_over(): value = value + lax.ppermute(own, axis, pairs)  5.48 us
    pallas_call x1, Pallas kernels, spread_call(): pl.pallas_call(functools.partial(spread_kernel, chain_total=chain_total),...  4.79 us
  transfers between devices with their start and end apart: 20, of which 8 were waited for; matrix products, arithmetic and copies ran while one was open for 1% of the time, Pallas kernels for 60%

profile of v2, /device:TPU:0, one launch (start us, length us, event | category | flops | bytes accessed | tf_op | source)
XLA Modules:
  0.0 235.5 jit_solution(14624899183291389249)
XLA Ops:
  15.2 6.4 %far.30 = f32[46,32,128]{2,1,0:T(8,128)} custom-call(s32[896]{0:T(1024)S(1)} %get-tuple-element.259.refs_0_, f32[64,4,128,128]{3,2,1,0:T(8,128)} %refs_1_.15, f32[64,8192]{1,0:T(8,128)S(1)} %copy-done), custom_call_target="tpu_custom_call" | custom-call | flops 1000 | bytes 1000 | tf_op jit(solution)/shard_map/far/pallas_call | solution.py:546
  23.4 6.3 %far.32 = f32[46,32,128]{2,1,0:T(8,128)} custom-call(s32[896]{0:T(1024)S(1)} %get-tuple-element.259.refs_0_, f32[64,4,128,128]{3,2,1,0:T(8,128)} %refs_1_.15, f32[64,8192]{1,0:T(8,128)S(1)} %copy-done), custom_call_target="tpu_custom_call" | custom-call | flops 1000 | bytes 1000 | tf_op jit(solution)/shard_map/far/pallas_call | solution.py:546
  30.4 4.1 %collective-permute-start.22 = (f32[46,32,128]{2,1,0:T(8,128)}, f32[46,32,128]{2,1,0:T(8,128)}, u32[]{:S(2)}, u32[]{:S(2)}) collective-permute-start(f32[46,32,128]{2,1,0:T(8,128)} %pack.9), channel_id=1, source_target_pairs={{0,28},{4,0},{8,4},{12,8},{16,12},{20,16},{24,20},{28,24},{1,29},{... | collective-permute-start | bytes 2261000 | tf_op jit(solution)/shard_map/ppermute | solution.py:27
  35.2 10.3 %near.24.refs_3_ = f32[32,8192]{1,0:T(8,128)} custom-call(s32[896]{0:T(1024)S(1)} %get-tuple-element.503.list_ref, f32[3]{0:T(128)S(1)} %pad_maximum_fusion.coef_ref.refs_2_, f32[64,8192]{1,0:T(8,128)S(1)} %copy-done, f32[64,8192]{1,0:T(8,128)} %v_hbm.3, f32[1,8192]{1,0:T(1,128)S(1)} %bitcast.38, f32[1,8192]{1,0:T(1,128)S(1)} %bitcast.45, ...), custom_call_target="tpu_custom_call" | custom-call | flops 1000 | bytes 1000 | tf_op jit(solution)/shard_map/near/pallas_call | solution.py:457
  45.5 10.3 %near.25.refs_3_ = f32[32,8192]{1,0:T(8,128)} custom-call(s32[896]{0:T(1024)S(1)} %get-tuple-element.503.list_ref, f32[3]{0:T(128)S(1)} %pad_maximum_fusion.coef_ref.refs_2_, f32[64,8192]{1,0:T(8,128)S(1)} %copy-done, f32[64,8192]{1,0:T(8,128)} %v_hbm.3, f32[1,8192]{1,0:T(1,128)S(1)} %bitcast.39, f32[1,8192]{1,0:T(1,128)S(1)} %bitcast.46, ...), custom_call_target="tpu_custom_call" | custom-call | flops 1000 | bytes 1000 | tf_op jit(solution)/shard_map/near/pallas_call | solution.py:457
  55.8 9.7 %collective-permute-done.20.parcel_ref.refs_4_ = f32[46,32,128]{2,1,0:T(8,128)S(1)} collective-permute-done((f32[46,32,128]{2,1,0:T(8,128)}, f32[46,32,128]{2,1,0:T(8,128)S(1)}, u32[]{:S(2)}, u32[]{:S(2)}) %collective-permute-start.20) | collective-permute-done | bytes 753696 | tf_op jit(solution)/shard_map/ppermute | solution.py:27
  67.4 10.1 %far.31 = (f32[32,8192]{1,0:T(8,128)}, f32[32,8192]{1,0:T(8,128)}, f32[46,32,128]{2,1,0:T(8,128)}, f32[46,32,128]{2,1,0:T(8,128)}) custom-call(s32[896]{0:T(1024)S(1)} %get-tuple-element.259.refs_0_, f32[64,4,128,128]{3,2,1,0:T(8,128)} %refs_1_.15, f32[3]{0:T(128)} %relay.2.refs_2_, f32[32,8192]{1,0:T(8,128)} %near.24.refs_3_, f32[46,32,128]{2,1,0:T(8,128)} %copy-done.6, ...), custom_call_target="tpu_custom_call" | custom-call | flops 1000 | bytes 1000 | tf_op jit(solution)/shard_map/far/pallas_call | solution.py:546
  79.6 11.6 %near.26.refs_3_ = f32[32,8192]{1,0:T(8,128)} custom-call(s32[896]{0:T(1024)S(1)} %get-tuple-element.503.list_ref, f32[3]{0:T(128)S(1)} %pad_maximum_fusion.coef_ref.refs_2_, f32[32,8192]{1,0:T(8,128)} %get-tuple-element.253.x_hbm.refs_7_, f32[32,8192]{1,0:T(8,128)} %get-tuple-element.254.v_hbm, f32[1,8192]{1,0:T(1,128)S(1)} %bitcast.40, ...), custom_call_target="tpu_custom_call" | custom-call | flops 1000 | bytes 1000 | tf_op jit(solution)/shard_map/near/pallas_call | solution.py:457
  91.2 3.9 %collective-permute-done.23.refs_6_ = f32[46,32,128]{2,1,0:T(8,128)} collective-permute-done((f32[46,32,128]{2,1,0:T(8,128)}, f32[46,32,128]{2,1,0:T(8,128)}, u32[]{:S(2)}, u32[]{:S(2)}) %collective-permute-start.23) | collective-permute-done | bytes 753696 | tf_op jit(solution)/shard_map/ppermute | solution.py:27
  95.2 10.1 %far.33 = (f32[32,8192]{1,0:T(8,128)}, f32[32,8192]{1,0:T(8,128)}, f32[46,32,128]{2,1,0:T(8,128)}, f32[46,32,128]{2,1,0:T(8,128)}) custom-call(s32[896]{0:T(1024)S(1)} %get-tuple-element.259.refs_0_, f32[64,4,128,128]{3,2,1,0:T(8,128)} %refs_1_.15, f32[3]{0:T(128)S(1)} %pad_maximum_fusion.coef_ref.refs_2_, f32[32,8192]{1,0:T(8,128)} %near.25.refs_3_, ...), custom_call_target="tpu_custom_call" | custom-call | flops 1000 | bytes 1000 | tf_op jit(solution)/shard_map/far/pallas_call | solution.py:546
  105.2 5.4 %collective-permute-start.26 = (f32[46,32,128]{2,1,0:T(8,128)}, f32[46,32,128]{2,1,0:T(8,128)S(1)}, u32[]{:S(2)}, u32[]{:S(2)}) collective-permute-start(f32[46,32,128]{2,1,0:T(8,128)} %get-tuple-element.269), channel_id=1, source_target_pairs={{0,28},{4,0},{8,4},{12,8},{16,12},{20,16},{24,20},{28,24},{1,29},{... | collective-permute-start | bytes 2261000 | tf_op jit(solution)/shard_map/ppermute | solution.py:27
  111.5 11.9 %near.27.refs_3_ = f32[32,8192]{1,0:T(8,128)} custom-call(s32[896]{0:T(1024)S(1)} %get-tuple-element.503.list_ref, f32[3]{0:T(128)S(1)} %pad_maximum_fusion.coef_ref.refs_2_, f32[32,8192]{1,0:T(8,128)} %get-tuple-element.260.x_hbm.refs_7_, f32[32,8192]{1,0:T(8,128)} %get-tuple-element.261.v_hbm, f32[1,8192]{1,0:T(1,128)S(1)} %bitcast.41, ...), custom_call_target="tpu_custom_call" | custom-call | flops 1000 | bytes 1000 | tf_op jit(solution)/shard_map/near/pallas_call | solution.py:457
  123.4 4.1 %collective-permute-done.25.refs_6_ = f32[46,32,128]{2,1,0:T(8,128)} collective-permute-done((f32[46,32,128]{2,1,0:T(8,128)}, f32[46,32,128]{2,1,0:T(8,128)}, u32[]{:S(2)}, u32[]{:S(2)}) %collective-permute-start.25) | collective-permute-done | bytes 753696 | tf_op jit(solution)/shard_map/ppermute | solution.py:27
  127.5 11.1 %far.34 = (f32[32,8192]{1,0:T(8,128)}, f32[32,8192]{1,0:T(8,128)}, f32[46,32,128]{2,1,0:T(8,128)}, f32[1,16384]{1,0:T(1,128)}, f32[46,32,128]{2,1,0:T(8,128)}) custom-call(s32[896]{0:T(1024)S(1)} %get-tuple-element.259.refs_0_, f32[64,4,128,128]{3,2,1,0:T(8,128)} %refs_1_.15, f32[3]{0:T(128)S(1)} %pad_maximum_fusion.coef_ref.refs_2_, ...), custom_call_target="tpu_custom_call" | custom-call | flops 1000 | bytes 1000 | tf_op jit(solution)/shard_map/far/pallas_call | solution.py:546
  138.6 5.4 %collective-permute-start.28 = (f32[46,32,128]{2,1,0:T(8,128)}, f32[46,32,128]{2,1,0:T(8,128)}, u32[]{:S(2)}, u32[]{:S(2)}) collective-permute-start(f32[46,32,128]{2,1,0:T(8,128)} %get-tuple-element.276), channel_id=1, source_target_pairs={{0,28},{4,0},{8,4},{12,8},{16,12},{20,16},{24,20},{28,24},{1,29},{... | collective-permute-start | bytes 2261000 | tf_op jit(solution)/shard_map/ppermute | solution.py:27
  144.0 11.6 %near.28.refs_3_ = f32[32,8192]{1,0:T(8,128)} custom-call(s32[896]{0:T(1024)S(1)} %get-tuple-element.503.list_ref, f32[3]{0:T(128)S(1)} %pad_maximum_fusion.coef_ref.refs_2_, f32[32,8192]{1,0:T(8,128)} %get-tuple-element.265.x_hbm.x0_ref, f32[32,8192]{1,0:T(8,128)} %get-tuple-element.266.v_hbm, f32[1,8192]{1,0:T(1,128)S(1)} %bitcast.42, ...), custom_call_target="tpu_custom_call" | custom-call | flops 1000 | bytes 1000 | tf_op jit(solution)/shard_map/near/pallas_call | solution.py:457
  155.6 4.1 %collective-permute-done.27.refs_6_ = f32[46,32,128]{2,1,0:T(8,128)} collective-permute-done((f32[46,32,128]{2,1,0:T(8,128)}, f32[46,32,128]{2,1,0:T(8,128)}, u32[]{:S(2)}, u32[]{:S(2)}) %collective-permute-start.27) | collective-permute-done | bytes 753696 | tf_op jit(solution)/shard_map/ppermute | solution.py:27
  159.8 11.1 %far.35 = (f32[32,8192]{1,0:T(8,128)}, f32[32,8192]{1,0:T(8,128)}, f32[46,32,128]{2,1,0:T(8,128)}, f32[1,16384]{1,0:T(1,128)}, f32[46,32,128]{2,1,0:T(8,128)}) custom-call(s32[896]{0:T(1024)S(1)} %get-tuple-element.259.refs_0_, f32[64,4,128,128]{3,2,1,0:T(8,128)} %refs_1_.15, f32[3]{0:T(128)S(1)} %pad_maximum_fusion.coef_ref.refs_2_, ...), custom_call_target="tpu_custom_call" | custom-call | flops 1000 | bytes 1000 | tf_op jit(solution)/shard_map/far/pallas_call | solution.py:546
  170.9 5.4 %collective-permute-start.33 = (f32[46,32,128]{2,1,0:T(8,128)}, f32[46,32,128]{2,1,0:T(8,128)S(1)}, u32[]{:S(2)}, u32[]{:S(2)}) collective-permute-start(f32[46,32,128]{2,1,0:T(8,128)} %get-tuple-element.284), channel_id=1, source_target_pairs={{0,28},{4,0},{8,4},{12,8},{16,12},{20,16},{24,20},{28,24},{1,29},{... | collective-permute-start | bytes 2261000 | tf_op jit(solution)/shard_map/ppermute | solution.py:27
  176.3 11.7 %near.29.refs_3_ = f32[32,8192]{1,0:T(8,128)} custom-call(s32[896]{0:T(1024)S(1)} %get-tuple-element.503.list_ref, f32[3]{0:T(128)S(1)} %pad_maximum_fusion.coef_ref.refs_2_, f32[32,8192]{1,0:T(8,128)} %get-tuple-element.272.x_hbm.x1_ref, f32[32,8192]{1,0:T(8,128)} %get-tuple-element.274.v_hbm, f32[1,8192]{1,0:T(1,128)S(1)} %bitcast.43, ...), custom_call_target="tpu_custom_call" | custom-call | flops 1000 | bytes 1000 | tf_op jit(solution)/shard_map/near/pallas_call | solution.py:457
  188.0 6.7 %collective-permute-done.28.refs_4_ = f32[46,32,128]{2,1,0:T(8,128)} collective-permute-done((f32[46,32,128]{2,1,0:T(8,128)}, f32[46,32,128]{2,1,0:T(8,128)}, u32[]{:S(2)}, u32[]{:S(2)}) %collective-permute-start.28) | collective-permute-done | bytes 753696 | tf_op jit(solution)/shard_map/ppermute | solution.py:27
  197.7 7.9 %far.36.v_ref.refs_8_ = f32[64,8192]{1,0:T(8,128)} custom-call(s32[896]{0:T(1024)S(1)} %get-tuple-element.259.refs_0_, f32[64,4,128,128]{3,2,1,0:T(8,128)} %refs_1_.15, f32[3]{0:T(128)S(1)} %pad_maximum_fusion.coef_ref.refs_2_, f32[32,8192]{1,0:T(8,128)} %near.28.refs_3_, f32[46,32,128]{2,1,0:T(8,128)} %collective-permute-done.28.refs_4_, ...), custom_call_target="tpu_custom_call" | custom-call | flops 1000 | bytes 1000 | tf_op jit(solution)/shard_map/far/pallas_call | solution.py:546
  206.8 4.8 %spread.4 = (f32[64,8192]{1,0:T(8,128)}, f32[32,8192]{1,0:T(8,128)}, f32[8,64]{1,0:T(8,128)}, f32[8,32]{1,0:T(8,128)}) custom-call(f32[64,8192]{1,0:T(8,128)S(1)} %copy-done, f32[32,8192]{1,0:T(8,128)} %get-tuple-element.265.x_hbm.x0_ref, f32[32,8192]{1,0:T(8,128)} %get-tuple-element.272.x_hbm.x1_ref, f32[64,8192]{1,0:T(8,128)} %far.36.v_ref.refs_8_, ...), custom_call_target="tpu_custom_call" | custom-call | flops 1000 | bytes 1000 | tf_op jit(solution)/shard_map/spread/pallas_call | solution.py:595
  212.8 8.5 %far.37 = (f32[64,8192]{1,0:T(8,128)}, f32[8,32]{1,0:T(8,128)}) custom-call(s32[896]{0:T(1024)S(1)} %get-tuple-element.259.refs_0_, f32[64,4,128,128]{3,2,1,0:T(8,128)} %refs_1_.15, f32[3]{0:T(128)S(1)} %pad_maximum_fusion.coef_ref.refs_2_, f32[32,8192]{1,0:T(8,128)} %near.29.refs_3_, f32[46,32,128]{2,1,0:T(8,128)} %copy-done.11, ...), custom_call_target="tpu_custom_call", output_to_operand_aliasing={{0}: (8, {})} | custom-call | flops 1000 | bytes 1000 | tf_op jit(solution)/shard_map/far/pallas_call | solution.py:546
  (76 shorter events, 39.9 us)
Async XLA Ops:
  0.6 14.5 %copy-start = (f32[64,8192]{1,0:T(8,128)S(1)}, f32[64,8192]{1,0:T(8,128)}, u32[]{:S(2)}) copy-start(f32[64,8192]{1,0:T(8,128)} %start_ref.1) | copy-start | bytes 6291460
  3.1 7.6 %collective-permute-start.19 = (s32[128]{0:T(128)}, s32[128]{0:T(128)S(1)}, u32[]{:S(2)}, u32[]{:S(2)}) collective-permute-start(s32[128]{0:T(128)} %get-tuple-element.249), channel_id=1, source_target_pairs={{0,4},{4,8},{8,12},{12,16},{16,20},{20,24},{24,28},{28,0},{1,5},{5... | collective-permute-start | bytes 1544 | tf_op jit(solution)/shard_map/ppermute | solution.py:27
  13.1 52.3 %collective-permute-start.20 = (f32[46,32,128]{2,1,0:T(8,128)}, f32[46,32,128]{2,1,0:T(8,128)S(1)}, u32[]{:S(2)}, u32[]{:S(2)}) collective-permute-start(f32[46,32,128]{2,1,0:T(8,128)} %pack.8), channel_id=1, source_target_pairs={{0,28},{4,0},{8,4},{12,8},{16,12},{20,16},{24,20},{28,24},{1,29},{... | collective-permute-start | bytes 2261000 | tf_op jit(solution)/shard_map/ppermute | solution.py:27
  21.5 45.8 %collective-permute-start.21 = (f32[46,32,128]{2,1,0:T(8,128)}, f32[46,32,128]{2,1,0:T(8,128)}, u32[]{:S(2)}, u32[]{:S(2)}) collective-permute-start(f32[46,32,128]{2,1,0:T(8,128)} %far.30), channel_id=1, source_target_pairs={{0,4},{4,8},{8,12},{12,16},{16,20},{20,24},{24,28},{28,0},{1,5},{5... | collective-permute-start | bytes 2261000 | tf_op jit(solution)/shard_map/ppermute | solution.py:27
  23.4 11.8 %copy-start.2 = (f32[8192]{0:T(1024)S(1)}, f32[8192]{0:T(1024)}, u32[]{:S(2)}) copy-start(f32[8192]{0:T(1024)} %param.13) | copy-start | bytes 98308
  23.4 11.8 %copy-start.3 = (f32[8192]{0:T(1024)S(1)}, f32[8192]{0:T(1024)}, u32[]{:S(2)}) copy-start(f32[8192]{0:T(1024)} %param.14) | copy-start | bytes 98308
  29.7 65.5 %collective-permute-start.23 = (f32[46,32,128]{2,1,0:T(8,128)}, f32[46,32,128]{2,1,0:T(8,128)}, u32[]{:S(2)}, u32[]{:S(2)}) collective-permute-start(f32[46,32,128]{2,1,0:T(8,128)} %far.32), channel_id=1, source_target_pairs={{0,4},{4,8},{8,12},{12,16},{16,20},{20,24},{24,28},{28,0},{1,5},{5... | collective-permute-start | bytes 2261000 | tf_op jit(solution)/shard_map/ppermute | solution.py:27
  30.4 64.8 %collective-permute-start.22 = (f32[46,32,128]{2,1,0:T(8,128)}, f32[46,32,128]{2,1,0:T(8,128)}, u32[]{:S(2)}, u32[]{:S(2)}) collective-permute-start(f32[46,32,128]{2,1,0:T(8,128)} %pack.9), channel_id=1, source_target_pairs={{0,28},{4,0},{8,4},{12,8},{16,12},{20,16},{24,20},{28,24},{1,29},{... | collective-permute-start | bytes 2261000 | tf_op jit(solution)/shard_map/ppermute | solution.py:27
  77.5 45.9 %collective-permute-start.24 = (f32[46,32,128]{2,1,0:T(8,128)}, f32[46,32,128]{2,1,0:T(8,128)}, u32[]{:S(2)}, u32[]{:S(2)}) collective-permute-start(f32[46,32,128]{2,1,0:T(8,128)} %get-tuple-element.263), channel_id=1, source_target_pairs={{0,28},{4,0},{8,4},{12,8},{16,12},{20,16},{24,20},{28,24},{1,29},{... | collective-permute-start | bytes 2261000 | tf_op jit(solution)/shard_map/ppermute | solution.py:27
  78.4 49.1 %collective-permute-start.25 = (f32[46,32,128]{2,1,0:T(8,128)}, f32[46,32,128]{2,1,0:T(8,128)}, u32[]{:S(2)}, u32[]{:S(2)}) collective-permute-start(f32[46,32,128]{2,1,0:T(8,128)} %get-tuple-element.264), channel_id=1, source_target_pairs={{0,4},{4,8},{8,12},{12,16},{16,20},{20,24},{24,28},{28,0},{1,5},{5... | collective-permute-start | bytes 2261000 | tf_op jit(solution)/shard_map/ppermute | solution.py:27
  105.2 50.4 %collective-permute-start.26 = (f32[46,32,128]{2,1,0:T(8,128)}, f32[46,32,128]{2,1,0:T(8,128)S(1)}, u32[]{:S(2)}, u32[]{:S(2)}) collective-permute-start(f32[46,32,128]{2,1,0:T(8,128)} %get-tuple-element.269), channel_id=1, source_target_pairs={{0,28},{4,0},{8,4},{12,8},{16,12},{20,16},{24,20},{28,24},{1,29},{... | collective-permute-start | bytes 2261000 | tf_op jit(solution)/shard_map/ppermute | solution.py:27
  110.6 49.1 %collective-permute-start.27 = (f32[46,32,128]{2,1,0:T(8,128)}, f32[46,32,128]{2,1,0:T(8,128)}, u32[]{:S(2)}, u32[]{:S(2)}) collective-permute-start(f32[46,32,128]{2,1,0:T(8,128)} %get-tuple-element.270), channel_id=1, source_target_pairs={{0,4},{4,8},{8,12},{12,16},{16,20},{20,24},{24,28},{28,0},{1,5},{5... | collective-permute-start | bytes 2261000 | tf_op jit(solution)/shard_map/ppermute | solution.py:27
  138.6 56.2 %collective-permute-start.28 = (f32[46,32,128]{2,1,0:T(8,128)}, f32[46,32,128]{2,1,0:T(8,128)}, u32[]{:S(2)}, u32[]{:S(2)}) collective-permute-start(f32[46,32,128]{2,1,0:T(8,128)} %get-tuple-element.276), channel_id=1, source_target_pairs={{0,28},{4,0},{8,4},{12,8},{16,12},{20,16},{24,20},{28,24},{1,29},{... | collective-permute-start | bytes 2261000 | tf_op jit(solution)/shard_map/ppermute | solution.py:27
  144.0 52.4 %collective-permute-start.29 = (f32[46,32,128]{2,1,0:T(8,128)}, f32[46,32,128]{2,1,0:T(8,128)}, u32[]{:S(2)}, u32[]{:S(2)}) collective-permute-start(f32[46,32,128]{2,1,0:T(8,128)} %get-tuple-element.277), channel_id=1, source_target_pairs={{0,4},{4,8},{8,12},{12,16},{16,20},{20,24},{24,28},{28,0},{1,5},{5... | collective-permute-start | bytes 2261000 | tf_op jit(solution)/shard_map/ppermute | solution.py:27
  170.9 40.8 %collective-permute-start.33 = (f32[46,32,128]{2,1,0:T(8,128)}, f32[46,32,128]{2,1,0:T(8,128)S(1)}, u32[]{:S(2)}, u32[]{:S(2)}) collective-permute-start(f32[46,32,128]{2,1,0:T(8,128)} %get-tuple-element.284), channel_id=1, source_target_pairs={{0,28},{4,0},{8,4},{12,8},{16,12},{20,16},{24,20},{28,24},{1,29},{... | collective-permute-start | bytes 2261000 | tf_op jit(solution)/shard_map/ppermute | solution.py:27
  176.3 35.4 %collective-permute-start.34 = (f32[46,32,128]{2,1,0:T(8,128)}, f32[46,32,128]{2,1,0:T(8,128)S(1)}, u32[]{:S(2)}, u32[]{:S(2)}) collective-permute-start(f32[46,32,128]{2,1,0:T(8,128)} %get-tuple-element.285), channel_id=1, source_target_pairs={{0,4},{4,8},{8,12},{12,16},{16,20},{20,24},{24,28},{28,0},{1,5},{5... | collective-permute-start | bytes 2261000 | tf_op jit(solution)/shard_map/ppermute | solution.py:27
  176.3 20.1 %copy-start.22 = (s32[128]{0:T(128)S(1)}, s32[128]{0:T(128)}, u32[]{:S(2)}) copy-start(s32[128]{0:T(128)} %get-tuple-element.249) | copy-start | bytes 1540
  188.0 17.6 %collective-permute-start.30 = (f32[1,16384]{1,0:T(1,128)S(1)}, f32[1,16384]{1,0:T(1,128)S(1)}, u32[]{:S(2)}, u32[]{:S(2)}) collective-permute-start(f32[1,16384]{1,0:T(1,128)S(1)} %copy-done.16), channel_id=1, source_target_pairs={{0,1},{1,2},{2,3},{3,0},{4,5},{5,6},{6,7},{7,4},{8,9},{9,10},{10,1... | collective-permute-start | bytes 196616 | tf_op jit(solution)/shard_map/ppermute | solution.py:622
  194.7 10.8 %collective-permute-start.31 = (f32[1,16384]{1,0:T(1,128)S(1)}, f32[1,16384]{1,0:T(1,128)S(1)}, u32[]{:S(2)}, u32[]{:S(2)}) collective-permute-start(f32[1,16384]{1,0:T(1,128)S(1)} %copy-done.16), channel_id=1, source_target_pairs={{0,2},{1,3},{2,0},{3,1},{4,6},{5,7},{6,4},{7,5},{8,10},{9,11},{10,... | collective-permute-start | bytes 196616 | tf_op jit(solution)/shard_map/ppermute | solution.py:622
  196.4 9.2 %collective-permute-start.32 = (f32[1,16384]{1,0:T(1,128)S(1)}, f32[1,16384]{1,0:T(1,128)S(1)}, u32[]{:S(2)}, u32[]{:S(2)}) collective-permute-start(f32[1,16384]{1,0:T(1,128)S(1)} %copy-done.16), channel_id=1, source_target_pairs={{0,3},{1,0},{2,1},{3,2},{4,7},{5,4},{6,5},{7,6},{8,11},{9,8},{10,9... | collective-permute-start | bytes 196616 | tf_op jit(solution)/shard_map/ppermute | solution.py:622
  222.0 3.7 %collective-permute-start.35 = (f32[8,136]{1,0:T(8,128)S(1)}, f32[8,136]{1,0:T(8,128)S(1)}, u32[]{:S(2)}, u32[]{:S(2)}) collective-permute-start(f32[8,136]{1,0:T(8,128)S(1)} %maximum_maximum_fusion.1), channel_id=1, source_target_pairs={{0,4},{4,0},{8,12},{12,8},{16,20},{20,16},{24,28},{28,24},{1,5},{5... | collective-permute-start | bytes 13064 | tf_op jit(solution)/shard_map/ppermute | solution.py:634
  225.7 5.0 %collective-permute-start.36 = (f32[8,136]{1,0:T(8,128)S(1)}, f32[8,136]{1,0:T(8,128)S(1)}, u32[]{:S(2)}, u32[]{:S(2)}) collective-permute-start(f32[8,136]{1,0:T(8,128)S(1)} %add.36), channel_id=1, source_target_pairs={{0,8},{4,12},{8,0},{12,4},{16,24},{20,28},{24,16},{28,20},{1,9},{5... | collective-permute-start | bytes 13064 | tf_op jit(solution)/shard_map/ppermute | solution.py:634
  225.7 5.1 %collective-permute-start.37 = (f32[8,136]{1,0:T(8,128)S(1)}, f32[8,136]{1,0:T(8,128)S(1)}, u32[]{:S(2)}, u32[]{:S(2)}) collective-permute-start(f32[8,136]{1,0:T(8,128)S(1)} %add.36), channel_id=1, source_target_pairs={{0,16},{4,20},{8,24},{12,28},{16,0},{20,4},{24,8},{28,12},{1,17},{... | collective-permute-start | bytes 13064 | tf_op jit(solution)/shard_map/ppermute | solution.py:634
  227.1 5.4 %collective-permute-start.38 = (f32[8,136]{1,0:T(8,128)S(1)}, f32[8,136]{1,0:T(8,128)S(1)}, u32[]{:S(2)}, u32[]{:S(2)}) collective-permute-start(f32[8,136]{1,0:T(8,128)S(1)} %add.36), channel_id=1, source_target_pairs={{0,24},{4,28},{8,16},{12,20},{16,8},{20,12},{24,0},{28,4},{1,25},{... | collective-permute-start | bytes 13064 | tf_op jit(solution)/shard_map/ppermute | solution.py:634
  (10 other events, 37.6 us)

commit v3 on v2

--- a/solution.py
+++ b/solution.py
@@ -287,7 +287,8 @@
     if receives and sends:
         get_x.start()
     if dots:
-        get_off = pltpu.make_async_copy(off_hbm, off_buf, sems.at[5])
+        off_rows = off_hbm.at[pl.ds(out_row, chains)]
+        get_off = pltpu.make_async_copy(off_rows, off_buf, sems.at[5])
         get_off.start()
 
     if receives:
@@ -411,9 +412,9 @@
 
 
 def spread_kernel(
-    start_ref, x0_ref, x1_ref, v_ref, *refs, chain_total
+    start_ref, x0_ref, x1_ref, *refs, chain_total
 ):
-    *column_refs, position_ref, offset_ref, gain_ref, dot_ref, sums, means = refs
+    *column_refs, position_ref, offset_ref, gain_ref, sums, means = refs
     chains = x0_ref.shape[0]
     cells = start_ref.shape[1]
     means[...] = sum(ref[...] for ref in column_refs) / chain_total
@@ -428,18 +429,11 @@
         position_ref[upper, part] = x0
         position_ref[lower, part] = x1
         off_start = start_ref[:, part] - mean_start
-        off1 = x1 - mean_end
-        offset_ref[:, part] = off1
-        off_end = jnp.concatenate([x0 - mean_end, off1], axis=0)
+        off_end = jnp.concatenate([x0, x1], axis=0) - mean_end
+        offset_ref[:, part] = off_end
         return off_end * off_end - off_start * off_start
 
     gain_ref[...] = chain_sums(ends, sums, cells)
-
-    def first_dot(part):
-        mean_end = means[:, pl.ds(pl.multiple_of(cells + part.start, 128), part.size)]
-        return (x0_ref[:, part] - mean_end) * v_ref[:, part]
-
-    dot_ref[...] = chain_sums(first_dot, sums.at[upper], cells)
 
 
 SMEM = pl.BlockSpec(memory_space=pltpu.SMEM)
@@ -589,21 +583,18 @@
     )(given, x)
 
 
-def spread_call(start, x, v, columns, side, chain_total):
+def spread_call(start, x, columns, side, chain_total):
     local_chains, cells = start.shape
     chains = x[0].shape[0]
     return pl.pallas_call(
         functools.partial(spread_kernel, chain_total=chain_total),
         out_shape=[
             jax.ShapeDtypeStruct(start.shape, jnp.float32),
-            jax.ShapeDtypeStruct((chains, cells), jnp.float32),
+            jax.ShapeDtypeStruct(start.shape, jnp.float32),
             jax.ShapeDtypeStruct((8, local_chains), jnp.float32),
-            jax.ShapeDtypeStruct((8, chains), jnp.float32),
         ],
-        grid=(1,),
-        in_specs=[VMEM, VMEM, VMEM, pl.BlockSpec((chains, cells), lambda i: (0, 0))]
-        + [VMEM] * len(columns),
-        out_specs=[VMEM] * 4,
+        in_specs=[VMEM] * (3 + len(columns)),
+        out_specs=[VMEM] * 3,
         scratch_shapes=[
             pltpu.VMEM((local_chains, 4 * side), jnp.float32),
             pltpu.VMEM((1, 2 * cells), jnp.float32),
@@ -611,16 +602,22 @@
         compiler_params=PARAMS,
         cost_estimate=COST,
         name="spread",
-    )(start, *x, v, *columns)
-
-
-def shared_over(axis, value):
-    count = lax.axis_size(axis)
-    shared = [value]
-    for k in range(1, count):
-        pairs = [(source, (source + k) % count) for source in range(count)]
-        shared.append(lax.ppermute(value, axis, pairs))
-    return shared
+    )(start, *x, *columns)
+
+
+def add_kernel(a_ref, b_ref, out_ref):
+    out_ref[...] = a_ref[...] + b_ref[...]
+
+
+def add_call(a, b):
+    return pl.pallas_call(
+        add_kernel,
+        out_shape=jax.ShapeDtypeStruct(a.shape, a.dtype),
+        in_specs=[VMEM, VMEM],
+        out_specs=VMEM,
+        cost_estimate=COST,
+        name="add",
+    )(a, b)
 
 
 def summed_over(axis, value):
@@ -713,16 +710,24 @@
                 rows[h] = 0
                 w[h] = near(x[h], v[h], 0, 0, 1 - turn)
                 w = list(lax.optimization_barrier(tuple(w)))
-        column, w[1] = lax.optimization_barrier((column, w[1]))
-        (momentum,) = far(None, w[0], *flight[0], chains, 0, 0, cap)
-        position, offset, gain, dot = spread_call(
-            start, x, momentum, shared_over("grp", column), side, chain_total
-        )
-        momentum, last_dot = far(
-            None, w[1], *flight[1], chains, 0, 0, cap, None, offset, momentum, chains
-        )
+        reach, columns = 1, [column]
+        while reach < lax.axis_size("grp"):
+            column = add_call(*columns) if reach > 1 else column
+            pairs = [(g, g ^ reach) for g in range(lax.axis_size("grp"))]
+            other = lax.ppermute(column, "grp", pairs)
+            if reach == 1:
+                other, w[1] = lax.optimization_barrier((other, w[1]))
+            columns = [column, other]
+            reach *= 2
+        position, offset, gain = spread_call(start, x, columns, side, chain_total)
+        momentum, dots = None, []
+        for h in parts:
+            momentum, dot = far(
+                None, w[h], *flight[h], chains, 0, 0, cap, None, offset, momentum, h * chains
+            )
+            dots.append(dot)
         over = jnp.full((8, 8), (tiles[1] > cap).astype(jnp.float32))
-        sums = summed_over("rows", jnp.concatenate([gain, dot, last_dot, over], axis=1))[0]
+        sums = summed_over("rows", jnp.concatenate([gain, *dots, over], axis=1))[0]
         spread, inner = sums[:local_chains], sums[local_chains : 2 * local_chains]
         chees = trajectory * (spread / all_cells) * (inner / all_cells)
         return sums[-1], position, momentum, chees

time: 236 us -> 242 us (1.025)
  waiting for transfers between devices: 35.3 us -> 39.7 us
    ppermute x13, waiting for transfers between devices: 29.8 us -> 33.1 us  [passed_along(): return lax.ppermute(value, 'rows', pairs)]
  transfers between devices with their start and end apart: 20 -> 19, of which waited for: 8 -> 11; matrix products, arithmetic and copies ran while one was open for 1% -> 1% of each run, Pallas kernels for 60% -> 59%
where the time goes in v3:
time: 242 us
  Pallas kernels  156 us (64%)
  waiting for transfers between devices  39.7 us (16%)
  starting transfers between devices  35 us (14%)
  local copies, waits for them, and re-layouts  5.06 us (2%)
  between operations  3.05 us (1%)
    pallas_call x8, Pallas kernels, far_call(): pl.pallas_call(functools.partial(far_kernel, bands=bands, side=side, cap=...  71.8 us
    pallas_call x6, Pallas kernels, near_call(): pl.pallas_call(functools.partial(near_kernel, bands=bands, side=side, x_r...  67.4 us
    ppermute x13, waiting for transfers between devices, passed_along(): return lax.ppermute(value, 'rows', pairs)  33.1 us
    ppermute x13, starting transfers between devices, passed_along(): return lax.ppermute(value, 'rows', pairs)  27 us
    ppermute x4, starting transfers between devices, summed_over(): value = value + lax.ppermute(own, axis, pairs)  6.46 us
  transfers between devices with their start and end apart: 19, of which 11 were waited for; matrix products, arithmetic and copies ran while one was open for 1% of the time, Pallas kernels for 59%

profile of v3, /device:TPU:0, one launch (start us, length us, event | category | flops | bytes accessed | tf_op | source)
XLA Modules:
  0.0 242.0 jit_solution(16815656319474910943)
XLA Ops:
  15.4 6.3 %far.32 = f32[46,32,128]{2,1,0:T(8,128)} custom-call(s32[896]{0:T(1024)S(1)} %get-tuple-element.261.refs_0_, f32[64,4,128,128]{3,2,1,0:T(8,128)} %refs_1_.15, f32[64,8192]{1,0:T(8,128)S(1)} %copy-done), custom_call_target="tpu_custom_call" | custom-call | flops 1000 | bytes 1000 | tf_op jit(solution)/shard_map/far/pallas_call | solution.py:540
  23.5 4.7 %collective-permute-start.21 = (f32[46,32,128]{2,1,0:T(8,128)}, f32[46,32,128]{2,1,0:T(8,128)}, u32[]{:S(2)}, u32[]{:S(2)}) collective-permute-start(f32[46,32,128]{2,1,0:T(8,128)} %pack.9), channel_id=1, source_target_pairs={{0,28},{4,0},{8,4},{12,8},{16,12},{20,16},{24,20},{28,24},{1,29},{... | collective-permute-start | bytes 2261000 | tf_op jit(solution)/shard_map/ppermute | solution.py:27
  28.2 6.3 %far.34 = f32[46,32,128]{2,1,0:T(8,128)} custom-call(s32[896]{0:T(1024)S(1)} %get-tuple-element.261.refs_0_, f32[64,4,128,128]{3,2,1,0:T(8,128)} %refs_1_.15, f32[64,8192]{1,0:T(8,128)S(1)} %copy-done), custom_call_target="tpu_custom_call" | custom-call | flops 1000 | bytes 1000 | tf_op jit(solution)/shard_map/far/pallas_call | solution.py:540
  35.4 10.3 %near.24.refs_3_ = f32[32,8192]{1,0:T(8,128)} custom-call(s32[896]{0:T(1024)S(1)} %get-tuple-element.508.list_ref, f32[3]{0:T(128)S(1)} %pad_maximum_fusion.coef_ref.refs_2_, f32[64,8192]{1,0:T(8,128)S(1)} %copy-done, f32[64,8192]{1,0:T(8,128)} %v_hbm.3, f32[1,8192]{1,0:T(1,128)S(1)} %bitcast.38, f32[1,8192]{1,0:T(1,128)S(1)} %bitcast.45, ...), custom_call_target="tpu_custom_call" | custom-call | flops 1000 | bytes 1000 | tf_op jit(solution)/shard_map/near/pallas_call | solution.py:451
  45.7 10.3 %near.25.refs_3_ = f32[32,8192]{1,0:T(8,128)} custom-call(s32[896]{0:T(1024)S(1)} %get-tuple-element.508.list_ref, f32[3]{0:T(128)S(1)} %pad_maximum_fusion.coef_ref.refs_2_, f32[64,8192]{1,0:T(8,128)S(1)} %copy-done, f32[64,8192]{1,0:T(8,128)} %v_hbm.3, f32[1,8192]{1,0:T(1,128)S(1)} %bitcast.39, f32[1,8192]{1,0:T(1,128)S(1)} %bitcast.46, ...), custom_call_target="tpu_custom_call" | custom-call | flops 1000 | bytes 1000 | tf_op jit(solution)/shard_map/near/pallas_call | solution.py:451
  55.9 9.7 %collective-permute-done.19.parcel_ref.refs_4_ = f32[46,32,128]{2,1,0:T(8,128)S(1)} collective-permute-done((f32[46,32,128]{2,1,0:T(8,128)}, f32[46,32,128]{2,1,0:T(8,128)S(1)}, u32[]{:S(2)}, u32[]{:S(2)}) %collective-permute-start.19) | collective-permute-done | bytes 753696 | tf_op jit(solution)/shard_map/ppermute | solution.py:27
  67.7 10.1 %far.33 = (f32[32,8192]{1,0:T(8,128)}, f32[32,8192]{1,0:T(8,128)}, f32[46,32,128]{2,1,0:T(8,128)}, f32[46,32,128]{2,1,0:T(8,128)}) custom-call(s32[896]{0:T(1024)S(1)} %get-tuple-element.261.refs_0_, f32[64,4,128,128]{3,2,1,0:T(8,128)} %refs_1_.15, f32[3]{0:T(128)} %relay.2.refs_2_, f32[32,8192]{1,0:T(8,128)} %near.24.refs_3_, f32[46,32,128]{2,1,0:T(8,128)} %copy-done.6, ...), custom_call_target="tpu_custom_call" | custom-call | flops 1000 | bytes 1000 | tf_op jit(solution)/shard_map/far/pallas_call | solution.py:540
  79.8 11.6 %near.26.refs_3_ = f32[32,8192]{1,0:T(8,128)} custom-call(s32[896]{0:T(1024)S(1)} %get-tuple-element.508.list_ref, f32[3]{0:T(128)S(1)} %pad_maximum_fusion.coef_ref.refs_2_, f32[32,8192]{1,0:T(8,128)} %get-tuple-element.255.x_hbm.refs_7_, f32[32,8192]{1,0:T(8,128)} %get-tuple-element.256.v_hbm, f32[1,8192]{1,0:T(1,128)S(1)} %bitcast.40, ...), custom_call_target="tpu_custom_call" | custom-call | flops 1000 | bytes 1000 | tf_op jit(solution)/shard_map/near/pallas_call | solution.py:451
  91.5 3.7 %collective-permute-done.22.refs_6_ = f32[46,32,128]{2,1,0:T(8,128)} collective-permute-done((f32[46,32,128]{2,1,0:T(8,128)}, f32[46,32,128]{2,1,0:T(8,128)}, u32[]{:S(2)}, u32[]{:S(2)}) %collective-permute-start.22) | collective-permute-done | bytes 753696 | tf_op jit(solution)/shard_map/ppermute | solution.py:27
  95.2 10.0 %far.35 = (f32[32,8192]{1,0:T(8,128)}, f32[32,8192]{1,0:T(8,128)}, f32[46,32,128]{2,1,0:T(8,128)}, f32[46,32,128]{2,1,0:T(8,128)}) custom-call(s32[896]{0:T(1024)S(1)} %get-tuple-element.261.refs_0_, f32[64,4,128,128]{3,2,1,0:T(8,128)} %refs_1_.15, f32[3]{0:T(128)S(1)} %pad_maximum_fusion.coef_ref.refs_2_, f32[32,8192]{1,0:T(8,128)} %near.25.refs_3_, ...), custom_call_target="tpu_custom_call" | custom-call | flops 1000 | bytes 1000 | tf_op jit(solution)/shard_map/far/pallas_call | solution.py:540
  105.2 5.5 %collective-permute-start.25 = (f32[46,32,128]{2,1,0:T(8,128)}, f32[46,32,128]{2,1,0:T(8,128)}, u32[]{:S(2)}, u32[]{:S(2)}) collective-permute-start(f32[46,32,128]{2,1,0:T(8,128)} %get-tuple-element.271), channel_id=1, source_target_pairs={{0,28},{4,0},{8,4},{12,8},{16,12},{20,16},{24,20},{28,24},{1,29},{... | collective-permute-start | bytes 2261000 | tf_op jit(solution)/shard_map/ppermute | solution.py:27
  111.5 11.9 %near.27.refs_3_ = f32[32,8192]{1,0:T(8,128)} custom-call(s32[896]{0:T(1024)S(1)} %get-tuple-element.508.list_ref, f32[3]{0:T(128)S(1)} %pad_maximum_fusion.coef_ref.refs_2_, f32[32,8192]{1,0:T(8,128)} %get-tuple-element.262.x_hbm.refs_7_, f32[32,8192]{1,0:T(8,128)} %get-tuple-element.263.v_hbm, f32[1,8192]{1,0:T(1,128)S(1)} %bitcast.41, ...), custom_call_target="tpu_custom_call" | custom-call | flops 1000 | bytes 1000 | tf_op jit(solution)/shard_map/near/pallas_call | solution.py:451
  123.4 4.1 %collective-permute-done.24.refs_6_ = f32[46,32,128]{2,1,0:T(8,128)} collective-permute-done((f32[46,32,128]{2,1,0:T(8,128)}, f32[46,32,128]{2,1,0:T(8,128)}, u32[]{:S(2)}, u32[]{:S(2)}) %collective-permute-start.24) | collective-permute-done | bytes 753696 | tf_op jit(solution)/shard_map/ppermute | solution.py:27
  127.5 11.0 %far.36 = (f32[32,8192]{1,0:T(8,128)}, f32[32,8192]{1,0:T(8,128)}, f32[46,32,128]{2,1,0:T(8,128)}, f32[1,16384]{1,0:T(1,128)}, f32[46,32,128]{2,1,0:T(8,128)}) custom-call(s32[896]{0:T(1024)S(1)} %get-tuple-element.261.refs_0_, f32[64,4,128,128]{3,2,1,0:T(8,128)} %refs_1_.15, f32[3]{0:T(128)S(1)} %pad_maximum_fusion.coef_ref.refs_2_, ...), custom_call_target="tpu_custom_call" | custom-call | flops 1000 | bytes 1000 | tf_op jit(solution)/shard_map/far/pallas_call | solution.py:540
  138.5 11.7 %near.28.refs_3_ = f32[32,8192]{1,0:T(8,128)} custom-call(s32[896]{0:T(1024)S(1)} %get-tuple-element.508.list_ref, f32[3]{0:T(128)S(1)} %pad_maximum_fusion.coef_ref.refs_2_, f32[32,8192]{1,0:T(8,128)} %get-tuple-element.267.x_hbm.x0_ref, f32[32,8192]{1,0:T(8,128)} %get-tuple-element.268.v_hbm, f32[1,8192]{1,0:T(1,128)S(1)} %bitcast.42, ...), custom_call_target="tpu_custom_call" | custom-call | flops 1000 | bytes 1000 | tf_op jit(solution)/shard_map/near/pallas_call | solution.py:451
  150.2 5.5 %collective-permute-start.29 = (f32[46,32,128]{2,1,0:T(8,128)}, f32[46,32,128]{2,1,0:T(8,128)S(1)}, u32[]{:S(2)}, u32[]{:S(2)}) collective-permute-start(f32[46,32,128]{2,1,0:T(8,128)} %get-tuple-element.282), channel_id=1, source_target_pairs={{0,28},{4,0},{8,4},{12,8},{16,12},{20,16},{24,20},{28,24},{1,29},{... | collective-permute-start | bytes 2261000 | tf_op jit(solution)/shard_map/ppermute | solution.py:27
  155.7 11.0 %far.37 = (f32[32,8192]{1,0:T(8,128)}, f32[32,8192]{1,0:T(8,128)}, f32[46,32,128]{2,1,0:T(8,128)}, f32[1,16384]{1,0:T(1,128)}, f32[46,32,128]{2,1,0:T(8,128)}) custom-call(s32[896]{0:T(1024)S(1)} %get-tuple-element.261.refs_0_, f32[64,4,128,128]{3,2,1,0:T(8,128)} %refs_1_.15, f32[3]{0:T(128)S(1)} %pad_maximum_fusion.coef_ref.refs_2_, ...), custom_call_target="tpu_custom_call" | custom-call | flops 1000 | bytes 1000 | tf_op jit(solution)/shard_map/far/pallas_call | solution.py:540
  166.7 4.1 %collective-permute-start.31 = (f32[46,32,128]{2,1,0:T(8,128)}, f32[46,32,128]{2,1,0:T(8,128)}, u32[]{:S(2)}, u32[]{:S(2)}) collective-permute-start(f32[46,32,128]{2,1,0:T(8,128)} %get-tuple-element.287), channel_id=1, source_target_pairs={{0,28},{4,0},{8,4},{12,8},{16,12},{20,16},{24,20},{28,24},{1,29},{... | collective-permute-start | bytes 2261000 | tf_op jit(solution)/shard_map/ppermute | solution.py:27
  170.8 11.7 %near.29.refs_3_ = f32[32,8192]{1,0:T(8,128)} custom-call(s32[896]{0:T(1024)S(1)} %get-tuple-element.508.list_ref, f32[3]{0:T(128)S(1)} %pad_maximum_fusion.coef_ref.refs_2_, f32[32,8192]{1,0:T(8,128)} %get-tuple-element.274.x_hbm.x1_ref, f32[32,8192]{1,0:T(8,128)} %get-tuple-element.277.v_hbm, f32[1,8192]{1,0:T(1,128)S(1)} %bitcast.43, ...), custom_call_target="tpu_custom_call" | custom-call | flops 1000 | bytes 1000 | tf_op jit(solution)/shard_map/near/pallas_call | solution.py:451
  190.0 4.3 %spread.4 = (f32[64,8192]{1,0:T(8,128)}, f32[64,8192]{1,0:T(8,128)}, f32[8,64]{1,0:T(8,128)}) custom-call(f32[64,8192]{1,0:T(8,128)S(1)} %copy-done, f32[32,8192]{1,0:T(8,128)} %get-tuple-element.267.x_hbm.x0_ref, f32[32,8192]{1,0:T(8,128)} %get-tuple-element.274.x_hbm.x1_ref, f32[1,16384]{1,0:T(1,128)} %add.56.refs_0_, f32[1,16384]{1,0:T(1,128)} %copy-done.13), custom_call_target="tpu_custom_call" | custom-call | flops 1000 | bytes 1000 | tf_op jit(solution)/shard_map/spread/pallas_call | solution.py:589
  194.3 8.2 %collective-permute-done.29.refs_4_ = f32[46,32,128]{2,1,0:T(8,128)S(1)} collective-permute-done((f32[46,32,128]{2,1,0:T(8,128)}, f32[46,32,128]{2,1,0:T(8,128)S(1)}, u32[]{:S(2)}, u32[]{:S(2)}) %collective-permute-start.29) | collective-permute-done | bytes 753696 | tf_op jit(solution)/shard_map/ppermute | solution.py:27
  203.4 8.5 %far.38 = (f32[64,8192]{1,0:T(8,128)}, f32[8,32]{1,0:T(8,128)}) custom-call(s32[896]{0:T(1024)S(1)} %get-tuple-element.261.refs_0_, f32[64,4,128,128]{3,2,1,0:T(8,128)} %refs_1_.15, f32[3]{0:T(128)S(1)} %pad_maximum_fusion.coef_ref.refs_2_, f32[32,8192]{1,0:T(8,128)} %near.28.refs_3_, f32[46,32,128]{2,1,0:T(8,128)} %copy-done.9, ...), custom_call_target="tpu_custom_call" | custom-call | flops 1000 | bytes 1000 | tf_op jit(solution)/shard_map/far/pallas_call | solution.py:540
  211.9 5.9 %collective-permute-done.31.refs_4_ = f32[46,32,128]{2,1,0:T(8,128)} collective-permute-done((f32[46,32,128]{2,1,0:T(8,128)}, f32[46,32,128]{2,1,0:T(8,128)}, u32[]{:S(2)}, u32[]{:S(2)}) %collective-permute-start.31) | collective-permute-done | bytes 753696 | tf_op jit(solution)/shard_map/ppermute | solution.py:27
  218.0 8.5 %far.39 = (f32[64,8192]{1,0:T(8,128)}, f32[8,32]{1,0:T(8,128)}) custom-call(s32[896]{0:T(1024)S(1)} %get-tuple-element.261.refs_0_, f32[64,4,128,128]{3,2,1,0:T(8,128)} %refs_1_.15, f32[3]{0:T(128)S(1)} %pad_maximum_fusion.coef_ref.refs_2_, f32[32,8192]{1,0:T(8,128)} %near.29.refs_3_, ...), custom_call_target="tpu_custom_call", output_to_operand_aliasing={{0}: (8, {})} | custom-call | flops 1000 | bytes 1000 | tf_op jit(solution)/shard_map/far/pallas_call | solution.py:540
  (69 shorter events, 44.1 us)
Async XLA Ops:
  0.6 14.8 %copy-start = (f32[64,8192]{1,0:T(8,128)S(1)}, f32[64,8192]{1,0:T(8,128)}, u32[]{:S(2)}) copy-start(f32[64,8192]{1,0:T(8,128)} %start_ref.1) | copy-start | bytes 6291460
  3.1 7.8 %collective-permute-start.18 = (s32[128]{0:T(128)}, s32[128]{0:T(128)S(1)}, u32[]{:S(2)}, u32[]{:S(2)}) collective-permute-start(s32[128]{0:T(128)} %get-tuple-element.251), channel_id=1, source_target_pairs={{0,4},{4,8},{8,12},{12,16},{16,20},{20,24},{24,28},{28,0},{1,5},{5... | collective-permute-start | bytes 1544 | tf_op jit(solution)/shard_map/ppermute | solution.py:27
  13.3 52.3 %collective-permute-start.19 = (f32[46,32,128]{2,1,0:T(8,128)}, f32[46,32,128]{2,1,0:T(8,128)S(1)}, u32[]{:S(2)}, u32[]{:S(2)}) collective-permute-start(f32[46,32,128]{2,1,0:T(8,128)} %pack.8), channel_id=1, source_target_pairs={{0,28},{4,0},{8,4},{12,8},{16,12},{20,16},{24,20},{28,24},{1,29},{... | collective-permute-start | bytes 2261000 | tf_op jit(solution)/shard_map/ppermute | solution.py:27
  21.7 45.9 %collective-permute-start.20 = (f32[46,32,128]{2,1,0:T(8,128)}, f32[46,32,128]{2,1,0:T(8,128)}, u32[]{:S(2)}, u32[]{:S(2)}) collective-permute-start(f32[46,32,128]{2,1,0:T(8,128)} %far.32), channel_id=1, source_target_pairs={{0,4},{4,8},{8,12},{12,16},{16,20},{20,24},{24,28},{28,0},{1,5},{5... | collective-permute-start | bytes 2261000 | tf_op jit(solution)/shard_map/ppermute | solution.py:27
  23.5 11.9 %copy-start.2 = (f32[8192]{0:T(1024)S(1)}, f32[8192]{0:T(1024)}, u32[]{:S(2)}) copy-start(f32[8192]{0:T(1024)} %param.13) | copy-start | bytes 98308
  23.5 11.9 %copy-start.3 = (f32[8192]{0:T(1024)S(1)}, f32[8192]{0:T(1024)}, u32[]{:S(2)}) copy-start(f32[8192]{0:T(1024)} %param.14) | copy-start | bytes 98308
  23.5 68.0 %collective-permute-start.21 = (f32[46,32,128]{2,1,0:T(8,128)}, f32[46,32,128]{2,1,0:T(8,128)}, u32[]{:S(2)}, u32[]{:S(2)}) collective-permute-start(f32[46,32,128]{2,1,0:T(8,128)} %pack.9), channel_id=1, source_target_pairs={{0,28},{4,0},{8,4},{12,8},{16,12},{20,16},{24,20},{28,24},{1,29},{... | collective-permute-start | bytes 2261000 | tf_op jit(solution)/shard_map/ppermute | solution.py:27
  34.6 60.6 %collective-permute-start.22 = (f32[46,32,128]{2,1,0:T(8,128)}, f32[46,32,128]{2,1,0:T(8,128)}, u32[]{:S(2)}, u32[]{:S(2)}) collective-permute-start(f32[46,32,128]{2,1,0:T(8,128)} %far.34), channel_id=1, source_target_pairs={{0,4},{4,8},{8,12},{12,16},{16,20},{20,24},{24,28},{28,0},{1,5},{5... | collective-permute-start | bytes 2261000 | tf_op jit(solution)/shard_map/ppermute | solution.py:27
  77.8 45.7 %collective-permute-start.23 = (f32[46,32,128]{2,1,0:T(8,128)}, f32[46,32,128]{2,1,0:T(8,128)S(1)}, u32[]{:S(2)}, u32[]{:S(2)}) collective-permute-start(f32[46,32,128]{2,1,0:T(8,128)} %get-tuple-element.265), channel_id=1, source_target_pairs={{0,28},{4,0},{8,4},{12,8},{16,12},{20,16},{24,20},{28,24},{1,29},{... | collective-permute-start | bytes 2261000 | tf_op jit(solution)/shard_map/ppermute | solution.py:27
  78.5 49.0 %collective-permute-start.24 = (f32[46,32,128]{2,1,0:T(8,128)}, f32[46,32,128]{2,1,0:T(8,128)}, u32[]{:S(2)}, u32[]{:S(2)}) collective-permute-start(f32[46,32,128]{2,1,0:T(8,128)} %get-tuple-element.266), channel_id=1, source_target_pairs={{0,4},{4,8},{8,12},{12,16},{16,20},{20,24},{24,28},{28,0},{1,5},{5... | collective-permute-start | bytes 2261000 | tf_op jit(solution)/shard_map/ppermute | solution.py:27
  105.2 50.4 %collective-permute-start.25 = (f32[46,32,128]{2,1,0:T(8,128)}, f32[46,32,128]{2,1,0:T(8,128)}, u32[]{:S(2)}, u32[]{:S(2)}) collective-permute-start(f32[46,32,128]{2,1,0:T(8,128)} %get-tuple-element.271), channel_id=1, source_target_pairs={{0,28},{4,0},{8,4},{12,8},{16,12},{20,16},{24,20},{28,24},{1,29},{... | collective-permute-start | bytes 2261000 | tf_op jit(solution)/shard_map/ppermute | solution.py:27
  110.7 45.0 %collective-permute-start.26 = (f32[46,32,128]{2,1,0:T(8,128)}, f32[46,32,128]{2,1,0:T(8,128)}, u32[]{:S(2)}, u32[]{:S(2)}) collective-permute-start(f32[46,32,128]{2,1,0:T(8,128)} %get-tuple-element.272), channel_id=1, source_target_pairs={{0,4},{4,8},{8,12},{12,16},{16,20},{20,24},{24,28},{28,0},{1,5},{5... | collective-permute-start | bytes 2261000 | tf_op jit(solution)/shard_map/ppermute | solution.py:27
  150.2 52.3 %collective-permute-start.29 = (f32[46,32,128]{2,1,0:T(8,128)}, f32[46,32,128]{2,1,0:T(8,128)S(1)}, u32[]{:S(2)}, u32[]{:S(2)}) collective-permute-start(f32[46,32,128]{2,1,0:T(8,128)} %get-tuple-element.282), channel_id=1, source_target_pairs={{0,28},{4,0},{8,4},{12,8},{16,12},{20,16},{24,20},{28,24},{1,29},{... | collective-permute-start | bytes 2261000 | tf_op jit(solution)/shard_map/ppermute | solution.py:27
  155.7 46.8 %collective-permute-start.30 = (f32[46,32,128]{2,1,0:T(8,128)}, f32[46,32,128]{2,1,0:T(8,128)}, u32[]{:S(2)}, u32[]{:S(2)}) collective-permute-start(f32[46,32,128]{2,1,0:T(8,128)} %get-tuple-element.283), channel_id=1, source_target_pairs={{0,4},{4,8},{8,12},{12,16},{16,20},{20,24},{24,28},{28,0},{1,5},{5... | collective-permute-start | bytes 2261000 | tf_op jit(solution)/shard_map/ppermute | solution.py:27
  166.7 51.1 %collective-permute-start.31 = (f32[46,32,128]{2,1,0:T(8,128)}, f32[46,32,128]{2,1,0:T(8,128)}, u32[]{:S(2)}, u32[]{:S(2)}) collective-permute-start(f32[46,32,128]{2,1,0:T(8,128)} %get-tuple-element.287), channel_id=1, source_target_pairs={{0,28},{4,0},{8,4},{12,8},{16,12},{20,16},{24,20},{28,24},{1,29},{... | collective-permute-start | bytes 2261000 | tf_op jit(solution)/shard_map/ppermute | solution.py:27
  170.8 47.2 %collective-permute-start.32 = (f32[46,32,128]{2,1,0:T(8,128)}, f32[46,32,128]{2,1,0:T(8,128)}, u32[]{:S(2)}, u32[]{:S(2)}) collective-permute-start(f32[46,32,128]{2,1,0:T(8,128)} %get-tuple-element.288), channel_id=1, source_target_pairs={{0,4},{4,8},{8,12},{12,16},{16,20},{20,24},{24,28},{28,0},{1,5},{5... | collective-permute-start | bytes 2261000 | tf_op jit(solution)/shard_map/ppermute | solution.py:27
  170.8 11.7 %collective-permute-start.27 = (f32[1,16384]{1,0:T(1,128)}, f32[1,16384]{1,0:T(1,128)S(1)}, u32[]{:S(2)}, u32[]{:S(2)}) collective-permute-start(f32[1,16384]{1,0:T(1,128)} %get-tuple-element.275.a_ref), channel_id=1, source_target_pairs={{0,1},{1,0},{2,3},{3,2},{4,5},{5,4},{6,7},{7,6},{8,9},{9,8},{10,11... | collective-permute-start | bytes 196616 | tf_op jit(solution)/shard_map/ppermute | solution.py:717
  170.8 15.3 %copy-start.17 = (s32[128]{0:T(128)S(1)}, s32[128]{0:T(128)}, u32[]{:S(2)}) copy-start(s32[128]{0:T(128)} %get-tuple-element.251) | copy-start | bytes 1540
  184.6 4.7 %collective-permute-start.28 = (f32[1,16384]{1,0:T(1,128)}, f32[1,16384]{1,0:T(1,128)S(1)}, u32[]{:S(2)}, u32[]{:S(2)}) collective-permute-start(f32[1,16384]{1,0:T(1,128)} %add.56.refs_0_), channel_id=1, source_target_pairs={{0,2},{1,3},{2,0},{3,1},{4,6},{5,7},{6,4},{7,5},{8,10},{9,11},{10,... | collective-permute-start | bytes 196616 | tf_op jit(solution)/shard_map/ppermute | solution.py:717
  217.9 8.5 %copy-start.16 = (f32[8,32]{1,0:T(8,128)S(1)}, f32[8,32]{1,0:T(8,128)}, u32[]{:S(2)}) copy-start(f32[8,32]{1,0:T(8,128)} %get-tuple-element.285) | copy-start | bytes 3076
  227.2 3.7 %collective-permute-start.33 = (f32[8,136]{1,0:T(8,128)S(1)}, f32[8,136]{1,0:T(8,128)S(1)}, u32[]{:S(2)}, u32[]{:S(2)}) collective-permute-start(f32[8,136]{1,0:T(8,128)S(1)} %maximum_maximum_fusion.1), channel_id=1, source_target_pairs={{0,4},{4,0},{8,12},{12,8},{16,20},{20,16},{24,28},{28,24},{1,5},{5... | collective-permute-start | bytes 13064 | tf_op jit(solution)/shard_map/ppermute | solution.py:631
  230.9 5.4 %collective-permute-start.36 = (f32[8,136]{1,0:T(8,128)S(1)}, f32[8,136]{1,0:T(8,128)S(1)}, u32[]{:S(2)}, u32[]{:S(2)}) collective-permute-start(f32[8,136]{1,0:T(8,128)S(1)} %add.38), channel_id=1, source_target_pairs={{0,24},{4,28},{8,16},{12,20},{16,8},{20,12},{24,0},{28,4},{1,25},{... | collective-permute-start | bytes 13064 | tf_op jit(solution)/shard_map/ppermute | solution.py:631
  234.4 4.5 %collective-permute-start.35 = (f32[8,136]{1,0:T(8,128)S(1)}, f32[8,136]{1,0:T(8,128)S(1)}, u32[]{:S(2)}, u32[]{:S(2)}) collective-permute-start(f32[8,136]{1,0:T(8,128)S(1)} %add.38), channel_id=1, source_target_pairs={{0,16},{4,20},{8,24},{12,28},{16,0},{20,4},{24,8},{28,12},{1,17},{... | collective-permute-start | bytes 13064 | tf_op jit(solution)/shard_map/ppermute | solution.py:631
  234.9 4.1 %collective-permute-start.34 = (f32[8,136]{1,0:T(8,128)S(1)}, f32[8,136]{1,0:T(8,128)S(1)}, u32[]{:S(2)}, u32[]{:S(2)}) collective-permute-start(f32[8,136]{1,0:T(8,128)S(1)} %add.38), channel_id=1, source_target_pairs={{0,8},{4,12},{8,0},{12,4},{16,24},{20,28},{24,16},{28,20},{1,9},{5... | collective-permute-start | bytes 13064 | tf_op jit(solution)/shard_map/ppermute | solution.py:631
  (6 other events, 15.7 us)

commit v4 on v2

--- a/solution.py
+++ b/solution.py
@@ -9,7 +9,7 @@
 
 CHUNKS = 2
 GROUP = 12
-CAP = 46
+CAP = 45
 VMEM_LIMIT = 60 * 2**20
 LIST_AT = 8
 ROW_AT = 128

time: 236 us -> 232 us (0.983)
  starting transfers between devices: 34.3 us -> 30.9 us
    ppermute x13, starting transfers between devices: 28.2 us -> 24.8 us  [passed_along(): return lax.ppermute(value, 'rows', pairs)]
  transfers between devices with their start and end apart: 20 -> 20, of which waited for: 8 -> 8; matrix products, arithmetic and copies ran while one was open for 1% -> 1% of each run, Pallas kernels for 60% -> 61%
where the time goes in v4:
time: 232 us
  Pallas kernels  154 us (66%)
  waiting for transfers between devices  35.3 us (15%)
  starting transfers between devices  30.9 us (13%)
  local copies, waits for them, and re-layouts  5.08 us (2%)
  between operations  3.13 us (1%)
    pallas_call x8, Pallas kernels, far_call(): pl.pallas_call(functools.partial(far_kernel, bands=bands, side=side, cap=...  71.2 us
    pallas_call x6, Pallas kernels, near_call(): pl.pallas_call(functools.partial(near_kernel, bands=bands, side=side, x_r...  67.5 us
    ppermute x13, waiting for transfers between devices, passed_along(): return lax.ppermute(value, 'rows', pairs)  29.5 us
    ppermute x13, starting transfers between devices, passed_along(): return lax.ppermute(value, 'rows', pairs)  24.8 us
    ppermute x4, waiting for transfers between devices, summed_over(): value = value + lax.ppermute(own, axis, pairs)  5.7 us
    pallas_call x1, Pallas kernels, spread_call(): pl.pallas_call(functools.partial(spread_kernel, chain_total=chain_total),...  4.79 us
  transfers between devices with their start and end apart: 20, of which 8 were waited for; matrix products, arithmetic and copies ran while one was open for 1% of the time, Pallas kernels for 61%

profile of v4, /device:TPU:0, one launch (start us, length us, event | category | flops | bytes accessed | tf_op | source)
XLA Modules:
  0.0 231.9 jit_solution(4118591335088317162)
XLA Ops:
  6.1 3.3 %edges.1 = (s32[896]{0:T(1024)S(1)}, s32[896]{0:T(1024)S(1)}) custom-call(s32[1]{0:T(128)} %bitcast.4.first_ref, s32[4,64]{1,0:T(4,128)} %bitcast.55, s32[64]{0:T(128)} %count_ref.3, s32[72]{0:T(128)} %get-tuple-element.246.place_ref), custom_call_target="tpu_custom_call" | custom-call | flops 1000 | bytes 1000 | tf_op jit(solution)/shard_map/edges/pallas_call | solution.py:664
  15.1 6.4 %far.30 = f32[45,32,128]{2,1,0:T(8,128)} custom-call(s32[896]{0:T(1024)S(1)} %get-tuple-element.259.refs_0_, f32[64,4,128,128]{3,2,1,0:T(8,128)} %refs_1_.15, f32[64,8192]{1,0:T(8,128)S(1)} %copy-done), custom_call_target="tpu_custom_call" | custom-call | flops 1000 | bytes 1000 | tf_op jit(solution)/shard_map/far/pallas_call | solution.py:546
  23.3 6.3 %far.32 = f32[45,32,128]{2,1,0:T(8,128)} custom-call(s32[896]{0:T(1024)S(1)} %get-tuple-element.259.refs_0_, f32[64,4,128,128]{3,2,1,0:T(8,128)} %refs_1_.15, f32[64,8192]{1,0:T(8,128)S(1)} %copy-done), custom_call_target="tpu_custom_call" | custom-call | flops 1000 | bytes 1000 | tf_op jit(solution)/shard_map/far/pallas_call | solution.py:546
  30.7 3.8 %collective-permute-start.22 = (f32[45,32,128]{2,1,0:T(8,128)}, f32[45,32,128]{2,1,0:T(8,128)}, u32[]{:S(2)}, u32[]{:S(2)}) collective-permute-start(f32[45,32,128]{2,1,0:T(8,128)} %pack.9), channel_id=1, source_target_pairs={{0,28},{4,0},{8,4},{12,8},{16,12},{20,16},{24,20},{28,24},{1,29},{... | collective-permute-start | bytes 2211848 | tf_op jit(solution)/shard_map/ppermute | solution.py:27
  35.2 10.3 %near.24.refs_3_ = f32[32,8192]{1,0:T(8,128)} custom-call(s32[896]{0:T(1024)S(1)} %get-tuple-element.503.list_ref, f32[3]{0:T(128)S(1)} %pad_maximum_fusion.coef_ref.refs_2_, f32[64,8192]{1,0:T(8,128)S(1)} %copy-done, f32[64,8192]{1,0:T(8,128)} %v_hbm.3, f32[1,8192]{1,0:T(1,128)S(1)} %bitcast.38, f32[1,8192]{1,0:T(1,128)S(1)} %bitcast.45, ...), custom_call_target="tpu_custom_call" | custom-call | flops 1000 | bytes 1000 | tf_op jit(solution)/shard_map/near/pallas_call | solution.py:457
  45.5 10.3 %near.25.refs_3_ = f32[32,8192]{1,0:T(8,128)} custom-call(s32[896]{0:T(1024)S(1)} %get-tuple-element.503.list_ref, f32[3]{0:T(128)S(1)} %pad_maximum_fusion.coef_ref.refs_2_, f32[64,8192]{1,0:T(8,128)S(1)} %copy-done, f32[64,8192]{1,0:T(8,128)} %v_hbm.3, f32[1,8192]{1,0:T(1,128)S(1)} %bitcast.39, f32[1,8192]{1,0:T(1,128)S(1)} %bitcast.46, ...), custom_call_target="tpu_custom_call" | custom-call | flops 1000 | bytes 1000 | tf_op jit(solution)/shard_map/near/pallas_call | solution.py:457
  55.8 8.6 %collective-permute-done.20.parcel_ref.refs_4_ = f32[45,32,128]{2,1,0:T(8,128)S(1)} collective-permute-done((f32[45,32,128]{2,1,0:T(8,128)}, f32[45,32,128]{2,1,0:T(8,128)S(1)}, u32[]{:S(2)}, u32[]{:S(2)}) %collective-permute-start.20) | collective-permute-done | bytes 737312 | tf_op jit(solution)/shard_map/ppermute | solution.py:27
  66.3 10.1 %far.31 = (f32[32,8192]{1,0:T(8,128)}, f32[32,8192]{1,0:T(8,128)}, f32[45,32,128]{2,1,0:T(8,128)}, f32[45,32,128]{2,1,0:T(8,128)}) custom-call(s32[896]{0:T(1024)S(1)} %get-tuple-element.259.refs_0_, f32[64,4,128,128]{3,2,1,0:T(8,128)} %refs_1_.15, f32[3]{0:T(128)} %relay.2.refs_2_, f32[32,8192]{1,0:T(8,128)} %near.24.refs_3_, f32[45,32,128]{2,1,0:T(8,128)} %copy-done.6, ...), custom_call_target="tpu_custom_call" | custom-call | flops 1000 | bytes 1000 | tf_op jit(solution)/shard_map/far/pallas_call | solution.py:546
  78.5 11.6 %near.26.refs_3_ = f32[32,8192]{1,0:T(8,128)} custom-call(s32[896]{0:T(1024)S(1)} %get-tuple-element.503.list_ref, f32[3]{0:T(128)S(1)} %pad_maximum_fusion.coef_ref.refs_2_, f32[32,8192]{1,0:T(8,128)} %get-tuple-element.253.x_hbm.refs_7_, f32[32,8192]{1,0:T(8,128)} %get-tuple-element.254.v_hbm, f32[1,8192]{1,0:T(1,128)S(1)} %bitcast.40, ...), custom_call_target="tpu_custom_call" | custom-call | flops 1000 | bytes 1000 | tf_op jit(solution)/shard_map/near/pallas_call | solution.py:457
  93.4 10.0 %far.33 = (f32[32,8192]{1,0:T(8,128)}, f32[32,8192]{1,0:T(8,128)}, f32[45,32,128]{2,1,0:T(8,128)}, f32[45,32,128]{2,1,0:T(8,128)}) custom-call(s32[896]{0:T(1024)S(1)} %get-tuple-element.259.refs_0_, f32[64,4,128,128]{3,2,1,0:T(8,128)} %refs_1_.15, f32[3]{0:T(128)S(1)} %pad_maximum_fusion.coef_ref.refs_2_, f32[32,8192]{1,0:T(8,128)} %near.25.refs_3_, ...), custom_call_target="tpu_custom_call" | custom-call | flops 1000 | bytes 1000 | tf_op jit(solution)/shard_map/far/pallas_call | solution.py:546
  103.4 5.4 %collective-permute-start.26 = (f32[45,32,128]{2,1,0:T(8,128)}, f32[45,32,128]{2,1,0:T(8,128)S(1)}, u32[]{:S(2)}, u32[]{:S(2)}) collective-permute-start(f32[45,32,128]{2,1,0:T(8,128)} %get-tuple-element.269), channel_id=1, source_target_pairs={{0,28},{4,0},{8,4},{12,8},{16,12},{20,16},{24,20},{28,24},{1,29},{... | collective-permute-start | bytes 2211848 | tf_op jit(solution)/shard_map/ppermute | solution.py:27
  109.6 11.9 %near.27.refs_3_ = f32[32,8192]{1,0:T(8,128)} custom-call(s32[896]{0:T(1024)S(1)} %get-tuple-element.503.list_ref, f32[3]{0:T(128)S(1)} %pad_maximum_fusion.coef_ref.refs_2_, f32[32,8192]{1,0:T(8,128)} %get-tuple-element.260.x_hbm.refs_7_, f32[32,8192]{1,0:T(8,128)} %get-tuple-element.261.v_hbm, f32[1,8192]{1,0:T(1,128)S(1)} %bitcast.41, ...), custom_call_target="tpu_custom_call" | custom-call | flops 1000 | bytes 1000 | tf_op jit(solution)/shard_map/near/pallas_call | solution.py:457
  121.6 3.4 %collective-permute-done.25.refs_6_ = f32[45,32,128]{2,1,0:T(8,128)} collective-permute-done((f32[45,32,128]{2,1,0:T(8,128)}, f32[45,32,128]{2,1,0:T(8,128)}, u32[]{:S(2)}, u32[]{:S(2)}) %collective-permute-start.25) | collective-permute-done | bytes 737312 | tf_op jit(solution)/shard_map/ppermute | solution.py:27
  125.0 11.1 %far.34 = (f32[32,8192]{1,0:T(8,128)}, f32[32,8192]{1,0:T(8,128)}, f32[45,32,128]{2,1,0:T(8,128)}, f32[1,16384]{1,0:T(1,128)}, f32[45,32,128]{2,1,0:T(8,128)}) custom-call(s32[896]{0:T(1024)S(1)} %get-tuple-element.259.refs_0_, f32[64,4,128,128]{3,2,1,0:T(8,128)} %refs_1_.15, f32[3]{0:T(128)S(1)} %pad_maximum_fusion.coef_ref.refs_2_, ...), custom_call_target="tpu_custom_call" | custom-call | flops 1000 | bytes 1000 | tf_op jit(solution)/shard_map/far/pallas_call | solution.py:546
  136.1 5.4 %collective-permute-start.28 = (f32[45,32,128]{2,1,0:T(8,128)}, f32[45,32,128]{2,1,0:T(8,128)}, u32[]{:S(2)}, u32[]{:S(2)}) collective-permute-start(f32[45,32,128]{2,1,0:T(8,128)} %get-tuple-element.276), channel_id=1, source_target_pairs={{0,28},{4,0},{8,4},{12,8},{16,12},{20,16},{24,20},{28,24},{1,29},{... | collective-permute-start | bytes 2211848 | tf_op jit(solution)/shard_map/ppermute | solution.py:27
  141.5 11.6 %near.28.refs_3_ = f32[32,8192]{1,0:T(8,128)} custom-call(s32[896]{0:T(1024)S(1)} %get-tuple-element.503.list_ref, f32[3]{0:T(128)S(1)} %pad_maximum_fusion.coef_ref.refs_2_, f32[32,8192]{1,0:T(8,128)} %get-tuple-element.265.x_hbm.x0_ref, f32[32,8192]{1,0:T(8,128)} %get-tuple-element.266.v_hbm, f32[1,8192]{1,0:T(1,128)S(1)} %bitcast.42, ...), custom_call_target="tpu_custom_call" | custom-call | flops 1000 | bytes 1000 | tf_op jit(solution)/shard_map/near/pallas_call | solution.py:457
  153.1 3.5 %collective-permute-done.27.refs_6_ = f32[45,32,128]{2,1,0:T(8,128)} collective-permute-done((f32[45,32,128]{2,1,0:T(8,128)}, f32[45,32,128]{2,1,0:T(8,128)}, u32[]{:S(2)}, u32[]{:S(2)}) %collective-permute-start.27) | collective-permute-done | bytes 737312 | tf_op jit(solution)/shard_map/ppermute | solution.py:27
  156.6 11.0 %far.35 = (f32[32,8192]{1,0:T(8,128)}, f32[32,8192]{1,0:T(8,128)}, f32[45,32,128]{2,1,0:T(8,128)}, f32[1,16384]{1,0:T(1,128)}, f32[45,32,128]{2,1,0:T(8,128)}) custom-call(s32[896]{0:T(1024)S(1)} %get-tuple-element.259.refs_0_, f32[64,4,128,128]{3,2,1,0:T(8,128)} %refs_1_.15, f32[3]{0:T(128)S(1)} %pad_maximum_fusion.coef_ref.refs_2_, ...), custom_call_target="tpu_custom_call" | custom-call | flops 1000 | bytes 1000 | tf_op jit(solution)/shard_map/far/pallas_call | solution.py:546
  169.7 11.7 %near.29.refs_3_ = f32[32,8192]{1,0:T(8,128)} custom-call(s32[896]{0:T(1024)S(1)} %get-tuple-element.503.list_ref, f32[3]{0:T(128)S(1)} %pad_maximum_fusion.coef_ref.refs_2_, f32[32,8192]{1,0:T(8,128)} %get-tuple-element.272.x_hbm.x1_ref, f32[32,8192]{1,0:T(8,128)} %get-tuple-element.274.v_hbm, f32[1,8192]{1,0:T(1,128)S(1)} %bitcast.43, ...), custom_call_target="tpu_custom_call" | custom-call | flops 1000 | bytes 1000 | tf_op jit(solution)/shard_map/near/pallas_call | solution.py:457
  181.5 9.5 %collective-permute-done.28.refs_4_ = f32[45,32,128]{2,1,0:T(8,128)} collective-permute-done((f32[45,32,128]{2,1,0:T(8,128)}, f32[45,32,128]{2,1,0:T(8,128)}, u32[]{:S(2)}, u32[]{:S(2)}) %collective-permute-start.28) | collective-permute-done | bytes 737312 | tf_op jit(solution)/shard_map/ppermute | solution.py:27
  193.9 7.9 %far.36.v_ref.refs_8_ = f32[64,8192]{1,0:T(8,128)} custom-call(s32[896]{0:T(1024)S(1)} %get-tuple-element.259.refs_0_, f32[64,4,128,128]{3,2,1,0:T(8,128)} %refs_1_.15, f32[3]{0:T(128)S(1)} %pad_maximum_fusion.coef_ref.refs_2_, f32[32,8192]{1,0:T(8,128)} %near.28.refs_3_, f32[45,32,128]{2,1,0:T(8,128)} %collective-permute-done.28.refs_4_, ...), custom_call_target="tpu_custom_call" | custom-call | flops 1000 | bytes 1000 | tf_op jit(solution)/shard_map/far/pallas_call | solution.py:546
  203.1 4.8 %spread.4 = (f32[64,8192]{1,0:T(8,128)}, f32[32,8192]{1,0:T(8,128)}, f32[8,64]{1,0:T(8,128)}, f32[8,32]{1,0:T(8,128)}) custom-call(f32[64,8192]{1,0:T(8,128)S(1)} %copy-done, f32[32,8192]{1,0:T(8,128)} %get-tuple-element.265.x_hbm.x0_ref, f32[32,8192]{1,0:T(8,128)} %get-tuple-element.272.x_hbm.x1_ref, f32[64,8192]{1,0:T(8,128)} %far.36.v_ref.refs_8_, ...), custom_call_target="tpu_custom_call" | custom-call | flops 1000 | bytes 1000 | tf_op jit(solution)/shard_map/spread/pallas_call | solution.py:595
  209.0 8.4 %far.37 = (f32[64,8192]{1,0:T(8,128)}, f32[8,32]{1,0:T(8,128)}) custom-call(s32[896]{0:T(1024)S(1)} %get-tuple-element.259.refs_0_, f32[64,4,128,128]{3,2,1,0:T(8,128)} %refs_1_.15, f32[3]{0:T(128)S(1)} %pad_maximum_fusion.coef_ref.refs_2_, f32[32,8192]{1,0:T(8,128)} %near.29.refs_3_, f32[45,32,128]{2,1,0:T(8,128)} %copy-done.11, ...), custom_call_target="tpu_custom_call", output_to_operand_aliasing={{0}: (8, {})} | custom-call | flops 1000 | bytes 1000 | tf_op jit(solution)/shard_map/far/pallas_call | solution.py:546
  218.2 3.6 %collective-permute-done.35 = f32[8,136]{1,0:T(8,128)S(1)} collective-permute-done((f32[8,136]{1,0:T(8,128)S(1)}, f32[8,136]{1,0:T(8,128)S(1)}, u32[]{:S(2)}, u32[]{:S(2)}) %collective-permute-start.35) | collective-permute-done | bytes 4384 | tf_op jit(solution)/shard_map/ppermute | solution.py:634
  (76 shorter events, 38.8 us)
Async XLA Ops:
  0.6 14.5 %copy-start = (f32[64,8192]{1,0:T(8,128)S(1)}, f32[64,8192]{1,0:T(8,128)}, u32[]{:S(2)}) copy-start(f32[64,8192]{1,0:T(8,128)} %start_ref.1) | copy-start | bytes 6291460
  3.1 7.6 %collective-permute-start.19 = (s32[128]{0:T(128)}, s32[128]{0:T(128)S(1)}, u32[]{:S(2)}, u32[]{:S(2)}) collective-permute-start(s32[128]{0:T(128)} %get-tuple-element.249), channel_id=1, source_target_pairs={{0,4},{4,8},{8,12},{12,16},{16,20},{20,24},{24,28},{28,0},{1,5},{5... | collective-permute-start | bytes 1544 | tf_op jit(solution)/shard_map/ppermute | solution.py:27
  13.1 51.2 %collective-permute-start.20 = (f32[45,32,128]{2,1,0:T(8,128)}, f32[45,32,128]{2,1,0:T(8,128)S(1)}, u32[]{:S(2)}, u32[]{:S(2)}) collective-permute-start(f32[45,32,128]{2,1,0:T(8,128)} %pack.8), channel_id=1, source_target_pairs={{0,28},{4,0},{8,4},{12,8},{16,12},{20,16},{24,20},{28,24},{1,29},{... | collective-permute-start | bytes 2211848 | tf_op jit(solution)/shard_map/ppermute | solution.py:27
  21.5 44.8 %collective-permute-start.21 = (f32[45,32,128]{2,1,0:T(8,128)}, f32[45,32,128]{2,1,0:T(8,128)}, u32[]{:S(2)}, u32[]{:S(2)}) collective-permute-start(f32[45,32,128]{2,1,0:T(8,128)} %far.30), channel_id=1, source_target_pairs={{0,4},{4,8},{8,12},{12,16},{16,20},{20,24},{24,28},{28,0},{1,5},{5... | collective-permute-start | bytes 2211848 | tf_op jit(solution)/shard_map/ppermute | solution.py:27
  23.3 11.8 %copy-start.2 = (f32[8192]{0:T(1024)S(1)}, f32[8192]{0:T(1024)}, u32[]{:S(2)}) copy-start(f32[8192]{0:T(1024)} %param.13) | copy-start | bytes 98308
  23.3 11.8 %copy-start.3 = (f32[8192]{0:T(1024)S(1)}, f32[8192]{0:T(1024)}, u32[]{:S(2)}) copy-start(f32[8192]{0:T(1024)} %param.14) | copy-start | bytes 98308
  29.7 63.7 %collective-permute-start.23 = (f32[45,32,128]{2,1,0:T(8,128)}, f32[45,32,128]{2,1,0:T(8,128)}, u32[]{:S(2)}, u32[]{:S(2)}) collective-permute-start(f32[45,32,128]{2,1,0:T(8,128)} %far.32), channel_id=1, source_target_pairs={{0,4},{4,8},{8,12},{12,16},{16,20},{20,24},{24,28},{28,0},{1,5},{5... | collective-permute-start | bytes 2211848 | tf_op jit(solution)/shard_map/ppermute | solution.py:27
  30.7 62.7 %collective-permute-start.22 = (f32[45,32,128]{2,1,0:T(8,128)}, f32[45,32,128]{2,1,0:T(8,128)}, u32[]{:S(2)}, u32[]{:S(2)}) collective-permute-start(f32[45,32,128]{2,1,0:T(8,128)} %pack.9), channel_id=1, source_target_pairs={{0,28},{4,0},{8,4},{12,8},{16,12},{20,16},{24,20},{28,24},{1,29},{... | collective-permute-start | bytes 2211848 | tf_op jit(solution)/shard_map/ppermute | solution.py:27
  76.4 45.2 %collective-permute-start.24 = (f32[45,32,128]{2,1,0:T(8,128)}, f32[45,32,128]{2,1,0:T(8,128)}, u32[]{:S(2)}, u32[]{:S(2)}) collective-permute-start(f32[45,32,128]{2,1,0:T(8,128)} %get-tuple-element.263), channel_id=1, source_target_pairs={{0,28},{4,0},{8,4},{12,8},{16,12},{20,16},{24,20},{28,24},{1,29},{... | collective-permute-start | bytes 2211848 | tf_op jit(solution)/shard_map/ppermute | solution.py:27
  77.3 47.7 %collective-permute-start.25 = (f32[45,32,128]{2,1,0:T(8,128)}, f32[45,32,128]{2,1,0:T(8,128)}, u32[]{:S(2)}, u32[]{:S(2)}) collective-permute-start(f32[45,32,128]{2,1,0:T(8,128)} %get-tuple-element.264), channel_id=1, source_target_pairs={{0,4},{4,8},{8,12},{12,16},{16,20},{20,24},{24,28},{28,0},{1,5},{5... | collective-permute-start | bytes 2211848 | tf_op jit(solution)/shard_map/ppermute | solution.py:27
  103.4 49.7 %collective-permute-start.26 = (f32[45,32,128]{2,1,0:T(8,128)}, f32[45,32,128]{2,1,0:T(8,128)S(1)}, u32[]{:S(2)}, u32[]{:S(2)}) collective-permute-start(f32[45,32,128]{2,1,0:T(8,128)} %get-tuple-element.269), channel_id=1, source_target_pairs={{0,28},{4,0},{8,4},{12,8},{16,12},{20,16},{24,20},{28,24},{1,29},{... | collective-permute-start | bytes 2211848 | tf_op jit(solution)/shard_map/ppermute | solution.py:27
  108.8 47.8 %collective-permute-start.27 = (f32[45,32,128]{2,1,0:T(8,128)}, f32[45,32,128]{2,1,0:T(8,128)}, u32[]{:S(2)}, u32[]{:S(2)}) collective-permute-start(f32[45,32,128]{2,1,0:T(8,128)} %get-tuple-element.270), channel_id=1, source_target_pairs={{0,4},{4,8},{8,12},{12,16},{16,20},{20,24},{24,28},{28,0},{1,5},{5... | collective-permute-start | bytes 2211848 | tf_op jit(solution)/shard_map/ppermute | solution.py:27
  136.1 54.9 %collective-permute-start.28 = (f32[45,32,128]{2,1,0:T(8,128)}, f32[45,32,128]{2,1,0:T(8,128)}, u32[]{:S(2)}, u32[]{:S(2)}) collective-permute-start(f32[45,32,128]{2,1,0:T(8,128)} %get-tuple-element.276), channel_id=1, source_target_pairs={{0,28},{4,0},{8,4},{12,8},{16,12},{20,16},{24,20},{28,24},{1,29},{... | collective-permute-start | bytes 2211848 | tf_op jit(solution)/shard_map/ppermute | solution.py:27
  141.5 51.2 %collective-permute-start.29 = (f32[45,32,128]{2,1,0:T(8,128)}, f32[45,32,128]{2,1,0:T(8,128)}, u32[]{:S(2)}, u32[]{:S(2)}) collective-permute-start(f32[45,32,128]{2,1,0:T(8,128)} %get-tuple-element.277), channel_id=1, source_target_pairs={{0,4},{4,8},{8,12},{12,16},{16,20},{20,24},{24,28},{28,0},{1,5},{5... | collective-permute-start | bytes 2211848 | tf_op jit(solution)/shard_map/ppermute | solution.py:27
  167.7 40.2 %collective-permute-start.33 = (f32[45,32,128]{2,1,0:T(8,128)}, f32[45,32,128]{2,1,0:T(8,128)S(1)}, u32[]{:S(2)}, u32[]{:S(2)}) collective-permute-start(f32[45,32,128]{2,1,0:T(8,128)} %get-tuple-element.284), channel_id=1, source_target_pairs={{0,28},{4,0},{8,4},{12,8},{16,12},{20,16},{24,20},{28,24},{1,29},{... | collective-permute-start | bytes 2211848 | tf_op jit(solution)/shard_map/ppermute | solution.py:27
  169.6 38.3 %collective-permute-start.34 = (f32[45,32,128]{2,1,0:T(8,128)}, f32[45,32,128]{2,1,0:T(8,128)S(1)}, u32[]{:S(2)}, u32[]{:S(2)}) collective-permute-start(f32[45,32,128]{2,1,0:T(8,128)} %get-tuple-element.285), channel_id=1, source_target_pairs={{0,4},{4,8},{8,12},{12,16},{16,20},{20,24},{24,28},{28,0},{1,5},{5... | collective-permute-start | bytes 2211848 | tf_op jit(solution)/shard_map/ppermute | solution.py:27
  169.7 22.9 %copy-start.22 = (s32[128]{0:T(128)S(1)}, s32[128]{0:T(128)}, u32[]{:S(2)}) copy-start(s32[128]{0:T(128)} %get-tuple-element.249) | copy-start | bytes 1540
  181.4 20.4 %collective-permute-start.30 = (f32[1,16384]{1,0:T(1,128)S(1)}, f32[1,16384]{1,0:T(1,128)S(1)}, u32[]{:S(2)}, u32[]{:S(2)}) collective-permute-start(f32[1,16384]{1,0:T(1,128)S(1)} %copy-done.16), channel_id=1, source_target_pairs={{0,1},{1,2},{2,3},{3,0},{4,5},{5,6},{6,7},{7,4},{8,9},{9,10},{10,1... | collective-permute-start | bytes 196616 | tf_op jit(solution)/shard_map/ppermute | solution.py:622
  191.0 10.8 %collective-permute-start.31 = (f32[1,16384]{1,0:T(1,128)S(1)}, f32[1,16384]{1,0:T(1,128)S(1)}, u32[]{:S(2)}, u32[]{:S(2)}) collective-permute-start(f32[1,16384]{1,0:T(1,128)S(1)} %copy-done.16), channel_id=1, source_target_pairs={{0,2},{1,3},{2,0},{3,1},{4,6},{5,7},{6,4},{7,5},{8,10},{9,11},{10,... | collective-permute-start | bytes 196616 | tf_op jit(solution)/shard_map/ppermute | solution.py:622
  192.6 9.2 %collective-permute-start.32 = (f32[1,16384]{1,0:T(1,128)S(1)}, f32[1,16384]{1,0:T(1,128)S(1)}, u32[]{:S(2)}, u32[]{:S(2)}) collective-permute-start(f32[1,16384]{1,0:T(1,128)S(1)} %copy-done.16), channel_id=1, source_target_pairs={{0,3},{1,0},{2,1},{3,2},{4,7},{5,4},{6,5},{7,6},{8,11},{9,8},{10,9... | collective-permute-start | bytes 196616 | tf_op jit(solution)/shard_map/ppermute | solution.py:622
  218.2 3.7 %collective-permute-start.35 = (f32[8,136]{1,0:T(8,128)S(1)}, f32[8,136]{1,0:T(8,128)S(1)}, u32[]{:S(2)}, u32[]{:S(2)}) collective-permute-start(f32[8,136]{1,0:T(8,128)S(1)} %maximum_maximum_fusion.1), channel_id=1, source_target_pairs={{0,4},{4,0},{8,12},{12,8},{16,20},{20,16},{24,28},{28,24},{1,5},{5... | collective-permute-start | bytes 13064 | tf_op jit(solution)/shard_map/ppermute | solution.py:634
  221.9 5.0 %collective-permute-start.36 = (f32[8,136]{1,0:T(8,128)S(1)}, f32[8,136]{1,0:T(8,128)S(1)}, u32[]{:S(2)}, u32[]{:S(2)}) collective-permute-start(f32[8,136]{1,0:T(8,128)S(1)} %add.36), channel_id=1, source_target_pairs={{0,8},{4,12},{8,0},{12,4},{16,24},{20,28},{24,16},{28,20},{1,9},{5... | collective-permute-start | bytes 13064 | tf_op jit(solution)/shard_map/ppermute | solution.py:634
  221.9 5.1 %collective-permute-start.37 = (f32[8,136]{1,0:T(8,128)S(1)}, f32[8,136]{1,0:T(8,128)S(1)}, u32[]{:S(2)}, u32[]{:S(2)}) collective-permute-start(f32[8,136]{1,0:T(8,128)S(1)} %add.36), channel_id=1, source_target_pairs={{0,16},{4,20},{8,24},{12,28},{16,0},{20,4},{24,8},{28,12},{1,17},{... | collective-permute-start | bytes 13064 | tf_op jit(solution)/shard_map/ppermute | solution.py:634
  223.5 5.4 %collective-permute-start.38 = (f32[8,136]{1,0:T(8,128)S(1)}, f32[8,136]{1,0:T(8,128)S(1)}, u32[]{:S(2)}, u32[]{:S(2)}) collective-permute-start(f32[8,136]{1,0:T(8,128)S(1)} %add.36), channel_id=1, source_target_pairs={{0,24},{4,28},{8,16},{12,20},{16,8},{20,12},{24,0},{28,4},{1,25},{... | collective-permute-start | bytes 13064 | tf_op jit(solution)/shard_map/ppermute | solution.py:634
  (10 other events, 36.8 us)
